TPU v7x, 128 devices: a whole 4x4x4 slice. The times are simulated.
128 devices in a mesh: group: 32 (over z, y, x_hi), tile: 4 (over x_lo, core).
Axes of the slice: x: 4 (x_hi: 2, x_lo: 2; x = x_hi * 2 + x_lo), y: 4, z: 4, core: 2. Of those that a mesh axis runs over, the one named last changes fastest.
Arguments:
- queries: bfloat16 [16384, 2560], P(('group', 'tile')), may hold values from -100 to 100
- keys: bfloat16 [16384, 2560], P(('group', 'tile')), may hold values from -4.5 to 4.5
- values: bfloat16 [16384, 2560], P(('group', 'tile')), may hold values from -8 to 8
- cotangent: bfloat16 [16384, 2560], P(('group', 'tile')), may hold values from -6 to 6
- window: int32 [20], replicated, may hold values from 1 to 32, as said below
Outputs:
- attended: bfloat16 [16384, 2560], P(('group', 'tile'))
- grad_queries: bfloat16 [16384, 2560], P(('group', 'tile'))
- grad_keys: bfloat16 [16384, 2560], P(('group', 'tile'))
- grad_values: bfloat16 [16384, 2560], P(('group', 'tile'))
Inputs may be any that keep to these rules, and one draw needn't show every extreme that they name: Some head has window 32.
All inputs are finite; a program needn't handle non-finite values.
Results may differ from a plain program's by a relative error of at most 0.04.
Values may be sent and summed in bfloat16 or wider, within the bound.
No kernel may reach another device: no remote copies, remote signals or barrier semaphores. Data moves between devices by JAX's collectives and lax.ppermute only.
A program may use at most 128 MiB of HBM per device.

v0:
```python
import math

import jax
import jax.numpy as jnp
from jax import lax
from jax.sharding import PartitionSpec as P

masked_score = -1e30


def extended(block, sides, width):
    for axis, dim in sides:
        count = lax.axis_size(axis)
        forward = [(i, i + 1) for i in range(count - 1)]
        backward = [(target, source) for source, target in forward]
        low = lax.ppermute(
            lax.slice_in_dim(block, block.shape[dim] - width, None, axis=dim), axis, forward
        )
        high = lax.ppermute(lax.slice_in_dim(block, 0, width, axis=dim), axis, backward)
        block = jnp.concatenate([low, block, high], axis=dim)
    return block


def from_behind(x, axis, by):
    length = lax.axis_size(axis)
    pairs = [(i, i + by) for i in range(length) if 0 <= i + by < length]
    return lax.ppermute(x, axis, pairs)


def split_pair(joined, feat_width, num_heads, head_width):
    tok_count = joined.shape[0]
    key_part = joined[:, :feat_width].reshape(tok_count, num_heads, head_width)
    value_part = joined[:, feat_width:].reshape(tok_count, num_heads, head_width)
    return (key_part, value_part)


def shards(queries, keys, values, cotangent, window):
    group_count = lax.axis_size("group")
    tile_count = lax.axis_size("tile")
    my_group = lax.axis_index("group")
    my_tile = lax.axis_index("tile")
    tok_rows, feat_width = queries.shape
    num_heads = window.shape[0]
    head_width = feat_width // num_heads
    halo_rows = tok_rows // 4
    ext_rows = tok_rows + 2 * halo_rows
    frame_rows = tok_rows * tile_count
    factor = head_width ** (-0.5)
    past_reach = min(8, group_count // 2)
    block_groups = math.gcd(past_reach, max(1, 512 // tok_rows))
    block_rows = block_groups * tok_rows
    block_total = past_reach // block_groups
    query_heads = queries.reshape(tok_rows, num_heads, head_width)
    cot_heads = cotangent.reshape(tok_rows, num_heads, head_width)
    joined = jnp.concatenate([keys, values], axis=1)
    bordered = extended(joined, (("tile", 0),), halo_rows)
    key_ext, value_ext = split_pair(bordered, feat_width, num_heads, head_width)
    pieces = []
    for group_lag in range(past_reach, 0, -1):
        pieces.append(from_behind(joined, "group", group_lag))
    earlier = jnp.concatenate(pieces, axis=0)
    query_pos = my_tile * tok_rows + jnp.arange(tok_rows)
    key_pos = my_tile * tok_rows - halo_rows + jnp.arange(ext_rows)
    spacing = jnp.abs(query_pos[:, None] - key_pos[None, :])
    inside = (key_pos >= 0) & (key_pos < frame_rows)
    near_mask = (spacing[None, :, :] <= window[:, None, None]) & inside[None, None, :]
    near_scores = (
        jnp.einsum("qhd,khd->hqk", query_heads, key_ext, preferred_element_type=jnp.float32)
        * factor
    )
    near_scores = jnp.where(near_mask, near_scores, masked_score)

    def block_scores(block):
        piece = earlier[block * block_rows : (block + 1) * block_rows]
        key_blk, value_blk = split_pair(piece, feat_width, num_heads, head_width)
        scores = (
            jnp.einsum("qhd,khd->hqk", query_heads, key_blk, preferred_element_type=jnp.float32)
            * factor
        )
        owner = my_group - past_reach + block * block_groups + jnp.arange(block_rows) // tok_rows
        scores = jnp.where((owner >= 0)[None, None, :], scores, masked_score)
        return (scores, key_blk, value_blk)

    top_score = near_scores.max(-1)
    summed = jnp.exp(near_scores - top_score[..., None]).sum(-1)
    for block in range(block_total):
        scores, key_blk, value_blk = block_scores(block)
        new_top = jnp.maximum(top_score, scores.max(-1))
        summed = summed * jnp.exp(top_score - new_top) + jnp.exp(scores - new_top[..., None]).sum(
            -1
        )
        top_score = new_top
    lse = top_score + jnp.log(summed)
    near_probs = jnp.exp(near_scores - lse[..., None])
    near_round = near_probs.astype(jnp.bfloat16)
    output = jnp.einsum("hqk,khd->qhd", near_round, value_ext, preferred_element_type=jnp.float32)
    for block in range(block_total):
        scores, key_blk, value_blk = block_scores(block)
        prob_blk = jnp.exp(scores - lse[..., None]).astype(jnp.bfloat16)
        output = output + jnp.einsum(
            "hqk,khd->qhd", prob_blk, value_blk, preferred_element_type=jnp.float32
        )
    output_b = output.astype(jnp.bfloat16)
    delta = jnp.sum(cot_heads.astype(jnp.float32) * output_b.astype(jnp.float32), -1).T
    near_dprob = jnp.einsum(
        "qhd,khd->hqk", cot_heads, value_ext, preferred_element_type=jnp.float32
    )
    near_dscore = (near_probs * (near_dprob - delta[..., None])).astype(jnp.bfloat16)
    near_dquery = jnp.einsum(
        "hqk,khd->qhd", near_dscore, key_ext, preferred_element_type=jnp.float32
    )
    near_dkey = factor * jnp.einsum(
        "hqk,qhd->khd", near_dscore, query_heads, preferred_element_type=jnp.float32
    )
    near_dvalue = jnp.einsum(
        "hqk,qhd->khd", near_round, cot_heads, preferred_element_type=jnp.float32
    )
    grad_ext = jnp.concatenate(
        [near_dkey.reshape(ext_rows, feat_width), near_dvalue.reshape(ext_rows, feat_width)], axis=1
    )
    returned = extended(grad_ext.astype(jnp.bfloat16), (("tile", 0),), halo_rows).astype(
        grad_ext.dtype
    )
    own_grads = grad_ext[halo_rows : halo_rows + tok_rows]
    own_grads = own_grads + jnp.pad(returned[:halo_rows], ((0, tok_rows - halo_rows), (0, 0)))
    own_grads = own_grads + jnp.pad(
        returned[ext_rows + halo_rows :], ((tok_rows - halo_rows, 0), (0, 0))
    )
    dquery = near_dquery
    term_blocks = []
    for block in range(block_total):
        scores, key_blk, value_blk = block_scores(block)
        probs = jnp.exp(scores - lse[..., None])
        dprob = jnp.einsum("qhd,khd->hqk", cot_heads, value_blk, preferred_element_type=jnp.float32)
        dscore = (probs * (dprob - delta[..., None])).astype(jnp.bfloat16)
        dquery = dquery + jnp.einsum(
            "hqk,khd->qhd", dscore, key_blk, preferred_element_type=jnp.float32
        )
        prob_round = probs.astype(jnp.bfloat16)
        key_term = factor * jnp.einsum(
            "hqk,qhd->khd", dscore, query_heads, preferred_element_type=jnp.float32
        )
        value_term = jnp.einsum(
            "hqk,qhd->khd", prob_round, cot_heads, preferred_element_type=jnp.float32
        )
        term_blocks.append(
            jnp.concatenate(
                [
                    key_term.reshape(block_rows, feat_width),
                    value_term.reshape(block_rows, feat_width),
                ],
                axis=1,
            ).astype(jnp.bfloat16)
        )
    terms = jnp.concatenate(term_blocks, axis=0)
    past_grads = jnp.zeros((tok_rows, 2 * feat_width), jnp.float32)
    for group_lag in range(1, past_reach + 1):
        row_start = (past_reach - group_lag) * tok_rows
        received = from_behind(terms[row_start : row_start + tok_rows], "group", -group_lag)
        past_grads = past_grads + received.astype(jnp.float32)
    total_grads = own_grads + past_grads
    grad_queries = (factor * dquery).reshape(tok_rows, feat_width).astype(jnp.bfloat16)
    grad_keys = total_grads[:, :feat_width].astype(jnp.bfloat16)
    grad_values = total_grads[:, feat_width:].astype(jnp.bfloat16)
    return (output_b.reshape(tok_rows, feat_width), grad_queries, grad_keys, grad_values)


def solution(mesh):
    return jax.shard_map(
        shards,
        mesh=mesh,
        in_specs=(
            P(("group", "tile"), None),
            P(("group", "tile"), None),
            P(("group", "tile"), None),
            P(("group", "tile"), None),
            P(),
        ),
        out_specs=(
            P(("group", "tile"), None),
            P(("group", "tile"), None),
            P(("group", "tile"), None),
            P(("group", "tile"), None),
        ),
        check_vma=False,
    )
```

profile of v0, /device:TPU:30, one launch (start us, length us, event | category | flops | bytes accessed | tf_op | source)
XLA Modules:
  0.0 555.0 jit_solution(16087735919784084240)
XLA Ops:
  2.0 1.4 copy.83
  4.7 4.5 collective-permute-start.6
  9.1 4.0 collective-permute-start.5
  13.1 4.3 collective-permute-start.4
  17.4 1.6 fusion.21
  19.0 2.2 copy.85
  21.2 1.9 collective-permute-start.1
  24.3 3.1 collective-permute-start
  27.5 1.4 copy.90
  28.9 2.2 copy.100
  31.2 15.8 %collective-permute-done = bf16[32,5120]{1,0:T(8,128)(2,1)S(1)} collective-permute-done((bf16[32,5120]{1,0:T(8,128)(2,1)}, bf16[32,5120]{1,0:T(8,128)(2,1)S(1)}, u32[]{:S(2)}, u32[]{:S(2)}) %collective-permute-start) | collective-permute-done | bytes 327712 | tf_op jit(solution)/shard_map/ppermute | solution.py:16
  47.7 8.0 %collective-permute-start.3 = (bf16[128,5120]{0,1:T(8,128)(2,1)}, bf16[128,5120]{0,1:T(8,128)(2,1)}, u32[]{:S(2)}, u32[]{:S(2)}) collective-permute-start(bf16[128,5120]{0,1:T(8,128)(2,1)} %pad_maximum_fusion.1), channel_id=1, source_target_pairs={{0,28},{4,32},{8,36},{12,40},{16,44},{20,48},{24,52},{28,56},{32,6... | collective-permute-start | bytes 3932168 | tf_op jit(solution)/shard_map/ppermute | solution.py:27
  55.7 1.6 copy.86
  57.3 4.8 collective-permute-start.2
  62.1 2.3 copy.87
  64.4 2.8 pad_maximum_fusion
  69.1 7.3 %collective-permute-done.2 = bf16[128,5120]{0,1:T(8,128)(2,1)} collective-permute-done((bf16[128,5120]{0,1:T(8,128)(2,1)}, bf16[128,5120]{0,1:T(8,128)(2,1)}, u32[]{:S(2)}, u32[]{:S(2)}) %collective-permute-start.2) | collective-permute-done | bytes 1310752 | tf_op jit(solution)/shard_map/ppermute | solution.py:27
  76.4 80.0 %collective-permute-start.9 = (bf16[128,5120]{0,1:T(8,128)(2,1)}, bf16[128,5120]{0,1:T(8,128)(2,1)S(1)}, u32[]{:S(2)}, u32[]{:S(2)}) collective-permute-start(bf16[128,5120]{0,1:T(8,128)(2,1)} %pad_maximum_fusion.1), channel_id=1, source_target_pairs={{0,4},{4,8},{8,12},{12,16},{16,20},{20,24},{24,28},{28,32},{32,36}... | collective-permute-start | bytes 3932168 | tf_op jit(solution)/shard_map/ppermute | solution.py:27
  156.4 1.5 constant_dynamic-update-slice_fusion.3
  158.0 5.0 collective-permute-start.7
  163.1 1.5 constant_dynamic-update-slice_fusion.7
  164.6 2.2 collective-permute-start.8
  166.8 1.6 constant_dynamic-update-slice_fusion.2
  168.5 1.6 constant_dynamic-update-slice_fusion.1
  170.1 1.6 constant_dynamic-update-slice_fusion
  171.7 65.2 %collective-permute-done.7 = bf16[128,5120]{0,1:T(8,128)(2,1)S(1)} collective-permute-done((bf16[128,5120]{0,1:T(8,128)(2,1)}, bf16[128,5120]{0,1:T(8,128)(2,1)S(1)}, u32[]{:S(2)}, u32[]{:S(2)}) %collective-permute-start.7) | collective-permute-done | bytes 1310752 | tf_op jit(solution)/shard_map/ppermute | solution.py:27
  238.6 1.5 bitcast_reduce_fusion
  240.1 1.4 bitcast_reduce_fusion.1
  241.6 3.4 fusion.3
  245.0 1.5 fusion.42
  247.6 2.9 multiply_reduce_fusion
  250.5 1.7 fusion.16
  252.2 3.5 fusion
  255.7 3.3 convolution_convert_fusion.1
  259.0 2.5 fusion.1
  261.6 3.4 convolution_convert_fusion
  264.9 1.8 convolution_bitcast_fusion
  266.8 2.3 fusion.11
  269.1 4.4 copy.122
  273.5 4.4 copy.124
  277.9 4.4 copy.125
  282.3 4.4 copy.119
  286.7 4.1 fusion.10
  290.8 4.4 copy.116
  295.2 4.4 copy.118
  299.6 1.9 multiply_bitcast_fusion
  301.6 3.5 fusion.24
  305.2 9.8 %collective-permute-start.16 = (bf16[128,5120]{1,0:T(8,128)(2,1)S(1)}, bf16[128,5120]{1,0:T(8,128)(2,1)S(1)}, u32[]{:S(2)}, u32[]{:S(2)}) collective-permute-start(bf16[128,5120]{1,0:T(8,128)(2,1)S(1)} %get-tuple-element.22), channel_id=1, source_target_pairs={{20,0},{24,4},{28,8},{32,12},{36,16},{40,20},{44,24},{48,28},{52,3... | collective-permute-start | bytes 3932168 | tf_op jit(solution)/shard_map/ppermute | solution.py:27
  315.0 1.9 collective-permute-start.17
  318.9 1.7 copy-done.4
  320.7 2.3 collective-permute-start.10
  323.0 3.8 collective-permute-start.11
  326.8 3.9 fusion.27
  332.8 16.9 %collective-permute-done.10 = bf16[32,5120]{1,0:T(8,128)(2,1)S(1)} collective-permute-done((bf16[32,5120]{1,0:T(8,128)(2,1)S(1)}, bf16[32,5120]{1,0:T(8,128)(2,1)S(1)}, u32[]{:S(2)}, u32[]{:S(2)}) %collective-permute-start.10) | collective-permute-done | bytes 327712 | tf_op jit(solution)/shard_map/ppermute | solution.py:16
  349.8 1.9 collective-permute-start.18
  351.7 1.9 collective-permute-start.12
  353.6 1.9 collective-permute-start.13
  355.6 91.2 %collective-permute-done.17 = bf16[128,5120]{1,0:T(8,128)(2,1)S(1)} collective-permute-done((bf16[128,5120]{1,0:T(8,128)(2,1)S(1)}, bf16[128,5120]{1,0:T(8,128)(2,1)S(1)}, u32[]{:S(2)}, u32[]{:S(2)}) %collective-permute-start.17) | collective-permute-done | bytes 1310752 | tf_op jit(solution)/shard_map/ppermute | solution.py:27
  446.8 1.9 collective-permute-start.15
  448.7 63.0 %collective-permute-done.19 = bf16[128,5120]{1,0:T(8,128)(2,1)S(1)} collective-permute-done((bf16[128,5120]{1,0:T(8,128)(2,1)S(1)}, bf16[128,5120]{1,0:T(8,128)(2,1)S(1)}, u32[]{:S(2)}, u32[]{:S(2)}) %collective-permute-start.19) | collective-permute-done | bytes 1310752 | tf_op jit(solution)/shard_map/ppermute | solution.py:27
  511.7 2.1 collective-permute-start.14
  515.9 2.2 copy.126
  518.8 30.6 %collective-permute-done.14 = bf16[128,5120]{1,0:T(8,128)(2,1)} collective-permute-done((bf16[128,5120]{1,0:T(8,128)(2,1)}, bf16[128,5120]{1,0:T(8,128)(2,1)}, u32[]{:S(2)}, u32[]{:S(2)}) %collective-permute-start.14) | collective-permute-done | bytes 1310752 | tf_op jit(solution)/shard_map/ppermute | solution.py:27
  549.5 4.1 fusion.15
  (104 shorter events, 17.4 us)
Async XLA Ops:
  4.7 153.3 %collective-permute-start.6 = (bf16[128,5120]{0,1:T(8,128)(2,1)}, bf16[128,5120]{0,1:T(8,128)(2,1)}, u32[]{:S(2)}, u32[]{:S(2)}) collective-permute-start(bf16[128,5120]{0,1:T(8,128)(2,1)} %pad_maximum_fusion.1), channel_id=1, source_target_pairs={{0,16},{4,20},{8,24},{12,28},{16,32},{20,36},{24,40},{28,44},{32,4... | collective-permute-start | bytes 3932168 | tf_op jit(solution)/shard_map/ppermute | solution.py:27
  9.1 161.0 %collective-permute-start.5 = (bf16[128,5120]{0,1:T(8,128)(2,1)}, bf16[128,5120]{0,1:T(8,128)(2,1)}, u32[]{:S(2)}, u32[]{:S(2)}) collective-permute-start(bf16[128,5120]{0,1:T(8,128)(2,1)} %pad_maximum_fusion.1), channel_id=1, source_target_pairs={{0,20},{4,24},{8,28},{12,32},{16,36},{20,40},{24,44},{28,48},{32,5... | collective-permute-start | bytes 3932168 | tf_op jit(solution)/shard_map/ppermute | solution.py:27
  13.1 155.4 %collective-permute-start.4 = (bf16[128,5120]{0,1:T(8,128)(2,1)}, bf16[128,5120]{0,1:T(8,128)(2,1)}, u32[]{:S(2)}, u32[]{:S(2)}) collective-permute-start(bf16[128,5120]{0,1:T(8,128)(2,1)} %pad_maximum_fusion.1), channel_id=1, source_target_pairs={{0,24},{4,28},{8,32},{12,36},{16,40},{20,44},{24,48},{28,52},{32,5... | collective-permute-start | bytes 3932168 | tf_op jit(solution)/shard_map/ppermute | solution.py:27
  21.2 36.2 %collective-permute-start.1 = (bf16[32,5120]{1,0:T(8,128)(2,1)}, bf16[32,5120]{1,0:T(8,128)(2,1)}, u32[]{:S(2)}, u32[]{:S(2)}) collective-permute-start(bf16[32,5120]{1,0:T(8,128)(2,1)} %copy.85), channel_id=1, source_target_pairs={{1,0},{2,1},{3,2},{5,4},{6,5},{7,6},{9,8},{10,9},{11,10},{13,12},{... | collective-permute-start | bytes 983048 | tf_op jit(solution)/shard_map/ppermute | solution.py:19
  24.3 22.7 %collective-permute-start = (bf16[32,5120]{1,0:T(8,128)(2,1)}, bf16[32,5120]{1,0:T(8,128)(2,1)S(1)}, u32[]{:S(2)}, u32[]{:S(2)}) collective-permute-start(bf16[32,5120]{1,0:T(8,128)(2,1)} %copy.84), channel_id=1, source_target_pairs={{0,1},{1,2},{2,3},{4,5},{5,6},{6,7},{8,9},{9,10},{10,11},{12,13},{... | collective-permute-start | bytes 983048 | tf_op jit(solution)/shard_map/ppermute | solution.py:16
  47.0 0.7 copy-start.27
  47.7 116.9 %collective-permute-start.3 = (bf16[128,5120]{0,1:T(8,128)(2,1)}, bf16[128,5120]{0,1:T(8,128)(2,1)}, u32[]{:S(2)}, u32[]{:S(2)}) collective-permute-start(bf16[128,5120]{0,1:T(8,128)(2,1)} %pad_maximum_fusion.1), channel_id=1, source_target_pairs={{0,28},{4,32},{8,36},{12,40},{16,44},{20,48},{24,52},{28,56},{32,6... | collective-permute-start | bytes 3932168 | tf_op jit(solution)/shard_map/ppermute | solution.py:27
  57.3 19.1 %collective-permute-start.2 = (bf16[128,5120]{0,1:T(8,128)(2,1)}, bf16[128,5120]{0,1:T(8,128)(2,1)}, u32[]{:S(2)}, u32[]{:S(2)}) collective-permute-start(bf16[128,5120]{0,1:T(8,128)(2,1)} %pad_maximum_fusion.1), channel_id=1, source_target_pairs={{0,32},{4,36},{8,40},{12,44},{16,48},{20,52},{24,56},{28,60},{32,6... | collective-permute-start | bytes 3932168 | tf_op jit(solution)/shard_map/ppermute | solution.py:27
  67.2 0.7 copy-start.29
  67.4 1.7 copy-start.15
  76.4 161.5 %collective-permute-start.9 = (bf16[128,5120]{0,1:T(8,128)(2,1)}, bf16[128,5120]{0,1:T(8,128)(2,1)S(1)}, u32[]{:S(2)}, u32[]{:S(2)}) collective-permute-start(bf16[128,5120]{0,1:T(8,128)(2,1)} %pad_maximum_fusion.1), channel_id=1, source_target_pairs={{0,4},{4,8},{8,12},{12,16},{16,20},{20,24},{24,28},{28,32},{32,36}... | collective-permute-start | bytes 3932168 | tf_op jit(solution)/shard_map/ppermute | solution.py:27
  158.0 78.9 %collective-permute-start.7 = (bf16[128,5120]{0,1:T(8,128)(2,1)}, bf16[128,5120]{0,1:T(8,128)(2,1)S(1)}, u32[]{:S(2)}, u32[]{:S(2)}) collective-permute-start(bf16[128,5120]{0,1:T(8,128)(2,1)} %pad_maximum_fusion.1), channel_id=1, source_target_pairs={{0,12},{4,16},{8,20},{12,24},{16,28},{20,32},{24,36},{28,40},{32,4... | collective-permute-start | bytes 3932168 | tf_op jit(solution)/shard_map/ppermute | solution.py:27
  164.6 72.6 %collective-permute-start.8 = (bf16[128,5120]{0,1:T(8,128)(2,1)}, bf16[128,5120]{0,1:T(8,128)(2,1)S(1)}, u32[]{:S(2)}, u32[]{:S(2)}) collective-permute-start(bf16[128,5120]{0,1:T(8,128)(2,1)} %pad_maximum_fusion.1), channel_id=1, source_target_pairs={{0,8},{4,12},{8,16},{12,20},{16,24},{20,28},{24,32},{28,36},{32,40... | collective-permute-start | bytes 3932168 | tf_op jit(solution)/shard_map/ppermute | solution.py:27
  238.6 1.5 copy-start
  246.5 1.1 copy-start.6
  261.6 5.2 copy-start.7
  299.6 2.0 copy-start.11
  305.2 13.2 %copy-start.14 = (f32[20,24,8,128]{3,2,1,0:T(8,128)S(1)}, f32[20,24,8,128]{3,2,1,0:T(8,128)}, u32[]{:S(2)}) copy-start(f32[20,24,8,128]{3,2,1,0:T(8,128)} %convolution_bitcast_fusion) | copy-start | bytes 5898244
  305.2 48.4 %collective-permute-start.16 = (bf16[128,5120]{1,0:T(8,128)(2,1)S(1)}, bf16[128,5120]{1,0:T(8,128)(2,1)S(1)}, u32[]{:S(2)}, u32[]{:S(2)}) collective-permute-start(bf16[128,5120]{1,0:T(8,128)(2,1)S(1)} %get-tuple-element.22), channel_id=1, source_target_pairs={{20,0},{24,4},{28,8},{32,12},{36,16},{40,20},{44,24},{48,28},{52,3... | collective-permute-start | bytes 3932168 | tf_op jit(solution)/shard_map/ppermute | solution.py:27
  315.0 131.8 %collective-permute-start.17 = (bf16[128,5120]{1,0:T(8,128)(2,1)S(1)}, bf16[128,5120]{1,0:T(8,128)(2,1)S(1)}, u32[]{:S(2)}, u32[]{:S(2)}) collective-permute-start(bf16[128,5120]{1,0:T(8,128)(2,1)S(1)} %get-tuple-element.23), channel_id=1, source_target_pairs={{24,0},{28,4},{32,8},{36,12},{40,16},{44,20},{48,24},{52,28},{56,3... | collective-permute-start | bytes 3932168 | tf_op jit(solution)/shard_map/ppermute | solution.py:27
  316.9 194.8 %collective-permute-start.19 = (bf16[128,5120]{1,0:T(8,128)(2,1)S(1)}, bf16[128,5120]{1,0:T(8,128)(2,1)S(1)}, u32[]{:S(2)}, u32[]{:S(2)}) collective-permute-start(bf16[128,5120]{1,0:T(8,128)(2,1)S(1)} %get-tuple-element.24), channel_id=1, source_target_pairs={{32,0},{36,4},{40,8},{44,12},{48,16},{52,20},{56,24},{60,28},{64,3... | collective-permute-start | bytes 3932168 | tf_op jit(solution)/shard_map/ppermute | solution.py:27
  318.7 2.0 copy-start.4
  318.7 8.2 %copy-start.9 = (bf16[512,2560]{1,0:T(8,128)(2,1)S(1)}, bf16[512,2560]{1,0:T(8,128)(2,1)}, u32[]{:S(2)}) copy-start(bf16[512,2560]{1,0:T(8,128)(2,1)} %copy.119) | copy-start | bytes 7864324
  318.7 8.2 %copy-start.10 = (bf16[512,2560]{1,0:T(8,128)(2,1)S(1)}, bf16[512,2560]{1,0:T(8,128)(2,1)}, u32[]{:S(2)}) copy-start(bf16[512,2560]{1,0:T(8,128)(2,1)} %copy.118) | copy-start | bytes 7864324
  320.7 10.0 %copy-start.2 = (bf16[192,5120]{1,0:T(8,128)(2,1)}, bf16[192,5120]{1,0:T(8,128)(2,1)S(1)}, u32[]{:S(2)}) copy-start(bf16[192,5120]{1,0:T(8,128)(2,1)S(1)} %convert_element_type.92) | copy-start | bytes 5898244
  320.7 29.0 %collective-permute-start.10 = (bf16[32,5120]{1,0:T(8,128)(2,1)S(1)}, bf16[32,5120]{1,0:T(8,128)(2,1)S(1)}, u32[]{:S(2)}, u32[]{:S(2)}) collective-permute-start(bf16[32,5120]{1,0:T(8,128)(2,1)S(1)} %get-tuple-element.32), channel_id=1, source_target_pairs={{0,1},{1,2},{2,3},{4,5},{5,6},{6,7},{8,9},{9,10},{10,11},{12,13},{... | collective-permute-start | bytes 983048 | tf_op jit(solution)/shard_map/ppermute | solution.py:16
  323.0 7.7 %copy-start.8 = (bf16[20,128,512]{1,2,0:T(8,128)(2,1)S(1)}, bf16[20,128,512]{1,2,0:T(8,128)(2,1)}, u32[]{:S(2)}) copy-start(bf16[20,128,512]{1,2,0:T(8,128)(2,1)} %copy-done.7) | copy-start | bytes 7864324
  323.0 28.6 %collective-permute-start.11 = (bf16[32,5120]{1,0:T(8,128)(2,1)S(1)}, bf16[32,5120]{1,0:T(8,128)(2,1)S(1)}, u32[]{:S(2)}, u32[]{:S(2)}) collective-permute-start(bf16[32,5120]{1,0:T(8,128)(2,1)S(1)} %get-tuple-element.33), channel_id=1, source_target_pairs={{1,0},{2,1},{3,2},{5,4},{6,5},{7,6},{9,8},{10,9},{11,10},{13,12},{... | collective-permute-start | bytes 983048 | tf_op jit(solution)/shard_map/ppermute | solution.py:19
  330.7 1.2 copy-start.13
  330.7 1.6 copy-start.16
  330.7 183.1 %copy-start.12 = (bf16[20,128,512]{1,2,0:T(8,128)(2,1)S(1)}, bf16[20,128,512]{1,2,0:T(8,128)(2,1)}, u32[]{:S(2)}) copy-start(bf16[20,128,512]{1,2,0:T(8,128)(2,1)} %fusion) | copy-start | bytes 7864324
  332.3 181.6 %copy-start.1 = (bf16[512,2560]{0,1:T(8,128)(2,1)S(1)}, bf16[512,2560]{0,1:T(8,128)(2,1)}, u32[]{:S(2)}) copy-start(bf16[512,2560]{0,1:T(8,128)(2,1)} %copy-done) | copy-start | bytes 7864324
  349.8 165.0 %copy-start.23 = (bf16[32,5120]{1,0:T(8,128)(2,1)}, bf16[32,5120]{1,0:T(8,128)(2,1)S(1)}, u32[]{:S(2)}) copy-start(bf16[32,5120]{1,0:T(8,128)(2,1)S(1)} %collective-permute-done.10) | copy-start | bytes 983044
  349.8 169.0 %collective-permute-start.18 = (bf16[128,5120]{1,0:T(8,128)(2,1)}, bf16[128,5120]{1,0:T(8,128)(2,1)}, u32[]{:S(2)}, u32[]{:S(2)}) collective-permute-start(bf16[128,5120]{1,0:T(8,128)(2,1)} %get-tuple-element.25), channel_id=1, source_target_pairs={{28,0},{32,4},{36,8},{40,12},{44,16},{48,20},{52,24},{56,28},{60,3... | collective-permute-start | bytes 3932168 | tf_op jit(solution)/shard_map/ppermute | solution.py:27
  351.7 163.1 %copy-start.25 = (bf16[32,5120]{1,0:T(8,128)(2,1)}, bf16[32,5120]{1,0:T(8,128)(2,1)S(1)}, u32[]{:S(2)}) copy-start(bf16[32,5120]{1,0:T(8,128)(2,1)S(1)} %collective-permute-done.11) | copy-start | bytes 983044
  351.7 167.1 %collective-permute-start.12 = (bf16[128,5120]{1,0:T(8,128)(2,1)}, bf16[128,5120]{1,0:T(8,128)(2,1)}, u32[]{:S(2)}, u32[]{:S(2)}) collective-permute-start(bf16[128,5120]{1,0:T(8,128)(2,1)} %get-tuple-element.18), channel_id=1, source_target_pairs={{4,0},{8,4},{12,8},{16,12},{20,16},{24,20},{28,24},{32,28},{36,32}... | collective-permute-start | bytes 3932168 | tf_op jit(solution)/shard_map/ppermute | solution.py:27
  353.6 161.1 %copy-start.17 = (bf16[128,5120]{1,0:T(8,128)(2,1)}, bf16[128,5120]{1,0:T(8,128)(2,1)S(1)}, u32[]{:S(2)}) copy-start(bf16[128,5120]{1,0:T(8,128)(2,1)S(1)} %collective-permute-done.16) | copy-start | bytes 3932164
  353.6 165.2 %collective-permute-start.13 = (bf16[128,5120]{1,0:T(8,128)(2,1)}, bf16[128,5120]{1,0:T(8,128)(2,1)}, u32[]{:S(2)}, u32[]{:S(2)}) collective-permute-start(bf16[128,5120]{1,0:T(8,128)(2,1)} %get-tuple-element.19), channel_id=1, source_target_pairs={{8,0},{12,4},{16,8},{20,12},{24,16},{28,20},{32,24},{36,28},{40,32... | collective-permute-start | bytes 3932168 | tf_op jit(solution)/shard_map/ppermute | solution.py:27
  446.8 68.0 %copy-start.19 = (bf16[128,5120]{1,0:T(8,128)(2,1)}, bf16[128,5120]{1,0:T(8,128)(2,1)S(1)}, u32[]{:S(2)}) copy-start(bf16[128,5120]{1,0:T(8,128)(2,1)S(1)} %collective-permute-done.17) | copy-start | bytes 3932164
  446.8 72.0 %collective-permute-start.15 = (bf16[128,5120]{1,0:T(8,128)(2,1)}, bf16[128,5120]{1,0:T(8,128)(2,1)}, u32[]{:S(2)}, u32[]{:S(2)}) collective-permute-start(bf16[128,5120]{1,0:T(8,128)(2,1)} %get-tuple-element.20), channel_id=1, source_target_pairs={{16,0},{20,4},{24,8},{28,12},{32,16},{36,20},{40,24},{44,28},{48,3... | collective-permute-start | bytes 3932168 | tf_op jit(solution)/shard_map/ppermute | solution.py:27
  511.7 3.0 copy-start.21
  511.7 37.7 %collective-permute-start.14 = (bf16[128,5120]{1,0:T(8,128)(2,1)}, bf16[128,5120]{1,0:T(8,128)(2,1)}, u32[]{:S(2)}, u32[]{:S(2)}) collective-permute-start(bf16[128,5120]{1,0:T(8,128)(2,1)} %get-tuple-element.21), channel_id=1, source_target_pairs={{12,0},{16,4},{20,8},{24,12},{28,16},{32,20},{36,24},{40,28},{44,3... | collective-permute-start | bytes 3932168 | tf_op jit(solution)/shard_map/ppermute | solution.py:27
  514.8 3.3 copy-start.3
  514.8 3.3 copy-start.24
  514.8 3.3 copy-start.26
  518.1 31.4 %copy-start.28 = (pred[128]{0:T(512)(128)(4,1)S(1)}, pred[128]{0:T(512)(128)(4,1)}, u32[]{:S(2)}) copy-start(pred[128]{0:T(512)(128)(4,1)} %constant.68.clone.1) | copy-start | bytes 388
  518.1 31.3 %copy-start.5 = (f32[192,5120]{1,0:T(8,128)S(1)}, f32[192,5120]{1,0:T(8,128)}, u32[]{:S(2)}) copy-start(f32[192,5120]{1,0:T(8,128)} %copy-done.4) | copy-start | bytes 11796484
  518.2 31.3 %copy-start.18 = (bf16[128,5120]{1,0:T(8,128)(2,1)S(1)}, bf16[128,5120]{1,0:T(8,128)(2,1)}, u32[]{:S(2)}) copy-start(bf16[128,5120]{1,0:T(8,128)(2,1)} %copy-done.17) | copy-start | bytes 3932164
  518.2 31.3 %copy-start.20 = (bf16[128,5120]{1,0:T(8,128)(2,1)S(1)}, bf16[128,5120]{1,0:T(8,128)(2,1)}, u32[]{:S(2)}) copy-start(bf16[128,5120]{1,0:T(8,128)(2,1)} %copy-done.19) | copy-start | bytes 3932164
  518.2 31.3 %copy-start.22 = (bf16[128,5120]{1,0:T(8,128)(2,1)S(1)}, bf16[128,5120]{1,0:T(8,128)(2,1)}, u32[]{:S(2)}) copy-start(bf16[128,5120]{1,0:T(8,128)(2,1)} %copy-done.21) | copy-start | bytes 3932164
where the time goes:
time: 562 us; the launch traced here: 555 us
  waiting for transfers between devices  290 us (52%)
  starting transfers between devices  147 us (26%)
  local copies, waits for them, and re-layouts  59.1 us (11%)
  matrix products  35.6 us (6%)
  other arithmetic  21.8 us (4%)
    ppermute x16, waiting for transfers between devices, from_behind(): return lax.ppermute(x, axis, pairs)  257 us
    ppermute x16, starting transfers between devices, from_behind(): return lax.ppermute(x, axis, pairs)  136 us
    ppermute x2, waiting for transfers between devices, extended(): lax.ppermute(lax.slice_in_dim(block, block.shape[dim] - width, None, axis...  32.7 us
    unnamed x73, local copies, waits for them, and re-layouts  21.2 us
  transfers between devices with their start and end apart: 20, of which 7 were waited for; matrix products, arithmetic and copies ran while one was open for 7% of the time, Pallas kernels for 0%

commit v1 on v0

v1 whole, which is shorter than its diff:
```python
import functools

import jax
import jax.numpy as jnp
from jax import lax
from jax.experimental import pallas as pl
from jax.experimental.pallas import tpu as pltpu
from jax.sharding import Mesh, PartitionSpec as P

HEADS = 20
DIM = 128
TOK = 128
HALO = 32
N_Z, N_Y, N_X = 4, 4, 2
N_LOC = N_Y * N_X
FULL = 2
SLOTS = 3
HALF = TOK // 2
Q_ROWS = FULL * TOK + HALF
LOW = -1.0e30
FACTOR = DIM ** -0.5
LOG2E = 1.4426950408889634
AXES = ("z", "y", "xh", "xl", "core")
F32 = jnp.float32
BF16 = jnp.bfloat16


def head_of(place, slot):
    y, x = place // N_X, place % N_X
    return 5 * y + (2 * x + slot if slot < FULL else 4)


def cols(head):
    return slice(head * DIM, (head + 1) * DIM)


def pack_kv_kernel(k_ref, v_ref, out_ref):
    for place in range(N_LOC):
        for slot in range(SLOTS):
            head = head_of(place, slot)
            out_ref[place, 0, slot] = k_ref[:, cols(head)]
            out_ref[place, 1, slot] = v_ref[:, cols(head)]


def pack_q_kernel(q_ref, do_ref, out_ref):
    for place in range(N_LOC):
        start = (place % N_X) * HALF
        for kind, ref in enumerate((q_ref, do_ref)):
            for slot in range(FULL):
                out_ref[place, kind, slot * TOK : (slot + 1) * TOK] = ref[:, cols(head_of(place, slot))]
            out_ref[place, kind, FULL * TOK : Q_ROWS] = ref[start : start + HALF, cols(head_of(place, FULL))]


def unpack_q_kernel(in_ref, o_ref, dq_ref):
    for place in range(N_LOC):
        start = (place % N_X) * HALF
        for kind, ref in enumerate((o_ref, dq_ref)):
            for slot in range(FULL):
                ref[:, cols(head_of(place, slot))] = in_ref[place, kind, slot * TOK : (slot + 1) * TOK]
            ref[start : start + HALF, cols(head_of(place, FULL))] = in_ref[place, kind, FULL * TOK : Q_ROWS]


def unpack_kv_kernel(in_ref, dk_ref, dv_ref):
    for y in range(N_Y):
        for kind, ref in enumerate((dk_ref, dv_ref)):
            for x in range(N_X):
                place = y * N_X + x
                for slot in range(FULL):
                    ref[:, cols(head_of(place, slot))] = in_ref[place, kind, slot]
            both = in_ref[y * N_X, kind, FULL].astype(F32) + in_ref[y * N_X + 1, kind, FULL].astype(F32)
            ref[:, cols(head_of(y * N_X, FULL))] = both.astype(BF16)


def merge_kernel(own_ref, past_ref, from_low_ref, from_high_ref, out_ref):
    for loc in range(N_LOC):
        for kind in range(2):
            total = own_ref[loc, kind, 0] + past_ref[loc, kind, 0].astype(F32)
            first = total[:HALO] + from_low_ref[loc, kind, 0].astype(F32)
            last = total[TOK - HALO :] + from_high_ref[loc, kind, 0].astype(F32)
            out_ref[loc, kind, 0, :HALO] = first.astype(BF16)
            out_ref[loc, kind, 0, HALO : TOK - HALO] = total[HALO : TOK - HALO].astype(BF16)
            out_ref[loc, kind, 0, TOK - HALO :] = last.astype(BF16)


def dot_nt(a, b):
    return lax.dot_general(a, b, (((1,), (1,)), ((), ())), preferred_element_type=F32)


def dot_nn(a, b):
    return lax.dot_general(a, b, (((1,), (0,)), ((), ())), preferred_element_type=F32)


N_WIN = 10
WIN = N_WIN * TOK
ROWS = WIN + TOK


def attention_job(
    rows, row_start, pair, slot, window, z, xh, tile,
    q_ref, low_ref, high_ref, o_ref, dlow_ref, dhigh_ref,
    kcat, vcat, ktr, vtr, dkacc, dvacc, s_ref, p_ref, ds_ref,
):
    lanes = 2 * rows
    base = pl.multiple_of(pair * (2 * TOK), 2 * TOK)
    la, lb = 2 * pair, 2 * pair + 1
    q = jnp.concatenate([q_ref[la, 0, row_start : row_start + rows], q_ref[lb, 0, row_start : row_start + rows]], axis=0)
    do = jnp.concatenate([q_ref[la, 1, row_start : row_start + rows], q_ref[lb, 1, row_start : row_start + rows]], axis=0)

    def border(kind):
        return jnp.concatenate([low_ref[la, kind, 0], high_ref[la, kind, 0], low_ref[lb, kind, 0], high_ref[lb, kind, 0]], axis=0)

    k_border, v_border = border(0), border(1)
    scale = FACTOR * LOG2E
    row = lax.broadcasted_iota(jnp.int32, (TOK, lanes), 0)
    lane = lax.broadcasted_iota(jnp.int32, (TOK, lanes), 1)
    is_b = lane >= rows
    place = jnp.where(is_b, lane - rows, lane) + (xh * HALF if rows < TOK else 0)
    near = jnp.abs(place - row) <= window
    half_row = row % (2 * HALO)
    border_place = jnp.where(half_row < HALO, half_row - HALO, half_row + TOK - HALO)
    first = jnp.where(tile > 0, -HALO, 0)
    end = jnp.where(tile < 3, TOK + HALO, TOK)
    border_ok = (jnp.abs(place - border_place) <= window) & (border_place >= first) & (border_place < end)
    border_ok &= jnp.where(row >= 2 * HALO, 1, 0) == jnp.where(is_b, 1, 0)

    tops = []
    biases = []
    for b in range(N_WIN + 1):
        if b < N_WIN:
            keys = kcat[pl.ds(base + b * TOK, TOK), :]
        else:
            keys = k_border
        s = dot_nt(keys, q)
        if b == 0:
            s = jnp.where(is_b, LOW, s)
        elif b == 8:
            s = jnp.where(is_b | near, s, LOW)
        elif b == 9:
            s = jnp.where(is_b & near, s, LOW)
        elif b == N_WIN:
            s = jnp.where(border_ok, s, LOW)
        s_ref[b * TOK : (b + 1) * TOK, :lanes] = s
        top = jnp.max(s.reshape(TOK // 8, 8, lanes), axis=0) * scale
        if b < 8:
            bias = jnp.where((z == 0) & (2 * pair + b < N_LOC), LOW, 0.0)
            top = top + bias
        else:
            bias = None
        tops.append(top)
        biases.append(bias)
    top = functools.reduce(jnp.maximum, tops)
    top = jnp.max(top, axis=0, keepdims=True)
    total = jnp.zeros((8, lanes), F32)
    for b in range(N_WIN + 1):
        shift = -top if biases[b] is None else biases[b] - top
        e = jnp.exp2(s_ref[b * TOK : (b + 1) * TOK, :lanes] * scale + shift)
        s_ref[b * TOK : (b + 1) * TOK, :lanes] = e
        total = total + jnp.sum(e.reshape(TOK // 8, 8, lanes), axis=0)
    inverse = 1.0 / jnp.sum(total, axis=0, keepdims=True)
    for b in range(N_WIN + 1):
        probs = s_ref[b * TOK : (b + 1) * TOK, :lanes] * inverse
        s_ref[b * TOK : (b + 1) * TOK, :lanes] = probs
        p_ref[b * TOK : (b + 1) * TOK, :lanes] = probs.astype(BF16)
    out_t = dot_nn(vtr[:, pl.ds(base, WIN)], p_ref[:WIN, :lanes])
    out_t = out_t + dot_nn(v_border.T, p_ref[WIN:, :lanes])
    out_b = out_t.astype(BF16).astype(F32)
    delta = jnp.sum(out_b * do.astype(F32).T, axis=0, keepdims=True)
    out = out_b.T.astype(BF16)
    o_ref[la, 0, row_start : row_start + rows] = out[:rows]
    o_ref[lb, 0, row_start : row_start + rows] = out[rows:]
    for b in range(N_WIN + 1):
        if b < N_WIN:
            vals = vcat[pl.ds(base + b * TOK, TOK), :]
        else:
            vals = v_border
        dp = dot_nt(vals, do)
        ds = s_ref[b * TOK : (b + 1) * TOK, :lanes] * (dp - delta)
        ds_ref[b * TOK : (b + 1) * TOK, :lanes] = ds.astype(BF16)
    dq_t = dot_nn(ktr[:, pl.ds(base, WIN)], ds_ref[:WIN, :lanes])
    dq_t = dq_t + dot_nn(k_border.T, ds_ref[WIN:, :lanes])
    dq = (dq_t * FACTOR).T.astype(BF16)
    o_ref[la, 1, row_start : row_start + rows] = dq[:rows]
    o_ref[lb, 1, row_start : row_start + rows] = dq[rows:]
    for b in range(N_WIN):
        at = pl.ds(base + b * TOK, TOK)
        dvacc[at, :] += dot_nn(p_ref[b * TOK : (b + 1) * TOK, :lanes], do)
        dkacc[at, :] += dot_nn(ds_ref[b * TOK : (b + 1) * TOK, :lanes], q)
    dv_border = dot_nn(p_ref[WIN:, :lanes], do).astype(BF16)
    dk_border = (dot_nn(ds_ref[WIN:, :lanes], q) * FACTOR).astype(BF16)
    for kind, grad in enumerate((dk_border, dv_border)):
        for which, loc in enumerate((la, lb)):
            at = which * 2 * HALO
            dlow_ref[loc, kind, 0] = grad[at : at + HALO]
            dhigh_ref[loc, kind, 0] = grad[at + HALO : at + 2 * HALO]


def attention_kernel(
    window_ref, kv_ref, past_ref, low_ref, high_ref, q_ref,
    o_ref, own_ref, back_ref, dlow_ref, dhigh_ref,
    kcat, vcat, ktr, vtr, dkacc, dvacc, s_ref, p_ref, ds_ref,
):
    slot, pair = pl.program_id(0), pl.program_id(1)
    z, y, xh = lax.axis_index("z"), lax.axis_index("y"), lax.axis_index("xh")
    tile = lax.axis_index("xl") * 2 + lax.axis_index("core")

    @pl.when(pair == 0)
    def _():
        for kind, cat, tr in ((0, kcat, ktr), (1, vcat, vtr)):
            for loc in range(2 * N_LOC):
                src = past_ref if loc < N_LOC else kv_ref
                block = src[loc % N_LOC, kind, 0]
                cat[loc * TOK : (loc + 1) * TOK, :] = block
                tr[:, loc * TOK : (loc + 1) * TOK] = block.T
        dkacc[...] = jnp.zeros_like(dkacc)
        dvacc[...] = jnp.zeros_like(dvacc)

    head = 5 * y + jnp.where(slot < FULL, 2 * xh + slot, 4)
    window = window_ref[head]
    rest = (
        q_ref, low_ref, high_ref, o_ref, dlow_ref, dhigh_ref,
        kcat, vcat, ktr, vtr, dkacc, dvacc, s_ref, p_ref, ds_ref,
    )
    for which in range(SLOTS):
        @pl.when(slot == which)
        def _(which=which):
            rows = TOK if which < FULL else HALF
            attention_job(rows, which * TOK, pair, slot, window, z, xh, tile, *rest)

    @pl.when(pair == N_LOC // 2 - 1)
    def _():
        for kind, acc in ((0, dkacc), (1, dvacc)):
            for loc in range(N_LOC):
                low = acc[loc * TOK : (loc + 1) * TOK, :]
                high = acc[(N_LOC + loc) * TOK : (N_LOC + loc + 1) * TOK, :]
                back_ref[loc, kind, 0] = (low * FACTOR if kind == 0 else low).astype(BF16)
                own_ref[loc, kind, 0] = high * FACTOR if kind == 0 else high


def whole(shape):
    return pl.BlockSpec(shape, lambda *_: (0,) * len(shape))


def simple_call(kernel, out_shapes, *args):
    outs = [jax.ShapeDtypeStruct(s, BF16) for s in out_shapes]
    moved = sum(a.size * a.dtype.itemsize for a in args) + sum(2 * o.size for o in outs)
    return pl.pallas_call(
        kernel,
        grid=(1,),
        out_shape=outs,
        in_specs=[whole(a.shape) for a in args],
        out_specs=[whole(s) for s in out_shapes],
        compiler_params=pltpu.CompilerParams(vmem_limit_bytes=32 * 2**20),
        cost_estimate=pl.CostEstimate(flops=0, bytes_accessed=moved, transcendentals=0),
    )(*args)


def by_slot(rows):
    return pl.BlockSpec((N_LOC, 2, 1, rows, DIM), lambda slot, *_: (0, 0, slot, 0, 0))


def attention(window, kv, past, low, high, qdo):
    kv_shape = (N_LOC, 2, SLOTS, TOK, DIM)
    border_shape = (N_LOC, 2, SLOTS, HALO, DIM)
    return pl.pallas_call(
        attention_kernel,
        grid=(SLOTS, N_LOC // 2),
        out_shape=[
            jax.ShapeDtypeStruct(qdo.shape, BF16),
            jax.ShapeDtypeStruct(kv_shape, F32),
            jax.ShapeDtypeStruct(kv_shape, BF16),
            jax.ShapeDtypeStruct(border_shape, BF16),
            jax.ShapeDtypeStruct(border_shape, BF16),
        ],
        in_specs=[
            pl.BlockSpec(memory_space=pltpu.SMEM),
            by_slot(TOK), by_slot(TOK), by_slot(HALO), by_slot(HALO),
            whole(qdo.shape),
        ],
        out_specs=[whole(qdo.shape), by_slot(TOK), by_slot(TOK), by_slot(HALO), by_slot(HALO)],
        scratch_shapes=[
            pltpu.VMEM((2 * N_LOC * TOK, DIM), BF16),
            pltpu.VMEM((2 * N_LOC * TOK, DIM), BF16),
            pltpu.VMEM((DIM, 2 * N_LOC * TOK), BF16),
            pltpu.VMEM((DIM, 2 * N_LOC * TOK), BF16),
            pltpu.VMEM((2 * N_LOC * TOK, DIM), F32),
            pltpu.VMEM((2 * N_LOC * TOK, DIM), F32),
            pltpu.VMEM((ROWS, 2 * TOK), F32),
            pltpu.VMEM((ROWS, 2 * TOK), BF16),
            pltpu.VMEM((ROWS, 2 * TOK), BF16),
        ],
        compiler_params=pltpu.CompilerParams(vmem_limit_bytes=48 * 2**20),
        cost_estimate=pl.CostEstimate(flops=6 * 10**9, bytes_accessed=10**7, transcendentals=4 * 10**6),
    )(window, kv, past, low, high, qdo)


def swap(x):
    return lax.all_to_all(x, ("y", "xh"), 0, 0)


def shards(queries, keys, values, cotangent, window):
    kv_shape = (N_LOC, 2, SLOTS, TOK, DIM)
    q_shape = (N_LOC, 2, Q_ROWS, DIM)
    up = [(i, i + 1) for i in range(N_Z - 1)]
    down = [(i + 1, i) for i in range(N_Z - 1)]
    tiles = ("xl", "core")
    (packed_kv,) = simple_call(pack_kv_kernel, [kv_shape], keys, values)
    (packed_q,) = simple_call(pack_q_kernel, [q_shape], queries, cotangent)
    kv = swap(packed_kv)
    past = lax.ppermute(kv, "z", up)
    low = lax.ppermute(kv[:, :, :, TOK - HALO :], tiles, up)
    high = lax.ppermute(kv[:, :, :, :HALO], tiles, down)
    qdo = swap(packed_q)
    odq, own, back, dlow, dhigh = attention(window, kv, past, low, high, qdo)
    past_grads = lax.ppermute(back, "z", down)
    from_high = lax.ppermute(dlow, tiles, down)
    from_low = lax.ppermute(dhigh, tiles, up)
    out_q = swap(odq)
    (merged,) = pl.pallas_call(
        merge_kernel,
        grid=(SLOTS,),
        out_shape=[jax.ShapeDtypeStruct(kv_shape, BF16)],
        in_specs=[by_slot(TOK), by_slot(TOK), by_slot(HALO), by_slot(HALO)],
        out_specs=[by_slot(TOK)],
        compiler_params=pltpu.CompilerParams(vmem_limit_bytes=32 * 2**20),
        cost_estimate=pl.CostEstimate(flops=10**6, bytes_accessed=8 * 10**6, transcendentals=0),
    )(own, past_grads, from_low, from_high)
    out_kv = swap(merged)
    attended, grad_queries = simple_call(unpack_q_kernel, [queries.shape] * 2, out_q)
    grad_keys, grad_values = simple_call(unpack_kv_kernel, [keys.shape] * 2, out_kv)
    return attended, grad_queries, grad_keys, grad_values


def solution(mesh):
    fine = Mesh(mesh.devices.reshape(N_Z, N_Y, N_X, 2, 2), AXES)
    rows = P(AXES, None)
    return jax.shard_map(
        shards,
        mesh=fine,
        in_specs=(rows, rows, rows, rows, P()),
        out_specs=(rows, rows, rows, rows),
        check_vma=False,
    )
```

time: 562 us -> 165 us (0.29)
  the two profiles are of different devices: /device:TPU:30 before, /device:TPU:0 now
where the time goes in v1:
time: 165 us; the launch traced here: 164 us
  waiting for transfers between devices  69.4 us (42%)
  Pallas kernels  33.2 us (20%)
  blocking collectives  29.9 us (18%)
  starting transfers between devices  24.1 us (15%)
  local copies, waits for them, and re-layouts  7.07 us (4%)
    all_to_all x3, waiting for transfers between devices, swap(): return lax.all_to_all(x, ('y', 'xh'), 0, 0)  34.9 us
    all_to_all x1, blocking collectives, swap(): return lax.all_to_all(x, ('y', 'xh'), 0, 0)  29.9 us
    pallas_call x1, Pallas kernels, attention(): pl.pallas_call(attention_kernel, grid=(SLOTS, N_LOC // 2), out_shape=[jax...  27 us
    ppermute x1, waiting for transfers between devices, shards(): past_grads = lax.ppermute(back, 'z', down)  26.1 us
    all_to_all x3, starting transfers between devices, swap(): return lax.all_to_all(x, ('y', 'xh'), 0, 0)  10.9 us
    unnamed x16, local copies, waits for them, and re-layouts  5.89 us
    ppermute x1, waiting for transfers between devices, shards(): past = lax.ppermute(kv, 'z', up)  5.14 us
    ppermute x1, starting transfers between devices, shards(): past = lax.ppermute(kv, 'z', up)  5 us
  transfers between devices with their start and end apart: 9, of which 6 were waited for; matrix products, arithmetic and copies ran while one was open for 1% of the time, Pallas kernels for 3%

profile of v1, /device:TPU:0, one launch (start us, length us, event | category | flops | bytes accessed | tf_op | source)
XLA Modules:
  0.0 164.4 jit_solution(15210115137554140178)
XLA Ops:
  0.6 0.0 copy-start.4
  0.6 1.1 copy-done.4
  1.7 0.0 copy-start.5
  1.7 1.1 copy-done.5
  2.8 0.2 shard_map.84
  3.1 0.0 copy-start.2
  3.1 0.0 copy-start.3
  3.1 29.9 %all_to_all.20.kv_ref = bf16[8,2,3,128,128]{4,3,2,1,0:T(8,128)(2,1)} all-to-all(bf16[8,2,3,128,128]{4,3,2,1,0:T(8,128)(2,1)S(1)} %shard_map.84), channel_id=1, replica_groups=mesh['z'=4,'y'=4,'xh'=2,'xl'=2,'core'=2] {'y','xh'}, dimensions={0} | all-to-all | bytes 3145728 | tf_op jit(solution)/shard_map/all_to_all | solution.py:297
  33.0 5.0 %collective-permute-start = (bf16[8,2,3,128,128]{4,3,2,1,0:T(8,128)(2,1)}, bf16[8,2,3,128,128]{4,3,2,1,0:T(8,128)(2,1)}, u32[]{:S(2)}, u32[]{:S(2)}) collective-permute-start(bf16[8,2,3,128,128]{4,3,2,1,0:T(8,128)(2,1)} %all_to_all.20.kv_ref), channel_id=1, source_target_pairs={{0,32},{32,64},{64,96},{1,33},{33,65},{65,97},{2,34},{34,66},{66,9... | collective-permute-start | bytes 4718600 | tf_op jit(solution)/shard_map/ppermute | solution.py:309
  38.0 0.0 copy-done.2
  38.0 0.0 copy-done.3
  38.0 1.3 shard_map.85
  39.3 0.0 copy-start.7
  39.3 3.7 %all-to-all-start.1 = ((bf16[8,2,320,128]{3,2,1,0:T(8,128)(2,1)}), bf16[8,2,320,128]{3,2,1,0:T(8,128)(2,1)S(1)}, u32[]{:S(2)}, u32[]{:S(2)}) async-start(bf16[8,2,320,128]{3,2,1,0:T(8,128)(2,1)} %shard_map.85), calls=%async_computation.1 | async-start | bytes 2621440 | tf_op jit(solution)/shard_map/all_to_all | solution.py:297
  43.0 1.2 fusion
  44.1 1.3 collective-permute-start.2
  45.4 3.1 %collective-permute-start.1 = (bf16[8,2,3,32,128]{4,3,2,1,0:T(8,128)(2,1)S(1)}, bf16[8,2,3,32,128]{4,3,2,1,0:T(8,128)(2,1)S(1)}, u32[]{:S(2)}, u32[]{:S(2)}) collective-permute-start(bf16[8,2,3,32,128]{4,3,2,1,0:T(8,128)(2,1)S(1)} %get-tuple-element.23), channel_id=1, source_target_pairs={{0,1},{1,2},{2,3},{4,5},{5,6},{6,7},{8,9},{9,10},{10,11},{12,13},{... | collective-permute-start | bytes 1179656 | tf_op jit(solution)/shard_map/ppermute | solution.py:310
  48.5 15.9 %all-to-all-done.1.q_ref = bf16[8,2,320,128]{3,2,1,0:T(8,128)(2,1)S(1)} async-done(((bf16[8,2,320,128]{3,2,1,0:T(8,128)(2,1)}), bf16[8,2,320,128]{3,2,1,0:T(8,128)(2,1)S(1)}, u32[]{:S(2)}, u32[]{:S(2)}) %all-to-all-start.1) | async-done | bytes 1310752 | tf_op jit(solution)/shard_map/all_to_all | solution.py:297
  64.4 0.0 collective-permute-done.2.high_ref
  64.4 0.0 collective-permute-done.1.low_ref
  64.4 5.1 %collective-permute-done.past_ref = bf16[8,2,3,128,128]{4,3,2,1,0:T(8,128)(2,1)} collective-permute-done((bf16[8,2,3,128,128]{4,3,2,1,0:T(8,128)(2,1)}, bf16[8,2,3,128,128]{4,3,2,1,0:T(8,128)(2,1)}, u32[]{:S(2)}, u32[]{:S(2)}) %collective-permute-start) | collective-permute-done | bytes 1572896 | tf_op jit(solution)/shard_map/ppermute | solution.py:309
  69.5 0.0 copy-done.7
  69.5 27.0 %shard_map.86 = (bf16[8,2,320,128]{3,2,1,0:T(8,128)(2,1)S(1)}, f32[8,2,3,128,128]{4,3,2,1,0:T(8,128)}, bf16[8,2,3,128,128]{4,3,2,1,0:T(8,128)(2,1)}, bf16[8,2,3,...) custom-call(s32[20]{0:T(128)S(1)} %copy-done.7, bf16[8,2,3,128,128]{4,3,2,1,0:T(8,128)(2,1)} %all_to_all.20.kv_ref, ...), custom_call_target="tpu_custom_call" | custom-call | flops 6000000000 | bytes 10000000 | tf_op jit(solution)/shard_map/pallas_call | solution.py:264
  96.6 0.0 copy-start.1
  96.6 1.1 copy-done.1
  97.6 0.0 copy-start.6
  97.6 0.7 copy-done.6
  98.4 1.3 collective-permute-start.3
  99.7 3.6 %all-to-all-start.2 = ((bf16[8,2,320,128]{3,2,1,0:T(8,128)(2,1)}), bf16[8,2,320,128]{3,2,1,0:T(8,128)(2,1)S(1)}, u32[]{:S(2)}, u32[]{:S(2)}) async-start(bf16[8,2,320,128]{3,2,1,0:T(8,128)(2,1)} %copy-done.1), calls=%async_computation.2 | async-start | bytes 2621440 | tf_op jit(solution)/shard_map/all_to_all | solution.py:297
  103.3 1.3 collective-permute-start.4
  104.6 1.3 collective-permute-start.5
  105.9 0.2 collective-permute-done.4.from_low_ref
  106.1 3.0 %collective-permute-done.5.from_high_ref = bf16[8,2,3,32,128]{4,3,2,1,0:T(8,128)(2,1)S(1)} collective-permute-done((bf16[8,2,3,32,128]{4,3,2,1,0:T(8,128)(2,1)S(1)}, bf16[8,2,3,32,128]{4,3,2,1,0:T(8,128)(2,1)S(1)}, u32[]{:S(2)}, u32[]{:S(2)}) %collective-permute-start.5) | collective-permute-done | bytes 393248 | tf_op jit(solution)/shard_map/ppermute | solution.py:315
  109.1 26.1 %collective-permute-done.3.past_ref = bf16[8,2,3,128,128]{4,3,2,1,0:T(8,128)(2,1)S(1)} collective-permute-done((bf16[8,2,3,128,128]{4,3,2,1,0:T(8,128)(2,1)}, bf16[8,2,3,128,128]{4,3,2,1,0:T(8,128)(2,1)S(1)}, u32[]{:S(2)}, u32[]{:S(2)}) %collective-permute-start.3) | collective-permute-done | bytes 1572896 | tf_op jit(solution)/shard_map/ppermute | solution.py:314
  135.3 0.0 copy-start
  135.3 1.9 %copy-done = f32[8,2,3,128,128]{4,3,2,1,0:T(8,128)S(1)} copy-done((f32[8,2,3,128,128]{4,3,2,1,0:T(8,128)S(1)}, f32[8,2,3,128,128]{4,3,2,1,0:T(8,128)}, u32[]{:S(2)}) %copy-start) | copy-done | bytes 3145752
  137.2 2.1 %shard_map.88 = bf16[8,2,3,128,128]{4,3,2,1,0:T(8,128)(2,1)} custom-call(f32[8,2,3,128,128]{4,3,2,1,0:T(8,128)S(1)} %copy-done, bf16[8,2,3,128,128]{4,3,2,1,0:T(8,128)(2,1)S(1)} %collective-permute-done.3.past_ref, bf16[8,2,3,32,128]{4,3,2,1,0:T(8,128)(2,1)S(1)} %collective-permute-done.4.from_low_ref, ...), custom_call_target="tpu_custom_call" | custom-call | flops 1000000 | bytes 8000000 | tf_op jit(solution)/shard_map/pallas_call | solution.py:318
  139.3 0.0 all-to-all-done.2.in_ref
  139.3 3.6 %all-to-all-start.3 = ((bf16[8,2,3,128,128]{4,3,2,1,0:T(8,128)(2,1)}), bf16[8,2,3,128,128]{4,3,2,1,0:T(8,128)(2,1)S(1)}, u32[]{:S(2)}, u32[]{:S(2)}) async-start(bf16[8,2,3,128,128]{4,3,2,1,0:T(8,128)(2,1)} %shard_map.88), calls=%async_computation.3 | async-start | bytes 3145728 | tf_op jit(solution)/shard_map/all_to_all | solution.py:297
  142.9 1.3 shard_map.87
  144.1 19.0 %all-to-all-done.3.in_ref = bf16[8,2,3,128,128]{4,3,2,1,0:T(8,128)(2,1)S(1)} async-done(((bf16[8,2,3,128,128]{4,3,2,1,0:T(8,128)(2,1)}), bf16[8,2,3,128,128]{4,3,2,1,0:T(8,128)(2,1)S(1)}, u32[]{:S(2)}, u32[]{:S(2)}) %all-to-all-start.3) | async-done | bytes 1572896 | tf_op jit(solution)/shard_map/all_to_all | solution.py:297
  163.1 1.3 shard_map.89
Async XLA Ops:
  0.6 1.1 copy-start.4
  1.7 1.1 copy-start.5
  3.1 34.9 %copy-start.2 = (bf16[128,2560]{1,0:T(8,128)(2,1)S(1)}, bf16[128,2560]{1,0:T(8,128)(2,1)}, u32[]{:S(2)}) copy-start(bf16[128,2560]{1,0:T(8,128)(2,1)} %q_ref.1) | copy-start | bytes 1966084
  3.1 34.9 %copy-start.3 = (bf16[128,2560]{1,0:T(8,128)(2,1)S(1)}, bf16[128,2560]{1,0:T(8,128)(2,1)}, u32[]{:S(2)}) copy-start(bf16[128,2560]{1,0:T(8,128)(2,1)} %do_ref.1) | copy-start | bytes 1966084
  33.0 36.6 %collective-permute-start = (bf16[8,2,3,128,128]{4,3,2,1,0:T(8,128)(2,1)}, bf16[8,2,3,128,128]{4,3,2,1,0:T(8,128)(2,1)}, u32[]{:S(2)}, u32[]{:S(2)}) collective-permute-start(bf16[8,2,3,128,128]{4,3,2,1,0:T(8,128)(2,1)} %all_to_all.20.kv_ref), channel_id=1, source_target_pairs={{0,32},{32,64},{64,96},{1,33},{33,65},{65,97},{2,34},{34,66},{66,9... | collective-permute-start | bytes 4718600 | tf_op jit(solution)/shard_map/ppermute | solution.py:309
  39.3 30.3 %copy-start.7 = (s32[20]{0:T(128)S(1)}, s32[20]{0:T(128)}, u32[]{:S(2)}) copy-start(s32[20]{0:T(128)} %window_ref.1) | copy-start | bytes 244
  39.3 25.1 %all-to-all-start.1 = ((bf16[8,2,320,128]{3,2,1,0:T(8,128)(2,1)}), bf16[8,2,320,128]{3,2,1,0:T(8,128)(2,1)S(1)}, u32[]{:S(2)}, u32[]{:S(2)}) async-start(bf16[8,2,320,128]{3,2,1,0:T(8,128)(2,1)} %shard_map.85), calls=%async_computation.1 | async-start | bytes 2621440 | tf_op jit(solution)/shard_map/all_to_all | solution.py:297
  44.1 20.2 %collective-permute-start.2 = (bf16[8,2,3,32,128]{4,3,2,1,0:T(8,128)(2,1)S(1)}, bf16[8,2,3,32,128]{4,3,2,1,0:T(8,128)(2,1)S(1)}, u32[]{:S(2)}, u32[]{:S(2)}) collective-permute-start(bf16[8,2,3,32,128]{4,3,2,1,0:T(8,128)(2,1)S(1)} %get-tuple-element.22), channel_id=1, source_target_pairs={{1,0},{2,1},{3,2},{5,4},{6,5},{7,6},{9,8},{10,9},{11,10},{13,12},{... | collective-permute-start | bytes 1179656 | tf_op jit(solution)/shard_map/ppermute | solution.py:311
  45.4 18.9 %collective-permute-start.1 = (bf16[8,2,3,32,128]{4,3,2,1,0:T(8,128)(2,1)S(1)}, bf16[8,2,3,32,128]{4,3,2,1,0:T(8,128)(2,1)S(1)}, u32[]{:S(2)}, u32[]{:S(2)}) collective-permute-start(bf16[8,2,3,32,128]{4,3,2,1,0:T(8,128)(2,1)S(1)} %get-tuple-element.23), channel_id=1, source_target_pairs={{0,1},{1,2},{2,3},{4,5},{5,6},{6,7},{8,9},{9,10},{10,11},{12,13},{... | collective-permute-start | bytes 1179656 | tf_op jit(solution)/shard_map/ppermute | solution.py:310
  96.6 1.1 copy-start.1
  97.6 0.7 copy-start.6
  98.4 36.9 %collective-permute-start.3 = (bf16[8,2,3,128,128]{4,3,2,1,0:T(8,128)(2,1)}, bf16[8,2,3,128,128]{4,3,2,1,0:T(8,128)(2,1)S(1)}, u32[]{:S(2)}, u32[]{:S(2)}) collective-permute-start(bf16[8,2,3,128,128]{4,3,2,1,0:T(8,128)(2,1)} %get-tuple-element.17), channel_id=1, source_target_pairs={{32,0},{64,32},{96,64},{33,1},{65,33},{97,65},{34,2},{66,34},{98,6... | collective-permute-start | bytes 4718600 | tf_op jit(solution)/shard_map/ppermute | solution.py:314
  99.7 39.6 %all-to-all-start.2 = ((bf16[8,2,320,128]{3,2,1,0:T(8,128)(2,1)}), bf16[8,2,320,128]{3,2,1,0:T(8,128)(2,1)S(1)}, u32[]{:S(2)}, u32[]{:S(2)}) async-start(bf16[8,2,320,128]{3,2,1,0:T(8,128)(2,1)} %copy-done.1), calls=%async_computation.2 | async-start | bytes 2621440 | tf_op jit(solution)/shard_map/all_to_all | solution.py:297
  103.3 2.8 %collective-permute-start.4 = (bf16[8,2,3,32,128]{4,3,2,1,0:T(8,128)(2,1)}, bf16[8,2,3,32,128]{4,3,2,1,0:T(8,128)(2,1)S(1)}, u32[]{:S(2)}, u32[]{:S(2)}) collective-permute-start(bf16[8,2,3,32,128]{4,3,2,1,0:T(8,128)(2,1)} %copy-done.6), channel_id=1, source_target_pairs={{0,1},{1,2},{2,3},{4,5},{5,6},{6,7},{8,9},{9,10},{10,11},{12,13},{... | collective-permute-start | bytes 1179656 | tf_op jit(solution)/shard_map/ppermute | solution.py:316
  104.6 4.5 %collective-permute-start.5 = (bf16[8,2,3,32,128]{4,3,2,1,0:T(8,128)(2,1)S(1)}, bf16[8,2,3,32,128]{4,3,2,1,0:T(8,128)(2,1)S(1)}, u32[]{:S(2)}, u32[]{:S(2)}) collective-permute-start(bf16[8,2,3,32,128]{4,3,2,1,0:T(8,128)(2,1)S(1)} %get-tuple-element.19), channel_id=1, source_target_pairs={{1,0},{2,1},{3,2},{5,4},{6,5},{7,6},{9,8},{10,9},{11,10},{13,12},{... | collective-permute-start | bytes 1179656 | tf_op jit(solution)/shard_map/ppermute | solution.py:315
  135.3 1.9 %copy-start = (f32[8,2,3,128,128]{4,3,2,1,0:T(8,128)S(1)}, f32[8,2,3,128,128]{4,3,2,1,0:T(8,128)}, u32[]{:S(2)}) copy-start(f32[8,2,3,128,128]{4,3,2,1,0:T(8,128)} %get-tuple-element.16.own_ref) | copy-start | bytes 9437188
  139.3 23.9 %all-to-all-start.3 = ((bf16[8,2,3,128,128]{4,3,2,1,0:T(8,128)(2,1)}), bf16[8,2,3,128,128]{4,3,2,1,0:T(8,128)(2,1)S(1)}, u32[]{:S(2)}, u32[]{:S(2)}) async-start(bf16[8,2,3,128,128]{4,3,2,1,0:T(8,128)(2,1)} %shard_map.88), calls=%async_computation.3 | async-start | bytes 3145728 | tf_op jit(solution)/shard_map/all_to_all | solution.py:297

commit v2 on v0

v2 whole, which is shorter than its diff:
```python
import functools
import math

import jax
import jax.numpy as jnp
from jax import lax
from jax.experimental import pallas as pl
from jax.experimental.pallas import tpu as pltpu
from jax.sharding import Mesh, PartitionSpec as P

HEADS = 20
DIM = 128
TOK = 128
HALO = 32
N_Z, N_Y, N_X = 4, 4, 2
N_LOC = N_Y * N_X
FULL = 2
SLOTS = 3
HALF = TOK // 2
Q_ROWS = FULL * TOK + HALF
LOW = -1.0e30
FACTOR = DIM ** -0.5
LOG2E = 1.4426950408889634
ATTEND_MIB = 60
AXES = ("z", "y", "xh", "xl", "core")
PLACES = ("y", "xh")
TILES = ("xl", "core")
F32 = jnp.float32
BF16 = jnp.bfloat16


def head_cols(place, slot):
    head = place // N_X * 5 + (place % N_X * 2 + slot if slot < FULL else 4)
    return slice(head * DIM, (head + 1) * DIM)


def pack_keys_kernel(k_ref, v_ref, kv_ref):
    for place in range(N_LOC):
        for kind, ref in enumerate((k_ref, v_ref)):
            for slot in range(SLOTS):
                kv_ref[place, kind, slot] = ref[:, head_cols(place, slot)]


def pack_queries_kernel(q_ref, do_ref, qdo_ref):
    for place in range(N_LOC):
        start = place % N_X * HALF
        for kind, ref in enumerate((q_ref, do_ref)):
            for slot in range(FULL):
                qdo_ref[place, kind, slot * TOK : (slot + 1) * TOK] = ref[:, head_cols(place, slot)]
            qdo_ref[place, kind, FULL * TOK :] = ref[start : start + HALF, head_cols(place, FULL)]


def unpack_queries_kernel(odq_ref, o_ref, dq_ref):
    for place in range(N_LOC):
        start = place % N_X * HALF
        for kind, ref in enumerate((o_ref, dq_ref)):
            for slot in range(FULL):
                ref[:, head_cols(place, slot)] = odq_ref[place, kind, slot * TOK : (slot + 1) * TOK]
            ref[start : start + HALF, head_cols(place, FULL)] = odq_ref[place, kind, FULL * TOK :]


def unpack_keys_kernel(grads_ref, dk_ref, dv_ref):
    for kind, ref in enumerate((dk_ref, dv_ref)):
        for place in range(N_LOC):
            for slot in range(FULL):
                ref[:, head_cols(place, slot)] = grads_ref[place, kind, slot]
        for place in range(0, N_LOC, N_X):
            both = grads_ref[place, kind, FULL].astype(F32) + grads_ref[place + 1, kind, FULL].astype(F32)
            ref[:, head_cols(place, FULL)] = both.astype(BF16)


def merge_kernel(own_ref, got_ref, from_low_ref, from_high_ref, out_ref):
    for loc in range(own_ref.shape[0]):
        for kind in range(2):
            for slot in range(SLOTS):
                at = (loc, kind, slot)
                total = own_ref[at].astype(F32) + got_ref[at].astype(F32)
                first = total[:HALO] + from_low_ref[at].astype(F32)
                last = total[TOK - HALO :] + from_high_ref[at].astype(F32)
                out_ref[loc, kind, slot, :HALO] = first.astype(BF16)
                out_ref[loc, kind, slot, HALO : TOK - HALO] = total[HALO : TOK - HALO].astype(BF16)
                out_ref[loc, kind, slot, TOK - HALO :] = last.astype(BF16)


def dot_nt(a, b):
    return lax.dot_general(a, b, (((1,), (1,)), ((), ())), preferred_element_type=F32)


def dot_nn(a, b):
    return lax.dot_general(a, b, (((1,), (0,)), ((), ())), preferred_element_type=F32)


LANES = 2 * TOK
UNIT = 2 * TOK
CAT = 2 * N_LOC * TOK
N_PAST = 8


def queries_job(
    rows, job, window, no_past, xh, tile, get_query, get_border, put_query, put_border,
    kcat, vcat, ktr, vtr, q_all, do_all, s_ref, p_ref, ds_ref,
):
    groups = LANES // rows
    n_win = N_PAST + groups
    n_blocks = n_win + groups // 2
    win = n_win * TOK
    base = job * groups * TOK
    locs = [job * groups + g for g in range(groups)]
    lanes = slice(job * LANES, (job + 1) * LANES)
    scale = FACTOR * LOG2E
    window_rows = slice(base, base + win)
    q = jnp.concatenate([get_query(loc, 0) for loc in locs], axis=0)
    do = jnp.concatenate([get_query(loc, 1) for loc in locs], axis=0)
    q_all[lanes, :] = q

    def border(kind, half):
        parts = [get_border(loc, kind, side) for loc in locs[2 * half : 2 * half + 2] for side in range(2)]
        return jnp.concatenate(parts, axis=0)

    row = lax.broadcasted_iota(jnp.int32, (TOK, LANES), 0)
    lane = lax.broadcasted_iota(jnp.int32, (TOK, LANES), 1)
    group = lane // rows
    place = lane - group * rows + (xh * HALF if rows < TOK else 0)
    near = jnp.abs(place - row) <= window
    half_row = row % (2 * HALO)
    border_place = jnp.where(half_row < HALO, half_row - HALO, half_row + TOK - HALO)
    first = jnp.where(tile > 0, -HALO, 0)
    end = jnp.where(tile < 3, TOK + HALO, TOK)
    border_near = (jnp.abs(place - border_place) <= window) & (border_place >= first) & (border_place < end)
    row_group = row // (2 * HALO)

    k_borders = [border(0, half) for half in range(groups // 2)]
    v_borders = [border(1, half) for half in range(groups // 2)]
    top = None
    biases = []
    for b in range(n_blocks):
        keys = kcat[base + b * TOK : base + (b + 1) * TOK, :] if b < n_win else k_borders[b - n_win]
        s = dot_nt(keys, q)
        if b < groups - 1:
            s = jnp.where(group <= b, s, LOW)
        elif N_PAST <= b < n_win:
            s = jnp.where((group > b - N_PAST) | ((group == b - N_PAST) & near), s, LOW)
        elif b >= n_win:
            s = jnp.where(border_near & (row_group + 2 * (b - n_win) == group), s, LOW)
        s_ref[b * TOK : (b + 1) * TOK, :] = s
        here = jnp.max(s.reshape(TOK // 8, 8, LANES), axis=0) * scale
        bias = None
        if b < N_PAST and job * groups + b < N_LOC:
            bias = jnp.where(no_past, LOW, 0.0)
            here = here + bias
        top = here if top is None else jnp.maximum(top, here)
        biases.append(bias)
    top = jnp.max(top, axis=0, keepdims=True)
    total = jnp.zeros((8, LANES), F32)
    for b in range(n_blocks):
        shift = -top if biases[b] is None else biases[b] - top
        e = jnp.exp2(s_ref[b * TOK : (b + 1) * TOK, :] * scale + shift)
        total = total + jnp.sum(e.reshape(TOK // 8, 8, LANES), axis=0)
        if b < n_win:
            p_ref[base + b * TOK : base + (b + 1) * TOK, lanes] = e.astype(BF16)
        else:
            p_ref[CAT + (b - n_win) * TOK : CAT + (b - n_win + 1) * TOK, lanes] = e.astype(BF16)
    inverse = 1.0 / jnp.sum(total, axis=0, keepdims=True)
    do_t = (do.astype(F32).T * inverse).astype(BF16).astype(F32)
    do = do_t.T.astype(BF16)
    do_all[lanes, :] = do
    out_t = dot_nn(vtr[:, window_rows], p_ref[window_rows, lanes])
    for half in range(groups // 2):
        out_t = out_t + dot_nn(v_borders[half].T, p_ref[CAT + half * TOK : CAT + (half + 1) * TOK, lanes])
    out_b = (out_t * inverse).astype(BF16).astype(F32)
    delta = jnp.sum(out_b * do_t, axis=0, keepdims=True)
    out = out_b.T.astype(BF16)
    for g, loc in enumerate(locs):
        put_query(loc, 0, out[g * rows : (g + 1) * rows])
    for b in range(n_blocks):
        vals = vcat[base + b * TOK : base + (b + 1) * TOK, :] if b < n_win else v_borders[b - n_win]
        at = base + b * TOK if b < n_win else CAT + (b - n_win) * TOK
        ds = p_ref[at : at + TOK, lanes].astype(F32) * (dot_nt(vals, do) - delta)
        ds_ref[at : at + TOK, lanes] = ds.astype(BF16)
    dq_t = dot_nn(ktr[:, window_rows], ds_ref[window_rows, lanes])
    for half in range(groups // 2):
        dq_t = dq_t + dot_nn(k_borders[half].T, ds_ref[CAT + half * TOK : CAT + (half + 1) * TOK, lanes])
    dq = (dq_t * FACTOR).T.astype(BF16)
    for g, loc in enumerate(locs):
        put_query(loc, 1, dq[g * rows : (g + 1) * rows])
    for half in range(groups // 2):
        rows_at = slice(CAT + half * TOK, CAT + (half + 1) * TOK)
        dv_border = dot_nn(p_ref[rows_at, lanes], do).astype(BF16)
        dk_border = (dot_nn(ds_ref[rows_at, lanes], q) * FACTOR).astype(BF16)
        for kind, grad in enumerate((dk_border, dv_border)):
            for which, loc in enumerate(locs[2 * half : 2 * half + 2]):
                at = which * 2 * HALO
                put_border(loc, kind, grad[at : at + HALO], grad[at + HALO : at + 2 * HALO])


def keys_job(rows, put_past, put_own, q_all, do_all, p_ref, ds_ref):
    groups = LANES // rows
    jobs = N_LOC // groups
    for unit in range(CAT // UNIT):
        mine = [j for j in range(jobs) if j * groups // 2 <= unit < j * groups // 2 + (N_PAST + groups) // 2]
        lanes = slice(mine[0] * LANES, (mine[-1] + 1) * LANES)
        at = slice(unit * UNIT, (unit + 1) * UNIT)
        dk = dot_nn(ds_ref[at, lanes], q_all[lanes, :]) * FACTOR
        dv = dot_nn(p_ref[at, lanes], do_all[lanes, :])
        for kind, grad in enumerate((dk, dv)):
            for which in range(2):
                loc = unit * 2 + which
                part = grad[which * TOK : (which + 1) * TOK]
                if loc < N_LOC:
                    put_past(loc, kind, part.astype(BF16))
                else:
                    put_own(loc - N_LOC, kind, part.astype(BF16))


def load_keys(get_past, get_own, kcat, vcat, ktr, vtr):
    for kind, cat, tr in ((0, kcat, ktr), (1, vcat, vtr)):
        for loc in range(2 * N_LOC):
            block = get_past(loc, kind) if loc < N_LOC else get_own(loc - N_LOC, kind)
            cat[loc * TOK : (loc + 1) * TOK, :] = block
            tr[:, loc * TOK : (loc + 1) * TOK] = block.T


def attention_body(rows, window, no_past, get_past, get_own, get_query, get_border, put_query, put_border, put_past, put_own, *scratch):
    kcat, vcat, ktr, vtr, q_all, do_all, s0_ref, s1_ref, p_ref, ds_ref = scratch
    xh, tile = lax.axis_index("xh"), lax.axis_index("xl") * 2 + lax.axis_index("core")
    load_keys(get_past, get_own, kcat, vcat, ktr, vtr)
    for job in range(N_LOC * rows // LANES):
        queries_job(
            rows, job, window, no_past, xh, tile, get_query, get_border, put_query, put_border,
            kcat, vcat, ktr, vtr, q_all, do_all, s1_ref if job % 2 else s0_ref, p_ref, ds_ref,
        )
    keys_job(rows, put_past, put_own, q_all, do_all, p_ref, ds_ref)


def put_into(ref, *rest):
    def put(loc, kind, value):
        ref[(loc, kind, *rest)] = value

    return put


def attention_kernel(
    window_ref, kv_ref, past_ref, low_ref, high_ref, q_ref, o_ref, own_ref, back_ref, dlow_ref, dhigh_ref, *scratch
):
    y, xh = lax.axis_index("y"), lax.axis_index("xh")

    def put_border(loc, kind, low, high):
        dlow_ref[loc, kind, 0] = low
        dhigh_ref[loc, kind, 0] = high

    def slot_work(slot):
        rows = TOK if slot < FULL else HALF
        q_rows = slice(slot * TOK, slot * TOK + rows)

        def put_query(loc, kind, value):
            o_ref[loc, kind, q_rows] = value

        attention_body(
            rows, window_ref[5 * y + (2 * xh + slot if slot < FULL else 4)], lax.axis_index("z") == 0,
            lambda loc, kind: past_ref[loc, kind, 0],
            lambda loc, kind: kv_ref[loc, kind, 0],
            lambda loc, kind: q_ref[loc, kind, q_rows],
            lambda loc, kind, side: (high_ref if side else low_ref)[loc, kind, 0],
            put_query, put_border, put_into(back_ref, 0), put_into(own_ref, 0),
            *scratch,
        )

    for slot in range(SLOTS):
        pl.when(pl.program_id(0) == slot)(functools.partial(slot_work, slot))


SCRATCH = [
    pltpu.VMEM((CAT, DIM), BF16),
    pltpu.VMEM((CAT, DIM), BF16),
    pltpu.VMEM((DIM, CAT), BF16),
    pltpu.VMEM((DIM, CAT), BF16),
    pltpu.VMEM((N_LOC * TOK, DIM), BF16),
    pltpu.VMEM((N_LOC * TOK, DIM), BF16),
    pltpu.VMEM((14 * TOK, LANES), F32),
    pltpu.VMEM((14 * TOK, LANES), F32),
    pltpu.VMEM((CAT + UNIT, N_LOC * TOK), BF16),
    pltpu.VMEM((CAT + UNIT, N_LOC * TOK), BF16),
]
SMEM = pl.BlockSpec(memory_space=pltpu.SMEM)
ANYWHERE = pl.BlockSpec(memory_space=pl.ANY)
KV_SHAPE = (N_LOC, 2, SLOTS, TOK, DIM)
BORDER_SHAPE = (N_LOC, 2, SLOTS, HALO, DIM)
Q_SHAPE = (N_LOC, 2, Q_ROWS, DIM)


def call(kernel, grid, in_specs, args, outs, flops=0, scratch=(), limit=60):
    moved = sum(a.size * a.dtype.itemsize for a in args) + sum(2 * math.prod(shape) for shape, _ in outs)
    return pl.pallas_call(
        kernel,
        grid=(grid,),
        out_shape=[jax.ShapeDtypeStruct(shape, BF16) for shape, _ in outs],
        in_specs=in_specs,
        out_specs=[spec for _, spec in outs],
        scratch_shapes=list(scratch),
        compiler_params=pltpu.CompilerParams(vmem_limit_bytes=limit * 2**20),
        cost_estimate=pl.CostEstimate(flops=flops, bytes_accessed=moved, transcendentals=0),
    )(*args)


def simple(kernel, args, outs, limit=32):
    return call(kernel, 1, [whole(a.shape) for a in args], args, [(o, whole(o)) for o in outs], limit=limit)


def by_slot(rows):
    return pl.BlockSpec((N_LOC, 2, 1, rows, DIM), lambda slot: (0, 0, slot, 0, 0))


def whole(shape):
    return pl.BlockSpec(shape, lambda _: (0,) * len(shape))


def split(shape, parts):
    return pl.BlockSpec((shape[0] // parts, *shape[1:]), lambda i: (i, *[0] * (len(shape) - 1)))


def attend(window, kv, past, low, high, qdo):
    specs = [SMEM, by_slot(TOK), by_slot(TOK), by_slot(HALO), by_slot(HALO), whole(Q_SHAPE)]
    outs = [(Q_SHAPE, whole(Q_SHAPE))] + [(KV_SHAPE, by_slot(TOK))] * 2 + [(BORDER_SHAPE, by_slot(HALO))] * 2
    return call(attention_kernel, SLOTS, specs, (window, kv, past, low, high, qdo), outs, 10**10, SCRATCH, limit=ATTEND_MIB)


def exchange(x):
    return lax.all_to_all(x, PLACES, 0, 0)


def shards(queries, keys, values, cotangent, window):
    up = [(i, i + 1) for i in range(N_Z - 1)]
    down = [(i + 1, i) for i in range(N_Z - 1)]
    (packed_kv,) = simple(pack_keys_kernel, (keys, values), [KV_SHAPE])
    (packed_q,) = simple(pack_queries_kernel, (queries, cotangent), [Q_SHAPE])
    kv = exchange(packed_kv)
    past = lax.ppermute(kv, "z", up)
    low = lax.ppermute(kv[:, :, :, TOK - HALO :], TILES, up)
    high = lax.ppermute(kv[:, :, :, :HALO], TILES, down)
    qdo = exchange(packed_q)
    odq, own, back, dlow, dhigh = attend(window, kv, past, low, high, qdo)
    got = lax.ppermute(back, "z", down)
    from_high = lax.ppermute(dlow, TILES, down)
    from_low = lax.ppermute(dhigh, TILES, up)
    out_q = exchange(odq)
    args = (own, got, from_low, from_high)
    outs = [(KV_SHAPE, split(KV_SHAPE, 4))]
    (merged,) = call(merge_kernel, 4, [split(a.shape, 4) for a in args], args, outs, limit=32)
    out_kv = exchange(merged)
    attended, grad_queries = simple(unpack_queries_kernel, (out_q,), [queries.shape] * 2)
    grad_keys, grad_values = simple(unpack_keys_kernel, (out_kv,), [keys.shape] * 2)
    return attended, grad_queries, grad_keys, grad_values


def solution(mesh):
    fine = Mesh(mesh.devices.reshape(N_Z, N_Y, N_X, 2, 2), AXES)
    rows = P(AXES, None)
    return jax.shard_map(
        shards,
        mesh=fine,
        in_specs=(rows, rows, rows, rows, P()),
        out_specs=(rows, rows, rows, rows),
        check_vma=False,
    )
```

time: 562 us -> 157 us (0.28)
  the two profiles are of different devices: /device:TPU:30 before, /device:TPU:0 now
where the time goes in v2:
time: 157 us
  waiting for transfers between devices  69 us (44%)
  blocking collectives  29.8 us (19%)
  Pallas kernels  29.1 us (19%)
  starting transfers between devices  24.8 us (16%)
  local copies, waits for them, and re-layouts  3.04 us (2%)
    all_to_all x3, waiting for transfers between devices, exchange(): return lax.all_to_all(x, PLACES, 0, 0)  34.5 us
    all_to_all x1, blocking collectives, exchange(): return lax.all_to_all(x, PLACES, 0, 0)  29.8 us
    pallas_call x6, Pallas kernels, call(): pl.pallas_call(kernel, grid=(grid,), out_shape=[jax.ShapeDtypeStruct(shap...  29.1 us
    ppermute x1, waiting for transfers between devices, shards(): got = lax.ppermute(back, 'z', down)  26.3 us
    all_to_all x3, starting transfers between devices, exchange(): return lax.all_to_all(x, PLACES, 0, 0)  10.7 us
    ppermute x1, waiting for transfers between devices, shards(): past = lax.ppermute(kv, 'z', up)  4.99 us
    ppermute x1, starting transfers between devices, shards(): past = lax.ppermute(kv, 'z', up)  4.95 us
    ppermute x1, starting transfers between devices, shards(): low = lax.ppermute(kv[:, :, :, TOK - HALO:], TILES, up)  3.8 us
  transfers between devices with their start and end apart: 9, of which 6 were waited for; matrix products, arithmetic and copies ran while one was open for 1% of the time, Pallas kernels for 4%

profile of v2, /device:TPU:0, one launch (start us, length us, event | category | flops | bytes accessed | tf_op | source)
XLA Modules:
  0.0 156.5 jit_solution(8125876573880220588)
XLA Ops:
  0.6 0.0 copy-start.3
  0.6 1.1 copy-done.3
  1.7 0.0 copy-start.4
  1.7 1.1 copy-done.4
  2.8 0.2 shard_map.84
  3.1 0.0 copy-start.1
  3.1 0.0 copy-start.2
  3.1 29.8 %all_to_all.20.kv_ref = bf16[8,2,3,128,128]{4,3,2,1,0:T(8,128)(2,1)S(1)} all-to-all(bf16[8,2,3,128,128]{4,3,2,1,0:T(8,128)(2,1)S(1)} %shard_map.84), channel_id=1, replica_groups=mesh['z'=4,'y'=4,'xh'=2,'xl'=2,'core'=2] {'y','xh'}, dimensions={0} | all-to-all | bytes 3145728 | tf_op jit(solution)/shard_map/all_to_all | solution.py:328
  32.8 0.0 copy-start.5
  32.8 5.0 %collective-permute-start = (bf16[8,2,3,128,128]{4,3,2,1,0:T(8,128)(2,1)S(1)}, bf16[8,2,3,128,128]{4,3,2,1,0:T(8,128)(2,1)}, u32[]{:S(2)}, u32[]{:S(2)}) collective-permute-start(bf16[8,2,3,128,128]{4,3,2,1,0:T(8,128)(2,1)S(1)} %all_to_all.20.kv_ref), channel_id=1, source_target_pairs={{0,32},{32,64},{64,96},{1,33},{33,65},{65,97},{2,34},{34,66},{66,9... | collective-permute-start | bytes 4718600 | tf_op jit(solution)/shard_map/ppermute | solution.py:337
  37.8 0.0 copy-done.1
  37.8 0.0 copy-done.2
  37.8 1.3 shard_map.85
  39.1 3.6 %all-to-all-start.1 = ((bf16[8,2,320,128]{3,2,1,0:T(8,128)(2,1)}), bf16[8,2,320,128]{3,2,1,0:T(8,128)(2,1)S(1)}, u32[]{:S(2)}, u32[]{:S(2)}) async-start(bf16[8,2,320,128]{3,2,1,0:T(8,128)(2,1)} %shard_map.85), calls=%async_computation.1 | async-start | bytes 2621440 | tf_op jit(solution)/shard_map/all_to_all | solution.py:328
  42.7 0.0 copy-done.5
  42.7 0.8 fusion
  43.5 1.3 collective-permute-start.2
  44.8 3.8 %collective-permute-start.1 = (bf16[8,2,3,32,128]{4,3,2,1,0:T(8,128)(2,1)S(1)}, bf16[8,2,3,32,128]{4,3,2,1,0:T(8,128)(2,1)}, u32[]{:S(2)}, u32[]{:S(2)}) collective-permute-start(bf16[8,2,3,32,128]{4,3,2,1,0:T(8,128)(2,1)S(1)} %get-tuple-element.23), channel_id=1, source_target_pairs={{0,1},{1,2},{2,3},{4,5},{5,6},{6,7},{8,9},{9,10},{10,11},{12,13},{... | collective-permute-start | bytes 1179656 | tf_op jit(solution)/shard_map/ppermute | solution.py:338
  48.6 15.5 %all-to-all-done.1.q_ref = bf16[8,2,320,128]{3,2,1,0:T(8,128)(2,1)S(1)} async-done(((bf16[8,2,320,128]{3,2,1,0:T(8,128)(2,1)}), bf16[8,2,320,128]{3,2,1,0:T(8,128)(2,1)S(1)}, u32[]{:S(2)}, u32[]{:S(2)}) %all-to-all-start.1) | async-done | bytes 1310752 | tf_op jit(solution)/shard_map/all_to_all | solution.py:328
  64.1 0.0 copy-start.6
  64.1 0.0 collective-permute-done.2.high_ref
  64.1 0.0 collective-permute-done.1.low_ref
  64.1 5.0 %collective-permute-done.past_ref = bf16[8,2,3,128,128]{4,3,2,1,0:T(8,128)(2,1)} collective-permute-done((bf16[8,2,3,128,128]{4,3,2,1,0:T(8,128)(2,1)S(1)}, bf16[8,2,3,128,128]{4,3,2,1,0:T(8,128)(2,1)}, u32[]{:S(2)}, u32[]{:S(2)}) %collective-permute-start) | collective-permute-done | bytes 1572896 | tf_op jit(solution)/shard_map/ppermute | solution.py:337
  69.1 0.0 copy-done.6
  69.1 21.3 %shard_map.86 = (bf16[8,2,320,128]{3,2,1,0:T(8,128)(2,1)}, bf16[8,2,3,128,128]{4,3,2,1,0:T(8,128)(2,1)}, bf16[8,2,3,128,128]{4,3,2,1,0:T(8,128)(2,1)}, bf16[8,2,...) custom-call(s32[20]{0:T(128)} %window_ref.1, bf16[8,2,3,128,128]{4,3,2,1,0:T(8,128)(2,1)} %copy-done.5, ...), custom_call_target="tpu_custom_call" | custom-call | flops 10000000000 | bytes 10485840 | tf_op jit(solution)/shard_map/pallas_call | solution.py:293
  90.4 0.0 copy-start.7
  90.4 0.0 copy-start
  90.4 1.4 collective-permute-start.3
  91.8 3.6 %all-to-all-start.2 = ((bf16[8,2,320,128]{3,2,1,0:T(8,128)(2,1)}), bf16[8,2,320,128]{3,2,1,0:T(8,128)(2,1)S(1)}, u32[]{:S(2)}, u32[]{:S(2)}) async-start(bf16[8,2,320,128]{3,2,1,0:T(8,128)(2,1)} %get-tuple-element.13), calls=%async_computation.2 | async-start | bytes 2621440 | tf_op jit(solution)/shard_map/all_to_all | solution.py:328
  95.4 1.3 collective-permute-start.4
  96.7 0.0 copy-done.7
  96.7 1.3 collective-permute-start.5
  98.0 0.2 collective-permute-done.4.from_low_ref
  98.3 3.0 %collective-permute-done.5.from_high_ref = bf16[8,2,3,32,128]{4,3,2,1,0:T(8,128)(2,1)S(1)} collective-permute-done((bf16[8,2,3,32,128]{4,3,2,1,0:T(8,128)(2,1)S(1)}, bf16[8,2,3,32,128]{4,3,2,1,0:T(8,128)(2,1)S(1)}, u32[]{:S(2)}, u32[]{:S(2)}) %collective-permute-start.5) | collective-permute-done | bytes 393248 | tf_op jit(solution)/shard_map/ppermute | solution.py:343
  101.3 26.3 %collective-permute-done.3.got_ref = bf16[8,2,3,128,128]{4,3,2,1,0:T(8,128)(2,1)} collective-permute-done((bf16[8,2,3,128,128]{4,3,2,1,0:T(8,128)(2,1)}, bf16[8,2,3,128,128]{4,3,2,1,0:T(8,128)(2,1)}, u32[]{:S(2)}, u32[]{:S(2)}) %collective-permute-start.3) | collective-permute-done | bytes 1572896 | tf_op jit(solution)/shard_map/ppermute | solution.py:342
  127.6 0.0 copy-done
  127.6 3.8 %shard_map.88 = bf16[8,2,3,128,128]{4,3,2,1,0:T(8,128)(2,1)} custom-call(bf16[8,2,3,128,128]{4,3,2,1,0:T(8,128)(2,1)S(1)} %copy-done, bf16[8,2,3,128,128]{4,3,2,1,0:T(8,128)(2,1)} %collective-permute-done.3.got_ref, bf16[8,2,3,32,128]{4,3,2,1,0:T(8,128)(2,1)S(1)} %collective-permute-done.4.from_low_ref, ...), custom_call_target="tpu_custom_call" | custom-call | bytes 5505024 | tf_op jit(solution)/shard_map/pallas_call | solution.py:293
  131.4 0.0 all-to-all-done.2.odq_ref
  131.4 3.6 %all-to-all-start.3 = ((bf16[8,2,3,128,128]{4,3,2,1,0:T(8,128)(2,1)}), bf16[8,2,3,128,128]{4,3,2,1,0:T(8,128)(2,1)S(1)}, u32[]{:S(2)}, u32[]{:S(2)}) async-start(bf16[8,2,3,128,128]{4,3,2,1,0:T(8,128)(2,1)} %shard_map.88), calls=%async_computation.3 | async-start | bytes 3145728 | tf_op jit(solution)/shard_map/all_to_all | solution.py:328
  135.0 1.3 shard_map.87
  136.3 19.0 %all-to-all-done.3.grads_ref = bf16[8,2,3,128,128]{4,3,2,1,0:T(8,128)(2,1)S(1)} async-done(((bf16[8,2,3,128,128]{4,3,2,1,0:T(8,128)(2,1)}), bf16[8,2,3,128,128]{4,3,2,1,0:T(8,128)(2,1)S(1)}, u32[]{:S(2)}, u32[]{:S(2)}) %all-to-all-start.3) | async-done | bytes 1572896 | tf_op jit(solution)/shard_map/all_to_all | solution.py:328
  155.3 1.3 shard_map.89
Async XLA Ops:
  0.6 1.1 copy-start.3
  1.7 1.1 copy-start.4
  3.1 34.7 %copy-start.1 = (bf16[128,2560]{1,0:T(8,128)(2,1)S(1)}, bf16[128,2560]{1,0:T(8,128)(2,1)}, u32[]{:S(2)}) copy-start(bf16[128,2560]{1,0:T(8,128)(2,1)} %q_ref.1) | copy-start | bytes 1966084
  3.1 34.7 %copy-start.2 = (bf16[128,2560]{1,0:T(8,128)(2,1)S(1)}, bf16[128,2560]{1,0:T(8,128)(2,1)}, u32[]{:S(2)}) copy-start(bf16[128,2560]{1,0:T(8,128)(2,1)} %do_ref.1) | copy-start | bytes 1966084
  32.8 9.8 %copy-start.5 = (bf16[8,2,3,128,128]{4,3,2,1,0:T(8,128)(2,1)}, bf16[8,2,3,128,128]{4,3,2,1,0:T(8,128)(2,1)S(1)}, u32[]{:S(2)}) copy-start(bf16[8,2,3,128,128]{4,3,2,1,0:T(8,128)(2,1)S(1)} %all_to_all.20.kv_ref) | copy-start | bytes 4718596
  32.8 36.3 %collective-permute-start = (bf16[8,2,3,128,128]{4,3,2,1,0:T(8,128)(2,1)S(1)}, bf16[8,2,3,128,128]{4,3,2,1,0:T(8,128)(2,1)}, u32[]{:S(2)}, u32[]{:S(2)}) collective-permute-start(bf16[8,2,3,128,128]{4,3,2,1,0:T(8,128)(2,1)S(1)} %all_to_all.20.kv_ref), channel_id=1, source_target_pairs={{0,32},{32,64},{64,96},{1,33},{33,65},{65,97},{2,34},{34,66},{66,9... | collective-permute-start | bytes 4718600 | tf_op jit(solution)/shard_map/ppermute | solution.py:337
  39.1 25.0 %all-to-all-start.1 = ((bf16[8,2,320,128]{3,2,1,0:T(8,128)(2,1)}), bf16[8,2,320,128]{3,2,1,0:T(8,128)(2,1)S(1)}, u32[]{:S(2)}, u32[]{:S(2)}) async-start(bf16[8,2,320,128]{3,2,1,0:T(8,128)(2,1)} %shard_map.85), calls=%async_computation.1 | async-start | bytes 2621440 | tf_op jit(solution)/shard_map/all_to_all | solution.py:328
  43.5 20.6 %collective-permute-start.2 = (bf16[8,2,3,32,128]{4,3,2,1,0:T(8,128)(2,1)}, bf16[8,2,3,32,128]{4,3,2,1,0:T(8,128)(2,1)}, u32[]{:S(2)}, u32[]{:S(2)}) collective-permute-start(bf16[8,2,3,32,128]{4,3,2,1,0:T(8,128)(2,1)} %get-tuple-element.22), channel_id=1, source_target_pairs={{1,0},{2,1},{3,2},{5,4},{6,5},{7,6},{9,8},{10,9},{11,10},{13,12},{... | collective-permute-start | bytes 1179656 | tf_op jit(solution)/shard_map/ppermute | solution.py:339
  44.8 19.3 %collective-permute-start.1 = (bf16[8,2,3,32,128]{4,3,2,1,0:T(8,128)(2,1)S(1)}, bf16[8,2,3,32,128]{4,3,2,1,0:T(8,128)(2,1)}, u32[]{:S(2)}, u32[]{:S(2)}) collective-permute-start(bf16[8,2,3,32,128]{4,3,2,1,0:T(8,128)(2,1)S(1)} %get-tuple-element.23), channel_id=1, source_target_pairs={{0,1},{1,2},{2,3},{4,5},{5,6},{6,7},{8,9},{9,10},{10,11},{12,13},{... | collective-permute-start | bytes 1179656 | tf_op jit(solution)/shard_map/ppermute | solution.py:338
  64.1 5.0 %copy-start.6 = (bf16[8,2,320,128]{3,2,1,0:T(8,128)(2,1)}, bf16[8,2,320,128]{3,2,1,0:T(8,128)(2,1)S(1)}, u32[]{:S(2)}) copy-start(bf16[8,2,320,128]{3,2,1,0:T(8,128)(2,1)S(1)} %all-to-all-done.1.q_ref) | copy-start | bytes 3932164
  90.4 6.4 %copy-start.7 = (bf16[8,2,3,32,128]{4,3,2,1,0:T(8,128)(2,1)S(1)}, bf16[8,2,3,32,128]{4,3,2,1,0:T(8,128)(2,1)}, u32[]{:S(2)}) copy-start(bf16[8,2,3,32,128]{4,3,2,1,0:T(8,128)(2,1)} %get-tuple-element.19) | copy-start | bytes 1179652
  90.4 37.2 %copy-start = (bf16[8,2,3,128,128]{4,3,2,1,0:T(8,128)(2,1)S(1)}, bf16[8,2,3,128,128]{4,3,2,1,0:T(8,128)(2,1)}, u32[]{:S(2)}) copy-start(bf16[8,2,3,128,128]{4,3,2,1,0:T(8,128)(2,1)} %get-tuple-element.16.own_ref) | copy-start | bytes 4718596
  90.4 37.2 %collective-permute-start.3 = (bf16[8,2,3,128,128]{4,3,2,1,0:T(8,128)(2,1)}, bf16[8,2,3,128,128]{4,3,2,1,0:T(8,128)(2,1)}, u32[]{:S(2)}, u32[]{:S(2)}) collective-permute-start(bf16[8,2,3,128,128]{4,3,2,1,0:T(8,128)(2,1)} %get-tuple-element.17), channel_id=1, source_target_pairs={{32,0},{64,32},{96,64},{33,1},{65,33},{97,65},{34,2},{66,34},{98,6... | collective-permute-start | bytes 4718600 | tf_op jit(solution)/shard_map/ppermute | solution.py:342
  91.8 39.6 %all-to-all-start.2 = ((bf16[8,2,320,128]{3,2,1,0:T(8,128)(2,1)}), bf16[8,2,320,128]{3,2,1,0:T(8,128)(2,1)S(1)}, u32[]{:S(2)}, u32[]{:S(2)}) async-start(bf16[8,2,320,128]{3,2,1,0:T(8,128)(2,1)} %get-tuple-element.13), calls=%async_computation.2 | async-start | bytes 2621440 | tf_op jit(solution)/shard_map/all_to_all | solution.py:328
  95.4 2.8 %collective-permute-start.4 = (bf16[8,2,3,32,128]{4,3,2,1,0:T(8,128)(2,1)}, bf16[8,2,3,32,128]{4,3,2,1,0:T(8,128)(2,1)S(1)}, u32[]{:S(2)}, u32[]{:S(2)}) collective-permute-start(bf16[8,2,3,32,128]{4,3,2,1,0:T(8,128)(2,1)} %get-tuple-element.18), channel_id=1, source_target_pairs={{0,1},{1,2},{2,3},{4,5},{5,6},{6,7},{8,9},{9,10},{10,11},{12,13},{... | collective-permute-start | bytes 1179656 | tf_op jit(solution)/shard_map/ppermute | solution.py:344
  96.7 4.5 %collective-permute-start.5 = (bf16[8,2,3,32,128]{4,3,2,1,0:T(8,128)(2,1)S(1)}, bf16[8,2,3,32,128]{4,3,2,1,0:T(8,128)(2,1)S(1)}, u32[]{:S(2)}, u32[]{:S(2)}) collective-permute-start(bf16[8,2,3,32,128]{4,3,2,1,0:T(8,128)(2,1)S(1)} %copy-done.7), channel_id=1, source_target_pairs={{1,0},{2,1},{3,2},{5,4},{6,5},{7,6},{9,8},{10,9},{11,10},{13,12},{... | collective-permute-start | bytes 1179656 | tf_op jit(solution)/shard_map/ppermute | solution.py:343
  131.4 23.9 %all-to-all-start.3 = ((bf16[8,2,3,128,128]{4,3,2,1,0:T(8,128)(2,1)}), bf16[8,2,3,128,128]{4,3,2,1,0:T(8,128)(2,1)S(1)}, u32[]{:S(2)}, u32[]{:S(2)}) async-start(bf16[8,2,3,128,128]{4,3,2,1,0:T(8,128)(2,1)} %shard_map.88), calls=%async_computation.3 | async-start | bytes 3145728 | tf_op jit(solution)/shard_map/all_to_all | solution.py:328

commit v3 on v2

--- a/solution.py
+++ b/solution.py
@@ -18,6 +18,7 @@
 SLOTS = 3
 HALF = TOK // 2
 Q_ROWS = FULL * TOK + HALF
+ALL_ROWS = Q_ROWS + TOK
 LOW = -1.0e30
 FACTOR = DIM ** -0.5
 LOG2E = 1.4426950408889634
@@ -34,38 +35,47 @@
     return slice(head * DIM, (head + 1) * DIM)
 
 
-def pack_keys_kernel(k_ref, v_ref, kv_ref):
+def pack_keys_kernel(k_ref, v_ref, kv_ref, raw_ref):
+    for y in range(N_Y):
+        raw_ref[y, 0] = k_ref[:, head_cols(y * N_X, FULL)]
+        raw_ref[y, 1] = v_ref[:, head_cols(y * N_X, FULL)]
     for place in range(N_LOC):
         for kind, ref in enumerate((k_ref, v_ref)):
             for slot in range(SLOTS):
                 kv_ref[place, kind, slot] = ref[:, head_cols(place, slot)]
 
 
-def pack_queries_kernel(q_ref, do_ref, qdo_ref):
+def pack_queries_kernel(q_ref, do_ref, raw_ref, qdo_ref):
     for place in range(N_LOC):
         start = place % N_X * HALF
         for kind, ref in enumerate((q_ref, do_ref)):
             for slot in range(FULL):
                 qdo_ref[place, kind, slot * TOK : (slot + 1) * TOK] = ref[:, head_cols(place, slot)]
-            qdo_ref[place, kind, FULL * TOK :] = ref[start : start + HALF, head_cols(place, FULL)]
-
-
-def unpack_queries_kernel(odq_ref, o_ref, dq_ref):
+            qdo_ref[place, kind, FULL * TOK : Q_ROWS] = ref[start : start + HALF, head_cols(place, FULL)]
+            qdo_ref[place, kind, Q_ROWS:] = raw_ref[place // N_X, kind]
+
+
+def unpack_queries_kernel(odq_ref, o_ref, dq_ref, raw_ref):
     for place in range(N_LOC):
         start = place % N_X * HALF
         for kind, ref in enumerate((o_ref, dq_ref)):
             for slot in range(FULL):
                 ref[:, head_cols(place, slot)] = odq_ref[place, kind, slot * TOK : (slot + 1) * TOK]
-            ref[start : start + HALF, head_cols(place, FULL)] = odq_ref[place, kind, FULL * TOK :]
-
-
-def unpack_keys_kernel(grads_ref, dk_ref, dv_ref):
+            ref[start : start + HALF, head_cols(place, FULL)] = odq_ref[place, kind, FULL * TOK : Q_ROWS]
+    for kind in range(2):
+        for y in range(N_Y):
+            first, second = odq_ref[y * N_X, kind, Q_ROWS:], odq_ref[y * N_X + 1, kind, Q_ROWS:]
+            raw_ref[y, kind] = (first.astype(F32) + second.astype(F32)).astype(BF16)
+
+
+def unpack_keys_kernel(grads_ref, raw_ref, dk_ref, dv_ref):
     for kind, ref in enumerate((dk_ref, dv_ref)):
         for place in range(N_LOC):
             for slot in range(FULL):
                 ref[:, head_cols(place, slot)] = grads_ref[place, kind, slot]
         for place in range(0, N_LOC, N_X):
             both = grads_ref[place, kind, FULL].astype(F32) + grads_ref[place + 1, kind, FULL].astype(F32)
+            both = both + raw_ref[place // N_X, kind].astype(F32)
             ref[:, head_cols(place, FULL)] = both.astype(BF16)
 
 
@@ -74,7 +84,9 @@
         for kind in range(2):
             for slot in range(SLOTS):
                 at = (loc, kind, slot)
-                total = own_ref[at].astype(F32) + got_ref[at].astype(F32)
+                total = own_ref[at].astype(F32)
+                if slot < FULL:
+                    total = total + got_ref[at].astype(F32)
                 first = total[:HALO] + from_low_ref[at].astype(F32)
                 last = total[TOK - HALO :] + from_high_ref[at].astype(F32)
                 out_ref[loc, kind, slot, :HALO] = first.astype(BF16)
@@ -255,13 +267,16 @@
         def put_query(loc, kind, value):
             o_ref[loc, kind, q_rows] = value
 
+        def put_past(loc, kind, value):
+            o_ref[loc, kind, Q_ROWS:] = value
+
         attention_body(
             rows, window_ref[5 * y + (2 * xh + slot if slot < FULL else 4)], lax.axis_index("z") == 0,
-            lambda loc, kind: past_ref[loc, kind, 0],
+            (lambda loc, kind: past_ref[loc, kind, 0]) if slot < FULL else (lambda loc, kind: q_ref[loc, kind, Q_ROWS:]),
             lambda loc, kind: kv_ref[loc, kind, 0],
             lambda loc, kind: q_ref[loc, kind, q_rows],
             lambda loc, kind, side: (high_ref if side else low_ref)[loc, kind, 0],
-            put_query, put_border, put_into(back_ref, 0), put_into(own_ref, 0),
+            put_query, put_border, put_into(back_ref, 0) if slot < FULL else put_past, put_into(own_ref, 0),
             *scratch,
         )
 
@@ -285,7 +300,9 @@
 ANYWHERE = pl.BlockSpec(memory_space=pl.ANY)
 KV_SHAPE = (N_LOC, 2, SLOTS, TOK, DIM)
 BORDER_SHAPE = (N_LOC, 2, SLOTS, HALO, DIM)
-Q_SHAPE = (N_LOC, 2, Q_ROWS, DIM)
+Q_SHAPE = (N_LOC, 2, ALL_ROWS, DIM)
+PAIR_SHAPE = (N_LOC, 2, FULL, TOK, DIM)
+RAW_SHAPE = (N_Y, 2, TOK, DIM)
 
 
 def call(kernel, grid, in_specs, args, outs, flops=0, scratch=(), limit=60):
@@ -310,6 +327,10 @@
     return pl.BlockSpec((N_LOC, 2, 1, rows, DIM), lambda slot: (0, 0, slot, 0, 0))
 
 
+def by_full_slot():
+    return pl.BlockSpec((N_LOC, 2, 1, TOK, DIM), lambda slot: (0, 0, jnp.minimum(slot, FULL - 1), 0, 0))
+
+
 def whole(shape):
     return pl.BlockSpec(shape, lambda _: (0,) * len(shape))
 
@@ -319,8 +340,8 @@
 
 
 def attend(window, kv, past, low, high, qdo):
-    specs = [SMEM, by_slot(TOK), by_slot(TOK), by_slot(HALO), by_slot(HALO), whole(Q_SHAPE)]
-    outs = [(Q_SHAPE, whole(Q_SHAPE))] + [(KV_SHAPE, by_slot(TOK))] * 2 + [(BORDER_SHAPE, by_slot(HALO))] * 2
+    specs = [SMEM, by_slot(TOK), by_full_slot(), by_slot(HALO), by_slot(HALO), whole(Q_SHAPE)]
+    outs = [(Q_SHAPE, whole(Q_SHAPE)), (KV_SHAPE, by_slot(TOK)), (PAIR_SHAPE, by_full_slot())] + [(BORDER_SHAPE, by_slot(HALO))] * 2
     return call(attention_kernel, SLOTS, specs, (window, kv, past, low, high, qdo), outs, 10**10, SCRATCH, limit=ATTEND_MIB)
 
 
@@ -331,10 +352,11 @@
 def shards(queries, keys, values, cotangent, window):
     up = [(i, i + 1) for i in range(N_Z - 1)]
     down = [(i + 1, i) for i in range(N_Z - 1)]
-    (packed_kv,) = simple(pack_keys_kernel, (keys, values), [KV_SHAPE])
-    (packed_q,) = simple(pack_queries_kernel, (queries, cotangent), [Q_SHAPE])
+    packed_kv, raw = simple(pack_keys_kernel, (keys, values), [KV_SHAPE, RAW_SHAPE])
+    raw = lax.ppermute(raw, "z", up)
+    (packed_q,) = simple(pack_queries_kernel, (queries, cotangent, raw), [Q_SHAPE])
     kv = exchange(packed_kv)
-    past = lax.ppermute(kv, "z", up)
+    past = lax.ppermute(kv[:, :, :FULL], "z", up)
     low = lax.ppermute(kv[:, :, :, TOK - HALO :], TILES, up)
     high = lax.ppermute(kv[:, :, :, :HALO], TILES, down)
     qdo = exchange(packed_q)
@@ -347,8 +369,9 @@
     outs = [(KV_SHAPE, split(KV_SHAPE, 4))]
     (merged,) = call(merge_kernel, 4, [split(a.shape, 4) for a in args], args, outs, limit=32)
     out_kv = exchange(merged)
-    attended, grad_queries = simple(unpack_queries_kernel, (out_q,), [queries.shape] * 2)
-    grad_keys, grad_values = simple(unpack_keys_kernel, (out_kv,), [keys.shape] * 2)
+    attended, grad_queries, raw = simple(unpack_queries_kernel, (out_q,), [queries.shape, queries.shape, RAW_SHAPE])
+    raw = lax.ppermute(raw, "z", down)
+    grad_keys, grad_values = simple(unpack_keys_kernel, (out_kv, raw), [keys.shape] * 2)
     return attended, grad_queries, grad_keys, grad_values
 
 

time: 157 us -> 153 us (0.975)
  blocking collectives: 29.8 us -> 0 us
  starting transfers between devices: 24.8 us -> 42.1 us
  waiting for transfers between devices: 69 us -> 77.7 us
    all_to_all x1 -> x0, blocking collectives: 29.8 us -> none  [exchange(): return lax.all_to_all(x, PLACES, 0, 0)]
    all_to_all x3 -> x4, starting transfers between devices: 10.7 us -> 23.3 us  [exchange(): return lax.all_to_all(x, PLACES, 0, 0)]
    ppermute x1 -> x3, waiting for transfers between devices: 4.99 us -> 12.7 us  [the longest x1 7.48 us: shards(): raw = lax.ppermute(raw, 'z', down)]
    all_to_all x3 -> x4, waiting for transfers between devices: 34.5 us -> 40.5 us  [exchange(): return lax.all_to_all(x, PLACES, 0, 0)]
    ppermute x1, waiting for transfers between devices: 26.3 us -> 20.5 us  [shards(): got = lax.ppermute(back, 'z', down)]
    ppermute x1 -> x3, starting transfers between devices: 4.95 us -> 9.92 us  [the longest x1 4.81 us: shards(): past = lax.ppermute(kv[:, :, :FULL], 'z', up)]
  transfers between devices with their start and end apart: 9 -> 12, of which waited for: 6 -> 9; matrix products, arithmetic and copies ran while one was open for 1% -> 0% of each run, Pallas kernels for 4% -> 3%
where the time goes in v3:
time: 153 us; the launch traced here: 152 us
  waiting for transfers between devices  77.7 us (51%)
  starting transfers between devices  42.1 us (28%)
  Pallas kernels  29.2 us (19%)
  local copies, waits for them, and re-layouts  2.38 us (2%)
    all_to_all x4, waiting for transfers between devices, exchange(): return lax.all_to_all(x, PLACES, 0, 0)  40.5 us
    pallas_call x6, Pallas kernels, call(): pl.pallas_call(kernel, grid=(grid,), out_shape=[jax.ShapeDtypeStruct(shap...  29.2 us
    all_to_all x4, starting transfers between devices, exchange(): return lax.all_to_all(x, PLACES, 0, 0)  23.3 us
    ppermute x1, waiting for transfers between devices, shards(): got = lax.ppermute(back, 'z', down)  20.5 us
    ppermute x1, waiting for transfers between devices, shards(): raw = lax.ppermute(raw, 'z', down)  7.48 us
    ppermute x1, waiting for transfers between devices, shards(): raw = lax.ppermute(raw, 'z', up)  5.25 us
    ppermute x1, starting transfers between devices, shards(): past = lax.ppermute(kv[:, :, :FULL], 'z', up)  4.81 us
    ppermute x1, starting transfers between devices, shards(): raw = lax.ppermute(raw, 'z', up)  3.83 us
  transfers between devices with their start and end apart: 12, of which 9 were waited for; matrix products, arithmetic and copies ran while one was open for 0% of the time, Pallas kernels for 3%

profile of v3, /device:TPU:0, one launch (start us, length us, event | category | flops | bytes accessed | tf_op | source)
XLA Modules:
  0.0 152.2 jit_solution(3207280796945474272)
XLA Ops:
  0.6 0.0 copy-start.1
  0.6 1.1 copy-done.1
  1.7 0.0 copy-start.2
  1.7 1.1 copy-done.2
  2.8 1.5 shard_map.84
  4.3 0.0 copy-start.3
  4.3 0.0 copy-start.4
  4.3 7.1 %all-to-all-start = ((bf16[8,2,3,128,128]{4,3,2,1,0:T(8,128)(2,1)}), bf16[8,2,3,128,128]{4,3,2,1,0:T(8,128)(2,1)S(1)}, u32[]{:S(2)}, u32[]{:S(2)}) async-start(bf16[8,2,3,128,128]{4,3,2,1,0:T(8,128)(2,1)} %get-tuple-element.16), calls=%async_computation | async-start | bytes 3145728 | tf_op jit(solution)/shard_map/all_to_all | solution.py:349
  11.4 3.8 %collective-permute-start.3 = (bf16[4,2,128,128]{3,2,1,0:T(8,128)(2,1)S(1)}, bf16[4,2,128,128]{3,2,1,0:T(8,128)(2,1)S(1)}, u32[]{:S(2)}, u32[]{:S(2)}) collective-permute-start(bf16[4,2,128,128]{3,2,1,0:T(8,128)(2,1)S(1)} %get-tuple-element.17), channel_id=1, source_target_pairs={{0,32},{32,64},{64,96},{1,33},{33,65},{65,97},{2,34},{34,66},{66,9... | collective-permute-start | bytes 786440 | tf_op jit(solution)/shard_map/ppermute | solution.py:356
  15.3 5.3 %collective-permute-done.3.raw_ref = bf16[4,2,128,128]{3,2,1,0:T(8,128)(2,1)S(1)} collective-permute-done((bf16[4,2,128,128]{3,2,1,0:T(8,128)(2,1)S(1)}, bf16[4,2,128,128]{3,2,1,0:T(8,128)(2,1)S(1)}, u32[]{:S(2)}, u32[]{:S(2)}) %collective-permute-start.3) | collective-permute-done | bytes 262176 | tf_op jit(solution)/shard_map/ppermute | solution.py:356
  20.5 0.0 copy-done.3
  20.5 0.0 copy-done.4
  20.5 1.5 shard_map.85
  22.0 12.3 %all-to-all-done.kv_ref = bf16[8,2,3,128,128]{4,3,2,1,0:T(8,128)(2,1)S(1)} async-done(((bf16[8,2,3,128,128]{4,3,2,1,0:T(8,128)(2,1)}), bf16[8,2,3,128,128]{4,3,2,1,0:T(8,128)(2,1)S(1)}, u32[]{:S(2)}, u32[]{:S(2)}) %all-to-all-start) | async-done | bytes 1572896 | tf_op jit(solution)/shard_map/all_to_all | solution.py:349
  34.3 0.0 copy-start.5
  34.3 4.3 %all-to-all-start.1 = ((bf16[8,2,448,128]{3,2,1,0:T(8,128)(2,1)}), bf16[8,2,448,128]{3,2,1,0:T(8,128)(2,1)}, u32[]{:S(2)}, u32[]{:S(2)}) async-start(bf16[8,2,448,128]{3,2,1,0:T(8,128)(2,1)} %shard_map.85), calls=%async_computation.1 | async-start | bytes 3670016 | tf_op jit(solution)/shard_map/all_to_all | solution.py:349
  38.6 0.1 slice.12
  38.7 4.8 %collective-permute-start = (bf16[8,2,2,128,128]{4,3,2,1,0:T(8,128)(2,1)S(1)}, bf16[8,2,2,128,128]{4,3,2,1,0:T(8,128)(2,1)}, u32[]{:S(2)}, u32[]{:S(2)}) collective-permute-start(bf16[8,2,2,128,128]{4,3,2,1,0:T(8,128)(2,1)S(1)} %slice.12), channel_id=1, source_target_pairs={{0,32},{32,64},{64,96},{1,33},{33,65},{65,97},{2,34},{34,66},{66,9... | collective-permute-start | bytes 3145736 | tf_op jit(solution)/shard_map/ppermute | solution.py:359
  43.5 0.0 copy-done.5
  43.5 0.1 fusion
  43.6 1.3 collective-permute-start.2
  44.9 3.1 %collective-permute-start.1 = (bf16[8,2,3,32,128]{4,3,2,1,0:T(8,128)(2,1)S(1)}, bf16[8,2,3,32,128]{4,3,2,1,0:T(8,128)(2,1)S(1)}, u32[]{:S(2)}, u32[]{:S(2)}) collective-permute-start(bf16[8,2,3,32,128]{4,3,2,1,0:T(8,128)(2,1)S(1)} %get-tuple-element.29), channel_id=1, source_target_pairs={{0,1},{1,2},{2,3},{4,5},{5,6},{6,7},{8,9},{9,10},{10,11},{12,13},{... | collective-permute-start | bytes 1179656 | tf_op jit(solution)/shard_map/ppermute | solution.py:360
  48.0 0.0 collective-permute-done.2.high_ref
  48.0 0.0 copy-start.6
  48.0 1.3 collective-permute-done.1.low_ref
  49.3 0.0 copy-start.7
  49.3 16.4 %all-to-all-done.1.q_ref = bf16[8,2,448,128]{3,2,1,0:T(8,128)(2,1)} async-done(((bf16[8,2,448,128]{3,2,1,0:T(8,128)(2,1)}), bf16[8,2,448,128]{3,2,1,0:T(8,128)(2,1)}, u32[]{:S(2)}, u32[]{:S(2)}) %all-to-all-start.1) | async-done | bytes 1835040 | tf_op jit(solution)/shard_map/all_to_all | solution.py:349
  65.7 0.0 collective-permute-done.past_ref
  65.7 0.0 copy-done.6
  65.7 0.0 copy-done.7
  65.8 21.8 %shard_map.86 = (bf16[8,2,448,128]{3,2,1,0:T(8,128)(2,1)}, bf16[8,2,3,128,128]{4,3,2,1,0:T(8,128)(2,1)}, bf16[8,2,2,128,128]{4,3,2,1,0:T(8,128)(2,1)}, bf16[8,2,...) custom-call(s32[20]{0:T(128)} %window_ref.1, bf16[8,2,3,128,128]{4,3,2,1,0:T(8,128)(2,1)} %copy-done.5, ...), custom_call_target="tpu_custom_call" | custom-call | flops 10000000000 | bytes 10485840 | tf_op jit(solution)/shard_map/pallas_call | solution.py:310
  87.5 0.0 copy-start
  87.5 4.9 %all-to-all-start.2 = ((bf16[8,2,448,128]{3,2,1,0:T(8,128)(2,1)}), bf16[8,2,448,128]{3,2,1,0:T(8,128)(2,1)S(1)}, u32[]{:S(2)}, u32[]{:S(2)}) async-start(bf16[8,2,448,128]{3,2,1,0:T(8,128)(2,1)} %get-tuple-element.18), calls=%async_computation.2 | async-start | bytes 3670016 | tf_op jit(solution)/shard_map/all_to_all | solution.py:349
  92.5 1.3 collective-permute-start.4
  93.7 2.0 %collective-permute-start.5 = (bf16[8,2,3,32,128]{4,3,2,1,0:T(8,128)(2,1)}, bf16[8,2,3,32,128]{4,3,2,1,0:T(8,128)(2,1)S(1)}, u32[]{:S(2)}, u32[]{:S(2)}) collective-permute-start(bf16[8,2,3,32,128]{4,3,2,1,0:T(8,128)(2,1)} %get-tuple-element.23), channel_id=1, source_target_pairs={{0,1},{1,2},{2,3},{4,5},{5,6},{6,7},{8,9},{9,10},{10,11},{12,13},{... | collective-permute-start | bytes 1179656 | tf_op jit(solution)/shard_map/ppermute | solution.py:366
  95.7 1.3 collective-permute-start.6
  97.0 0.2 collective-permute-done.5.from_low_ref
  97.2 2.5 %collective-permute-done.6.from_high_ref = bf16[8,2,3,32,128]{4,3,2,1,0:T(8,128)(2,1)S(1)} collective-permute-done((bf16[8,2,3,32,128]{4,3,2,1,0:T(8,128)(2,1)}, bf16[8,2,3,32,128]{4,3,2,1,0:T(8,128)(2,1)S(1)}, u32[]{:S(2)}, u32[]{:S(2)}) %collective-permute-start.6) | collective-permute-done | bytes 393248 | tf_op jit(solution)/shard_map/ppermute | solution.py:365
  99.7 20.5 %collective-permute-done.4.got_ref = bf16[8,2,2,128,128]{4,3,2,1,0:T(8,128)(2,1)S(1)} collective-permute-done((bf16[8,2,2,128,128]{4,3,2,1,0:T(8,128)(2,1)}, bf16[8,2,2,128,128]{4,3,2,1,0:T(8,128)(2,1)S(1)}, u32[]{:S(2)}, u32[]{:S(2)}) %collective-permute-start.4) | collective-permute-done | bytes 1048608 | tf_op jit(solution)/shard_map/ppermute | solution.py:364
  120.2 0.0 copy-done
  120.2 1.9 %shard_map.88 = bf16[8,2,3,128,128]{4,3,2,1,0:T(8,128)(2,1)} custom-call(bf16[8,2,3,128,128]{4,3,2,1,0:T(8,128)(2,1)S(1)} %copy-done, bf16[8,2,2,128,128]{4,3,2,1,0:T(8,128)(2,1)S(1)} %collective-permute-done.4.got_ref, bf16[8,2,3,32,128]{4,3,2,1,0:T(8,128)(2,1)S(1)} %collective-permute-done.5.from_low_ref, ...), custom_call_target="tpu_custom_call" | custom-call | bytes 4980736 | tf_op jit(solution)/shard_map/pallas_call | solution.py:310
  122.1 0.0 all-to-all-done.2.odq_ref
  122.1 6.9 %all-to-all-start.3 = ((bf16[8,2,3,128,128]{4,3,2,1,0:T(8,128)(2,1)}), bf16[8,2,3,128,128]{4,3,2,1,0:T(8,128)(2,1)S(1)}, u32[]{:S(2)}, u32[]{:S(2)}) async-start(bf16[8,2,3,128,128]{4,3,2,1,0:T(8,128)(2,1)} %shard_map.88), calls=%async_computation.3 | async-start | bytes 3145728 | tf_op jit(solution)/shard_map/all_to_all | solution.py:349
  129.0 1.3 shard_map.87
  130.3 1.3 collective-permute-start.7
  131.6 7.5 %collective-permute-done.7.raw_ref = bf16[4,2,128,128]{3,2,1,0:T(8,128)(2,1)S(1)} collective-permute-done((bf16[4,2,128,128]{3,2,1,0:T(8,128)(2,1)S(1)}, bf16[4,2,128,128]{3,2,1,0:T(8,128)(2,1)S(1)}, u32[]{:S(2)}, u32[]{:S(2)}) %collective-permute-start.7) | collective-permute-done | bytes 262176 | tf_op jit(solution)/shard_map/ppermute | solution.py:373
  139.1 11.8 %all-to-all-done.3.grads_ref = bf16[8,2,3,128,128]{4,3,2,1,0:T(8,128)(2,1)S(1)} async-done(((bf16[8,2,3,128,128]{4,3,2,1,0:T(8,128)(2,1)}), bf16[8,2,3,128,128]{4,3,2,1,0:T(8,128)(2,1)S(1)}, u32[]{:S(2)}, u32[]{:S(2)}) %all-to-all-start.3) | async-done | bytes 1572896 | tf_op jit(solution)/shard_map/all_to_all | solution.py:349
  150.9 1.3 shard_map.89
Async XLA Ops:
  0.6 1.1 copy-start.1
  1.7 1.1 copy-start.2
  4.3 16.2 %copy-start.3 = (bf16[128,2560]{1,0:T(8,128)(2,1)S(1)}, bf16[128,2560]{1,0:T(8,128)(2,1)}, u32[]{:S(2)}) copy-start(bf16[128,2560]{1,0:T(8,128)(2,1)} %q_ref.1) | copy-start | bytes 1966084
  4.3 16.2 %copy-start.4 = (bf16[128,2560]{1,0:T(8,128)(2,1)S(1)}, bf16[128,2560]{1,0:T(8,128)(2,1)}, u32[]{:S(2)}) copy-start(bf16[128,2560]{1,0:T(8,128)(2,1)} %do_ref.1) | copy-start | bytes 1966084
  4.3 30.0 %all-to-all-start = ((bf16[8,2,3,128,128]{4,3,2,1,0:T(8,128)(2,1)}), bf16[8,2,3,128,128]{4,3,2,1,0:T(8,128)(2,1)S(1)}, u32[]{:S(2)}, u32[]{:S(2)}) async-start(bf16[8,2,3,128,128]{4,3,2,1,0:T(8,128)(2,1)} %get-tuple-element.16), calls=%async_computation | async-start | bytes 3145728 | tf_op jit(solution)/shard_map/all_to_all | solution.py:349
  11.4 9.1 %collective-permute-start.3 = (bf16[4,2,128,128]{3,2,1,0:T(8,128)(2,1)S(1)}, bf16[4,2,128,128]{3,2,1,0:T(8,128)(2,1)S(1)}, u32[]{:S(2)}, u32[]{:S(2)}) collective-permute-start(bf16[4,2,128,128]{3,2,1,0:T(8,128)(2,1)S(1)} %get-tuple-element.17), channel_id=1, source_target_pairs={{0,32},{32,64},{64,96},{1,33},{33,65},{65,97},{2,34},{34,66},{66,9... | collective-permute-start | bytes 786440 | tf_op jit(solution)/shard_map/ppermute | solution.py:356
  34.3 9.3 %copy-start.5 = (bf16[8,2,3,128,128]{4,3,2,1,0:T(8,128)(2,1)}, bf16[8,2,3,128,128]{4,3,2,1,0:T(8,128)(2,1)S(1)}, u32[]{:S(2)}) copy-start(bf16[8,2,3,128,128]{4,3,2,1,0:T(8,128)(2,1)S(1)} %all-to-all-done.kv_ref) | copy-start | bytes 4718596
  34.3 31.5 %all-to-all-start.1 = ((bf16[8,2,448,128]{3,2,1,0:T(8,128)(2,1)}), bf16[8,2,448,128]{3,2,1,0:T(8,128)(2,1)}, u32[]{:S(2)}, u32[]{:S(2)}) async-start(bf16[8,2,448,128]{3,2,1,0:T(8,128)(2,1)} %shard_map.85), calls=%async_computation.1 | async-start | bytes 3670016 | tf_op jit(solution)/shard_map/all_to_all | solution.py:349
  38.7 27.0 %collective-permute-start = (bf16[8,2,2,128,128]{4,3,2,1,0:T(8,128)(2,1)S(1)}, bf16[8,2,2,128,128]{4,3,2,1,0:T(8,128)(2,1)}, u32[]{:S(2)}, u32[]{:S(2)}) collective-permute-start(bf16[8,2,2,128,128]{4,3,2,1,0:T(8,128)(2,1)S(1)} %slice.12), channel_id=1, source_target_pairs={{0,32},{32,64},{64,96},{1,33},{33,65},{65,97},{2,34},{34,66},{66,9... | collective-permute-start | bytes 3145736 | tf_op jit(solution)/shard_map/ppermute | solution.py:359
  43.6 4.4 %collective-permute-start.2 = (bf16[8,2,3,32,128]{4,3,2,1,0:T(8,128)(2,1)S(1)}, bf16[8,2,3,32,128]{4,3,2,1,0:T(8,128)(2,1)S(1)}, u32[]{:S(2)}, u32[]{:S(2)}) collective-permute-start(bf16[8,2,3,32,128]{4,3,2,1,0:T(8,128)(2,1)S(1)} %get-tuple-element.28), channel_id=1, source_target_pairs={{1,0},{2,1},{3,2},{5,4},{6,5},{7,6},{9,8},{10,9},{11,10},{13,12},{... | collective-permute-start | bytes 1179656 | tf_op jit(solution)/shard_map/ppermute | solution.py:361
  44.9 4.4 %collective-permute-start.1 = (bf16[8,2,3,32,128]{4,3,2,1,0:T(8,128)(2,1)S(1)}, bf16[8,2,3,32,128]{4,3,2,1,0:T(8,128)(2,1)S(1)}, u32[]{:S(2)}, u32[]{:S(2)}) collective-permute-start(bf16[8,2,3,32,128]{4,3,2,1,0:T(8,128)(2,1)S(1)} %get-tuple-element.29), channel_id=1, source_target_pairs={{0,1},{1,2},{2,3},{4,5},{5,6},{6,7},{8,9},{9,10},{10,11},{12,13},{... | collective-permute-start | bytes 1179656 | tf_op jit(solution)/shard_map/ppermute | solution.py:360
  48.0 17.7 %copy-start.6 = (bf16[8,2,3,32,128]{4,3,2,1,0:T(8,128)(2,1)}, bf16[8,2,3,32,128]{4,3,2,1,0:T(8,128)(2,1)S(1)}, u32[]{:S(2)}) copy-start(bf16[8,2,3,32,128]{4,3,2,1,0:T(8,128)(2,1)S(1)} %collective-permute-done.2.high_ref) | copy-start | bytes 1179652
  49.3 16.4 %copy-start.7 = (bf16[8,2,3,32,128]{4,3,2,1,0:T(8,128)(2,1)}, bf16[8,2,3,32,128]{4,3,2,1,0:T(8,128)(2,1)S(1)}, u32[]{:S(2)}) copy-start(bf16[8,2,3,32,128]{4,3,2,1,0:T(8,128)(2,1)S(1)} %collective-permute-done.1.low_ref) | copy-start | bytes 1179652
  87.5 32.7 %copy-start = (bf16[8,2,3,128,128]{4,3,2,1,0:T(8,128)(2,1)S(1)}, bf16[8,2,3,128,128]{4,3,2,1,0:T(8,128)(2,1)}, u32[]{:S(2)}) copy-start(bf16[8,2,3,128,128]{4,3,2,1,0:T(8,128)(2,1)} %get-tuple-element.21.own_ref) | copy-start | bytes 4718596
  87.5 34.6 %all-to-all-start.2 = ((bf16[8,2,448,128]{3,2,1,0:T(8,128)(2,1)}), bf16[8,2,448,128]{3,2,1,0:T(8,128)(2,1)S(1)}, u32[]{:S(2)}, u32[]{:S(2)}) async-start(bf16[8,2,448,128]{3,2,1,0:T(8,128)(2,1)} %get-tuple-element.18), calls=%async_computation.2 | async-start | bytes 3670016 | tf_op jit(solution)/shard_map/all_to_all | solution.py:349
  92.5 27.8 %collective-permute-start.4 = (bf16[8,2,2,128,128]{4,3,2,1,0:T(8,128)(2,1)}, bf16[8,2,2,128,128]{4,3,2,1,0:T(8,128)(2,1)S(1)}, u32[]{:S(2)}, u32[]{:S(2)}) collective-permute-start(bf16[8,2,2,128,128]{4,3,2,1,0:T(8,128)(2,1)} %get-tuple-element.22), channel_id=1, source_target_pairs={{32,0},{64,32},{96,64},{33,1},{65,33},{97,65},{34,2},{66,34},{98,6... | collective-permute-start | bytes 3145736 | tf_op jit(solution)/shard_map/ppermute | solution.py:364
  93.7 3.5 %collective-permute-start.5 = (bf16[8,2,3,32,128]{4,3,2,1,0:T(8,128)(2,1)}, bf16[8,2,3,32,128]{4,3,2,1,0:T(8,128)(2,1)S(1)}, u32[]{:S(2)}, u32[]{:S(2)}) collective-permute-start(bf16[8,2,3,32,128]{4,3,2,1,0:T(8,128)(2,1)} %get-tuple-element.23), channel_id=1, source_target_pairs={{0,1},{1,2},{2,3},{4,5},{5,6},{6,7},{8,9},{9,10},{10,11},{12,13},{... | collective-permute-start | bytes 1179656 | tf_op jit(solution)/shard_map/ppermute | solution.py:366
  95.7 4.0 %collective-permute-start.6 = (bf16[8,2,3,32,128]{4,3,2,1,0:T(8,128)(2,1)}, bf16[8,2,3,32,128]{4,3,2,1,0:T(8,128)(2,1)S(1)}, u32[]{:S(2)}, u32[]{:S(2)}) collective-permute-start(bf16[8,2,3,32,128]{4,3,2,1,0:T(8,128)(2,1)} %get-tuple-element.24), channel_id=1, source_target_pairs={{1,0},{2,1},{3,2},{5,4},{6,5},{7,6},{9,8},{10,9},{11,10},{13,12},{... | collective-permute-start | bytes 1179656 | tf_op jit(solution)/shard_map/ppermute | solution.py:365
  122.1 28.8 %all-to-all-start.3 = ((bf16[8,2,3,128,128]{4,3,2,1,0:T(8,128)(2,1)}), bf16[8,2,3,128,128]{4,3,2,1,0:T(8,128)(2,1)S(1)}, u32[]{:S(2)}, u32[]{:S(2)}) async-start(bf16[8,2,3,128,128]{4,3,2,1,0:T(8,128)(2,1)} %shard_map.88), calls=%async_computation.3 | async-start | bytes 3145728 | tf_op jit(solution)/shard_map/all_to_all | solution.py:349
  130.3 8.8 %collective-permute-start.7 = (bf16[4,2,128,128]{3,2,1,0:T(8,128)(2,1)S(1)}, bf16[4,2,128,128]{3,2,1,0:T(8,128)(2,1)S(1)}, u32[]{:S(2)}, u32[]{:S(2)}) collective-permute-start(bf16[4,2,128,128]{3,2,1,0:T(8,128)(2,1)S(1)} %get-tuple-element.25), channel_id=1, source_target_pairs={{32,0},{64,32},{96,64},{33,1},{65,33},{97,65},{34,2},{66,34},{98,6... | collective-permute-start | bytes 786440 | tf_op jit(solution)/shard_map/ppermute | solution.py:373

commit v4 on v3

--- a/solution.py
+++ b/solution.py
@@ -17,8 +17,9 @@
 FULL = 2
 SLOTS = 3
 HALF = TOK // 2
-Q_ROWS = FULL * TOK + HALF
-ALL_ROWS = Q_ROWS + TOK
+PAST_ROWS = slice(2 * TOK, 3 * TOK)
+SHARED_ROWS = slice(3 * TOK, 3 * TOK + HALF)
+ALL_ROWS = 3 * TOK + HALF
 LOW = -1.0e30
 FACTOR = DIM ** -0.5
 LOG2E = 1.4426950408889634
@@ -51,8 +52,8 @@
         for kind, ref in enumerate((q_ref, do_ref)):
             for slot in range(FULL):
                 qdo_ref[place, kind, slot * TOK : (slot + 1) * TOK] = ref[:, head_cols(place, slot)]
-            qdo_ref[place, kind, FULL * TOK : Q_ROWS] = ref[start : start + HALF, head_cols(place, FULL)]
-            qdo_ref[place, kind, Q_ROWS:] = raw_ref[place // N_X, kind]
+            qdo_ref[place, kind, SHARED_ROWS] = ref[start : start + HALF, head_cols(place, FULL)]
+            qdo_ref[place, kind, PAST_ROWS] = raw_ref[place // N_X, kind]
 
 
 def unpack_queries_kernel(odq_ref, o_ref, dq_ref, raw_ref):
@@ -61,10 +62,10 @@
         for kind, ref in enumerate((o_ref, dq_ref)):
             for slot in range(FULL):
                 ref[:, head_cols(place, slot)] = odq_ref[place, kind, slot * TOK : (slot + 1) * TOK]
-            ref[start : start + HALF, head_cols(place, FULL)] = odq_ref[place, kind, FULL * TOK : Q_ROWS]
+            ref[start : start + HALF, head_cols(place, FULL)] = odq_ref[place, kind, SHARED_ROWS]
     for kind in range(2):
         for y in range(N_Y):
-            first, second = odq_ref[y * N_X, kind, Q_ROWS:], odq_ref[y * N_X + 1, kind, Q_ROWS:]
+            first, second = odq_ref[y * N_X, kind, PAST_ROWS], odq_ref[y * N_X + 1, kind, PAST_ROWS]
             raw_ref[y, kind] = (first.astype(F32) + second.astype(F32)).astype(BF16)
 
 
@@ -106,6 +107,7 @@
 UNIT = 2 * TOK
 CAT = 2 * N_LOC * TOK
 N_PAST = 8
+N_PHASES = 5
 
 
 def queries_job(
@@ -162,6 +164,7 @@
             here = here + bias
         top = here if top is None else jnp.maximum(top, here)
         biases.append(bias)
+    yield
     top = jnp.max(top, axis=0, keepdims=True)
     total = jnp.zeros((8, LANES), F32)
     for b in range(n_blocks):
@@ -176,6 +179,7 @@
     do_t = (do.astype(F32).T * inverse).astype(BF16).astype(F32)
     do = do_t.T.astype(BF16)
     do_all[lanes, :] = do
+    yield
     out_t = dot_nn(vtr[:, window_rows], p_ref[window_rows, lanes])
     for half in range(groups // 2):
         out_t = out_t + dot_nn(v_borders[half].T, p_ref[CAT + half * TOK : CAT + (half + 1) * TOK, lanes])
@@ -184,11 +188,13 @@
     out = out_b.T.astype(BF16)
     for g, loc in enumerate(locs):
         put_query(loc, 0, out[g * rows : (g + 1) * rows])
+    yield
     for b in range(n_blocks):
         vals = vcat[base + b * TOK : base + (b + 1) * TOK, :] if b < n_win else v_borders[b - n_win]
         at = base + b * TOK if b < n_win else CAT + (b - n_win) * TOK
         ds = p_ref[at : at + TOK, lanes].astype(F32) * (dot_nt(vals, do) - delta)
         ds_ref[at : at + TOK, lanes] = ds.astype(BF16)
+    yield
     dq_t = dot_nn(ktr[:, window_rows], ds_ref[window_rows, lanes])
     for half in range(groups // 2):
         dq_t = dq_t + dot_nn(k_borders[half].T, ds_ref[CAT + half * TOK : CAT + (half + 1) * TOK, lanes])
@@ -203,6 +209,7 @@
             for which, loc in enumerate(locs[2 * half : 2 * half + 2]):
                 at = which * 2 * HALO
                 put_border(loc, kind, grad[at : at + HALO], grad[at + HALO : at + 2 * HALO])
+    yield
 
 
 def keys_job(rows, put_past, put_own, q_all, do_all, p_ref, ds_ref):
@@ -236,11 +243,17 @@
     kcat, vcat, ktr, vtr, q_all, do_all, s0_ref, s1_ref, p_ref, ds_ref = scratch
     xh, tile = lax.axis_index("xh"), lax.axis_index("xl") * 2 + lax.axis_index("core")
     load_keys(get_past, get_own, kcat, vcat, ktr, vtr)
-    for job in range(N_LOC * rows // LANES):
+    jobs = [
         queries_job(
             rows, job, window, no_past, xh, tile, get_query, get_border, put_query, put_border,
             kcat, vcat, ktr, vtr, q_all, do_all, s1_ref if job % 2 else s0_ref, p_ref, ds_ref,
         )
+        for job in range(N_LOC * rows // LANES)
+    ]
+    for step in range(N_PHASES + len(jobs) - 1):
+        for at, job in reversed(list(enumerate(jobs))):
+            if 0 <= step - at < N_PHASES:
+                next(job)
     keys_job(rows, put_past, put_own, q_all, do_all, p_ref, ds_ref)
 
 
@@ -252,7 +265,8 @@
 
 
 def attention_kernel(
-    window_ref, kv_ref, past_ref, low_ref, high_ref, q_ref, o_ref, own_ref, back_ref, dlow_ref, dhigh_ref, *scratch
+    window_ref, kv_ref, past_ref, low_ref, high_ref, q_ref, past2_ref, q2_ref,
+    o_out, own_ref, back_ref, dlow_ref, dhigh_ref, o_ref, sems, *scratch,
 ):
     y, xh = lax.axis_index("y"), lax.axis_index("xh")
 
@@ -260,25 +274,41 @@
         dlow_ref[loc, kind, 0] = low
         dhigh_ref[loc, kind, 0] = high
 
+    def moves(rows, first):
+        return [
+            pltpu.make_async_copy(o_ref.at[:, kind, rows], o_out.at[:, kind, rows], sems.at[first + kind])
+            for kind in range(2)
+        ]
+
+    parts = (slice(0, TOK), slice(TOK, 2 * TOK), PAST_ROWS, SHARED_ROWS)
+
     def slot_work(slot):
         rows = TOK if slot < FULL else HALF
-        q_rows = slice(slot * TOK, slot * TOK + rows)
+        q_rows = parts[slot] if slot < FULL else SHARED_ROWS
 
         def put_query(loc, kind, value):
             o_ref[loc, kind, q_rows] = value
 
         def put_past(loc, kind, value):
-            o_ref[loc, kind, Q_ROWS:] = value
+            o_ref[loc, kind, PAST_ROWS] = value
 
         attention_body(
             rows, window_ref[5 * y + (2 * xh + slot if slot < FULL else 4)], lax.axis_index("z") == 0,
-            (lambda loc, kind: past_ref[loc, kind, 0]) if slot < FULL else (lambda loc, kind: q_ref[loc, kind, Q_ROWS:]),
+            (lambda loc, kind: past_ref[loc, kind, 0]) if slot < FULL else (lambda loc, kind: past2_ref[loc, kind]),
             lambda loc, kind: kv_ref[loc, kind, 0],
-            lambda loc, kind: q_ref[loc, kind, q_rows],
+            lambda loc, kind: (q_ref if slot < FULL else q2_ref)[loc, kind],
             lambda loc, kind, side: (high_ref if side else low_ref)[loc, kind, 0],
             put_query, put_border, put_into(back_ref, 0) if slot < FULL else put_past, put_into(own_ref, 0),
             *scratch,
         )
+        mine = [slot] if slot < FULL else [2, 3]
+        for part in mine:
+            for move in moves(parts[part], 2 * part):
+                move.start()
+        if slot == FULL:
+            for part in range(4):
+                for move in moves(parts[part], 2 * part):
+                    move.wait()
 
     for slot in range(SLOTS):
         pl.when(pl.program_id(0) == slot)(functools.partial(slot_work, slot))
@@ -340,9 +370,15 @@
 
 
 def attend(window, kv, past, low, high, qdo):
-    specs = [SMEM, by_slot(TOK), by_full_slot(), by_slot(HALO), by_slot(HALO), whole(Q_SHAPE)]
-    outs = [(Q_SHAPE, whole(Q_SHAPE)), (KV_SHAPE, by_slot(TOK)), (PAIR_SHAPE, by_full_slot())] + [(BORDER_SHAPE, by_slot(HALO))] * 2
-    return call(attention_kernel, SLOTS, specs, (window, kv, past, low, high, qdo), outs, 10**10, SCRATCH, limit=ATTEND_MIB)
+    q_spec = pl.BlockSpec((N_LOC, 2, TOK, DIM), lambda slot: (0, 0, jnp.minimum(slot, FULL - 1), 0))
+    past2_spec = pl.BlockSpec((N_LOC, 2, TOK, DIM), lambda slot: (0, 0, 2, 0))
+    q2_spec = pl.BlockSpec((N_LOC, 2, HALF, DIM), lambda slot: (0, 0, 6, 0))
+    specs = [SMEM, by_slot(TOK), by_full_slot(), by_slot(HALO), by_slot(HALO), q_spec, past2_spec, q2_spec]
+    outs = [(Q_SHAPE, ANYWHERE), (KV_SHAPE, by_slot(TOK)), (PAIR_SHAPE, by_full_slot())]
+    outs += [(BORDER_SHAPE, by_slot(HALO))] * 2
+    scratch = [pltpu.VMEM(Q_SHAPE, BF16), pltpu.SemaphoreType.DMA((8,)), *SCRATCH]
+    args = (window, kv, past, low, high, qdo, qdo, qdo)
+    return call(attention_kernel, SLOTS, specs, args, outs, 10**10, scratch, limit=ATTEND_MIB)
 
 
 def exchange(x):
@@ -352,7 +388,7 @@
 def shards(queries, keys, values, cotangent, window):
     up = [(i, i + 1) for i in range(N_Z - 1)]
     down = [(i + 1, i) for i in range(N_Z - 1)]
-    packed_kv, raw = simple(pack_keys_kernel, (keys, values), [KV_SHAPE, RAW_SHAPE])
+    packed_kv, raw = simple(pack_keys_kernel, (keys, values), [KV_SHAPE, RAW_SHAPE], limit=60)
     raw = lax.ppermute(raw, "z", up)
     (packed_q,) = simple(pack_queries_kernel, (queries, cotangent, raw), [Q_SHAPE])
     kv = exchange(packed_kv)

time: 153 us -> 149 us (0.974)
  local copies, waits for them, and re-layouts: 2.38 us -> 0.22 us
    unnamed x16 -> x14, local copies, waits for them, and re-layouts: 2.19 us -> 0.03 us
where the time goes in v4:
time: 149 us
  waiting for transfers between devices  77.7 us (52%)
  starting transfers between devices  42.1 us (28%)
  Pallas kernels  28 us (19%)
    all_to_all x4, waiting for transfers between devices, exchange(): return lax.all_to_all(x, PLACES, 0, 0)  40.5 us
    pallas_call x6, Pallas kernels, call(): pl.pallas_call(kernel, grid=(grid,), out_shape=[jax.ShapeDtypeStruct(shap...  28 us
    all_to_all x4, starting transfers between devices, exchange(): return lax.all_to_all(x, PLACES, 0, 0)  23.3 us
    ppermute x1, waiting for transfers between devices, shards(): got = lax.ppermute(back, 'z', down)  20.5 us
    ppermute x1, waiting for transfers between devices, shards(): raw = lax.ppermute(raw, 'z', down)  7.47 us
    ppermute x1, waiting for transfers between devices, shards(): raw = lax.ppermute(raw, 'z', up)  5.25 us
    ppermute x1, starting transfers between devices, shards(): past = lax.ppermute(kv[:, :, :FULL], 'z', up)  4.8 us
    ppermute x1, starting transfers between devices, shards(): raw = lax.ppermute(raw, 'z', up)  3.84 us
  transfers between devices with their start and end apart: 12, of which 9 were waited for; matrix products, arithmetic and copies ran while one was open for 0% of the time, Pallas kernels for 3%

profile of v4, /device:TPU:0, one launch (start us, length us, event | category | flops | bytes accessed | tf_op | source)
XLA Modules:
  0.0 148.8 jit_solution(15117409665391205580)
XLA Ops:
  0.6 2.8 %shard_map.84 = (bf16[8,2,3,128,128]{4,3,2,1,0:T(8,128)(2,1)}, bf16[4,2,128,128]{3,2,1,0:T(8,128)(2,1)}) custom-call(bf16[128,2560]{1,0:T(8,128)(2,1)} %k_ref.1, bf16[128,2560]{1,0:T(8,128)(2,1)} %v_ref.1), custom_call_target="tpu_custom_call" | custom-call | bytes 3145728 | tf_op jit(solution)/shard_map/pallas_call | solution.py:340
  3.4 0.0 copy-start.6
  3.4 0.0 copy-start.1
  3.4 0.0 copy-start.2
  3.4 7.2 %all-to-all-start = ((bf16[8,2,3,128,128]{4,3,2,1,0:T(8,128)(2,1)}), bf16[8,2,3,128,128]{4,3,2,1,0:T(8,128)(2,1)S(1)}, u32[]{:S(2)}, u32[]{:S(2)}) async-start(bf16[8,2,3,128,128]{4,3,2,1,0:T(8,128)(2,1)} %get-tuple-element.16), calls=%async_computation | async-start | bytes 3145728 | tf_op jit(solution)/shard_map/all_to_all | solution.py:385
  10.6 0.0 copy-done.6
  10.6 3.8 %collective-permute-start.3 = (bf16[4,2,128,128]{3,2,1,0:T(8,128)(2,1)S(1)}, bf16[4,2,128,128]{3,2,1,0:T(8,128)(2,1)S(1)}, u32[]{:S(2)}, u32[]{:S(2)}) collective-permute-start(bf16[4,2,128,128]{3,2,1,0:T(8,128)(2,1)S(1)} %copy-done.6), channel_id=1, source_target_pairs={{0,32},{32,64},{64,96},{1,33},{33,65},{65,97},{2,34},{34,66},{66,9... | collective-permute-start | bytes 786440 | tf_op jit(solution)/shard_map/ppermute | solution.py:392
  14.4 5.3 %collective-permute-done.3.raw_ref = bf16[4,2,128,128]{3,2,1,0:T(8,128)(2,1)S(1)} collective-permute-done((bf16[4,2,128,128]{3,2,1,0:T(8,128)(2,1)S(1)}, bf16[4,2,128,128]{3,2,1,0:T(8,128)(2,1)S(1)}, u32[]{:S(2)}, u32[]{:S(2)}) %collective-permute-start.3) | collective-permute-done | bytes 262176 | tf_op jit(solution)/shard_map/ppermute | solution.py:392
  19.7 0.0 copy-done.1
  19.7 0.0 copy-done.2
  19.7 1.5 %shard_map.85 = bf16[8,2,448,128]{3,2,1,0:T(8,128)(2,1)} custom-call(bf16[128,2560]{1,0:T(8,128)(2,1)S(1)} %copy-done.1, bf16[128,2560]{1,0:T(8,128)(2,1)S(1)} %copy-done.2, bf16[4,2,128,128]{3,2,1,0:T(8,128)(2,1)S(1)} %collective-permute-done.3.raw_ref), custom_call_target="tpu_custom_call" | custom-call | bytes 3407872 | tf_op jit(solution)/shard_map/pallas_call | solution.py:340
  21.2 12.3 %all-to-all-done.kv_ref = bf16[8,2,3,128,128]{4,3,2,1,0:T(8,128)(2,1)S(1)} async-done(((bf16[8,2,3,128,128]{4,3,2,1,0:T(8,128)(2,1)}), bf16[8,2,3,128,128]{4,3,2,1,0:T(8,128)(2,1)S(1)}, u32[]{:S(2)}, u32[]{:S(2)}) %all-to-all-start) | async-done | bytes 1572896 | tf_op jit(solution)/shard_map/all_to_all | solution.py:385
  33.4 0.0 copy-start.3
  33.5 4.3 %all-to-all-start.1 = ((bf16[8,2,448,128]{3,2,1,0:T(8,128)(2,1)}), bf16[8,2,448,128]{3,2,1,0:T(8,128)(2,1)}, u32[]{:S(2)}, u32[]{:S(2)}) async-start(bf16[8,2,448,128]{3,2,1,0:T(8,128)(2,1)} %shard_map.85), calls=%async_computation.1 | async-start | bytes 3670016 | tf_op jit(solution)/shard_map/all_to_all | solution.py:385
  37.8 0.1 slice.12
  37.9 4.8 %collective-permute-start = (bf16[8,2,2,128,128]{4,3,2,1,0:T(8,128)(2,1)S(1)}, bf16[8,2,2,128,128]{4,3,2,1,0:T(8,128)(2,1)}, u32[]{:S(2)}, u32[]{:S(2)}) collective-permute-start(bf16[8,2,2,128,128]{4,3,2,1,0:T(8,128)(2,1)S(1)} %slice.12), channel_id=1, source_target_pairs={{0,32},{32,64},{64,96},{1,33},{33,65},{65,97},{2,34},{34,66},{66,9... | collective-permute-start | bytes 3145736 | tf_op jit(solution)/shard_map/ppermute | solution.py:395
  42.7 0.0 copy-done.3
  42.7 0.1 fusion
  42.8 1.3 collective-permute-start.2
  44.1 3.1 %collective-permute-start.1 = (bf16[8,2,3,32,128]{4,3,2,1,0:T(8,128)(2,1)S(1)}, bf16[8,2,3,32,128]{4,3,2,1,0:T(8,128)(2,1)S(1)}, u32[]{:S(2)}, u32[]{:S(2)}) collective-permute-start(bf16[8,2,3,32,128]{4,3,2,1,0:T(8,128)(2,1)S(1)} %get-tuple-element.29), channel_id=1, source_target_pairs={{0,1},{1,2},{2,3},{4,5},{5,6},{6,7},{8,9},{9,10},{10,11},{12,13},{... | collective-permute-start | bytes 1179656 | tf_op jit(solution)/shard_map/ppermute | solution.py:396
  47.2 0.0 collective-permute-done.2.high_ref
  47.2 0.0 copy-start.4
  47.2 1.3 collective-permute-done.1.low_ref
  48.5 0.0 copy-start.5
  48.5 16.4 %all-to-all-done.1.q_ref.past2_ref.q2_ref = bf16[8,2,448,128]{3,2,1,0:T(8,128)(2,1)} async-done(((bf16[8,2,448,128]{3,2,1,0:T(8,128)(2,1)}), bf16[8,2,448,128]{3,2,1,0:T(8,128)(2,1)}, u32[]{:S(2)}, u32[]{:S(2)}) %all-to-all-start.1) | async-done | bytes 1835040 | tf_op jit(solution)/shard_map/all_to_all | solution.py:385
  64.9 0.0 collective-permute-done.past_ref
  64.9 0.0 copy-done.4
  64.9 0.0 copy-done.5
  64.9 19.2 %shard_map.86 = (bf16[8,2,448,128]{3,2,1,0:T(8,128)(2,1)}, bf16[8,2,3,128,128]{4,3,2,1,0:T(8,128)(2,1)}, bf16[8,2,2,128,128]{4,3,2,1,0:T(8,128)(2,1)}, bf16[8,2,...) custom-call(s32[20]{0:T(128)} %window_ref.1, bf16[8,2,3,128,128]{4,3,2,1,0:T(8,128)(2,1)} %copy-done.3, ...), custom_call_target="tpu_custom_call" | custom-call | flops 10000000000 | bytes 14155856 | tf_op jit(solution)/shard_map/pallas_call | solution.py:340
  84.2 0.0 copy-start
  84.2 4.9 %all-to-all-start.2 = ((bf16[8,2,448,128]{3,2,1,0:T(8,128)(2,1)}), bf16[8,2,448,128]{3,2,1,0:T(8,128)(2,1)S(1)}, u32[]{:S(2)}, u32[]{:S(2)}) async-start(bf16[8,2,448,128]{3,2,1,0:T(8,128)(2,1)} %get-tuple-element.18), calls=%async_computation.2 | async-start | bytes 3670016 | tf_op jit(solution)/shard_map/all_to_all | solution.py:385
  89.1 1.3 collective-permute-start.4
  90.4 2.0 %collective-permute-start.5 = (bf16[8,2,3,32,128]{4,3,2,1,0:T(8,128)(2,1)}, bf16[8,2,3,32,128]{4,3,2,1,0:T(8,128)(2,1)S(1)}, u32[]{:S(2)}, u32[]{:S(2)}) collective-permute-start(bf16[8,2,3,32,128]{4,3,2,1,0:T(8,128)(2,1)} %get-tuple-element.23), channel_id=1, source_target_pairs={{0,1},{1,2},{2,3},{4,5},{5,6},{6,7},{8,9},{9,10},{10,11},{12,13},{... | collective-permute-start | bytes 1179656 | tf_op jit(solution)/shard_map/ppermute | solution.py:402
  92.4 1.3 collective-permute-start.6
  93.7 0.2 collective-permute-done.5.from_low_ref
  93.9 2.5 %collective-permute-done.6.from_high_ref = bf16[8,2,3,32,128]{4,3,2,1,0:T(8,128)(2,1)S(1)} collective-permute-done((bf16[8,2,3,32,128]{4,3,2,1,0:T(8,128)(2,1)}, bf16[8,2,3,32,128]{4,3,2,1,0:T(8,128)(2,1)S(1)}, u32[]{:S(2)}, u32[]{:S(2)}) %collective-permute-start.6) | collective-permute-done | bytes 393248 | tf_op jit(solution)/shard_map/ppermute | solution.py:401
  96.3 20.5 %collective-permute-done.4.got_ref = bf16[8,2,2,128,128]{4,3,2,1,0:T(8,128)(2,1)S(1)} collective-permute-done((bf16[8,2,2,128,128]{4,3,2,1,0:T(8,128)(2,1)}, bf16[8,2,2,128,128]{4,3,2,1,0:T(8,128)(2,1)S(1)}, u32[]{:S(2)}, u32[]{:S(2)}) %collective-permute-start.4) | collective-permute-done | bytes 1048608 | tf_op jit(solution)/shard_map/ppermute | solution.py:400
  116.9 0.0 copy-done
  116.9 1.9 %shard_map.88 = bf16[8,2,3,128,128]{4,3,2,1,0:T(8,128)(2,1)} custom-call(bf16[8,2,3,128,128]{4,3,2,1,0:T(8,128)(2,1)S(1)} %copy-done, bf16[8,2,2,128,128]{4,3,2,1,0:T(8,128)(2,1)S(1)} %collective-permute-done.4.got_ref, bf16[8,2,3,32,128]{4,3,2,1,0:T(8,128)(2,1)S(1)} %collective-permute-done.5.from_low_ref, ...), custom_call_target="tpu_custom_call" | custom-call | bytes 4980736 | tf_op jit(solution)/shard_map/pallas_call | solution.py:340
  118.7 0.0 all-to-all-done.2.odq_ref
  118.7 6.9 %all-to-all-start.3 = ((bf16[8,2,3,128,128]{4,3,2,1,0:T(8,128)(2,1)}), bf16[8,2,3,128,128]{4,3,2,1,0:T(8,128)(2,1)S(1)}, u32[]{:S(2)}, u32[]{:S(2)}) async-start(bf16[8,2,3,128,128]{4,3,2,1,0:T(8,128)(2,1)} %shard_map.88), calls=%async_computation.3 | async-start | bytes 3145728 | tf_op jit(solution)/shard_map/all_to_all | solution.py:385
  125.7 1.3 shard_map.87
  127.0 1.3 collective-permute-start.7
  128.3 7.5 %collective-permute-done.7.raw_ref = bf16[4,2,128,128]{3,2,1,0:T(8,128)(2,1)S(1)} collective-permute-done((bf16[4,2,128,128]{3,2,1,0:T(8,128)(2,1)S(1)}, bf16[4,2,128,128]{3,2,1,0:T(8,128)(2,1)S(1)}, u32[]{:S(2)}, u32[]{:S(2)}) %collective-permute-start.7) | collective-permute-done | bytes 262176 | tf_op jit(solution)/shard_map/ppermute | solution.py:409
  135.7 11.8 %all-to-all-done.3.grads_ref = bf16[8,2,3,128,128]{4,3,2,1,0:T(8,128)(2,1)S(1)} async-done(((bf16[8,2,3,128,128]{4,3,2,1,0:T(8,128)(2,1)}), bf16[8,2,3,128,128]{4,3,2,1,0:T(8,128)(2,1)S(1)}, u32[]{:S(2)}, u32[]{:S(2)}) %all-to-all-start.3) | async-done | bytes 1572896 | tf_op jit(solution)/shard_map/all_to_all | solution.py:385
  147.5 1.3 shard_map.89
Async XLA Ops:
  3.4 7.2 %copy-start.6 = (bf16[4,2,128,128]{3,2,1,0:T(8,128)(2,1)S(1)}, bf16[4,2,128,128]{3,2,1,0:T(8,128)(2,1)}, u32[]{:S(2)}) copy-start(bf16[4,2,128,128]{3,2,1,0:T(8,128)(2,1)} %get-tuple-element.17) | copy-start | bytes 786436
  3.4 16.3 %copy-start.1 = (bf16[128,2560]{1,0:T(8,128)(2,1)S(1)}, bf16[128,2560]{1,0:T(8,128)(2,1)}, u32[]{:S(2)}) copy-start(bf16[128,2560]{1,0:T(8,128)(2,1)} %q_ref.1) | copy-start | bytes 1966084
  3.4 16.3 %copy-start.2 = (bf16[128,2560]{1,0:T(8,128)(2,1)S(1)}, bf16[128,2560]{1,0:T(8,128)(2,1)}, u32[]{:S(2)}) copy-start(bf16[128,2560]{1,0:T(8,128)(2,1)} %do_ref.1) | copy-start | bytes 1966084
  3.4 30.0 %all-to-all-start = ((bf16[8,2,3,128,128]{4,3,2,1,0:T(8,128)(2,1)}), bf16[8,2,3,128,128]{4,3,2,1,0:T(8,128)(2,1)S(1)}, u32[]{:S(2)}, u32[]{:S(2)}) async-start(bf16[8,2,3,128,128]{4,3,2,1,0:T(8,128)(2,1)} %get-tuple-element.16), calls=%async_computation | async-start | bytes 3145728 | tf_op jit(solution)/shard_map/all_to_all | solution.py:385
  10.6 9.1 %collective-permute-start.3 = (bf16[4,2,128,128]{3,2,1,0:T(8,128)(2,1)S(1)}, bf16[4,2,128,128]{3,2,1,0:T(8,128)(2,1)S(1)}, u32[]{:S(2)}, u32[]{:S(2)}) collective-permute-start(bf16[4,2,128,128]{3,2,1,0:T(8,128)(2,1)S(1)} %copy-done.6), channel_id=1, source_target_pairs={{0,32},{32,64},{64,96},{1,33},{33,65},{65,97},{2,34},{34,66},{66,9... | collective-permute-start | bytes 786440 | tf_op jit(solution)/shard_map/ppermute | solution.py:392
  33.4 9.2 %copy-start.3 = (bf16[8,2,3,128,128]{4,3,2,1,0:T(8,128)(2,1)}, bf16[8,2,3,128,128]{4,3,2,1,0:T(8,128)(2,1)S(1)}, u32[]{:S(2)}) copy-start(bf16[8,2,3,128,128]{4,3,2,1,0:T(8,128)(2,1)S(1)} %all-to-all-done.kv_ref) | copy-start | bytes 4718596
  33.5 31.5 %all-to-all-start.1 = ((bf16[8,2,448,128]{3,2,1,0:T(8,128)(2,1)}), bf16[8,2,448,128]{3,2,1,0:T(8,128)(2,1)}, u32[]{:S(2)}, u32[]{:S(2)}) async-start(bf16[8,2,448,128]{3,2,1,0:T(8,128)(2,1)} %shard_map.85), calls=%async_computation.1 | async-start | bytes 3670016 | tf_op jit(solution)/shard_map/all_to_all | solution.py:385
  37.9 27.0 %collective-permute-start = (bf16[8,2,2,128,128]{4,3,2,1,0:T(8,128)(2,1)S(1)}, bf16[8,2,2,128,128]{4,3,2,1,0:T(8,128)(2,1)}, u32[]{:S(2)}, u32[]{:S(2)}) collective-permute-start(bf16[8,2,2,128,128]{4,3,2,1,0:T(8,128)(2,1)S(1)} %slice.12), channel_id=1, source_target_pairs={{0,32},{32,64},{64,96},{1,33},{33,65},{65,97},{2,34},{34,66},{66,9... | collective-permute-start | bytes 3145736 | tf_op jit(solution)/shard_map/ppermute | solution.py:395
  42.8 4.4 %collective-permute-start.2 = (bf16[8,2,3,32,128]{4,3,2,1,0:T(8,128)(2,1)S(1)}, bf16[8,2,3,32,128]{4,3,2,1,0:T(8,128)(2,1)S(1)}, u32[]{:S(2)}, u32[]{:S(2)}) collective-permute-start(bf16[8,2,3,32,128]{4,3,2,1,0:T(8,128)(2,1)S(1)} %get-tuple-element.28), channel_id=1, source_target_pairs={{1,0},{2,1},{3,2},{5,4},{6,5},{7,6},{9,8},{10,9},{11,10},{13,12},{... | collective-permute-start | bytes 1179656 | tf_op jit(solution)/shard_map/ppermute | solution.py:397
  44.1 4.4 %collective-permute-start.1 = (bf16[8,2,3,32,128]{4,3,2,1,0:T(8,128)(2,1)S(1)}, bf16[8,2,3,32,128]{4,3,2,1,0:T(8,128)(2,1)S(1)}, u32[]{:S(2)}, u32[]{:S(2)}) collective-permute-start(bf16[8,2,3,32,128]{4,3,2,1,0:T(8,128)(2,1)S(1)} %get-tuple-element.29), channel_id=1, source_target_pairs={{0,1},{1,2},{2,3},{4,5},{5,6},{6,7},{8,9},{9,10},{10,11},{12,13},{... | collective-permute-start | bytes 1179656 | tf_op jit(solution)/shard_map/ppermute | solution.py:396
  47.2 17.8 %copy-start.4 = (bf16[8,2,3,32,128]{4,3,2,1,0:T(8,128)(2,1)}, bf16[8,2,3,32,128]{4,3,2,1,0:T(8,128)(2,1)S(1)}, u32[]{:S(2)}) copy-start(bf16[8,2,3,32,128]{4,3,2,1,0:T(8,128)(2,1)S(1)} %collective-permute-done.2.high_ref) | copy-start | bytes 1179652
  48.5 16.5 %copy-start.5 = (bf16[8,2,3,32,128]{4,3,2,1,0:T(8,128)(2,1)}, bf16[8,2,3,32,128]{4,3,2,1,0:T(8,128)(2,1)S(1)}, u32[]{:S(2)}) copy-start(bf16[8,2,3,32,128]{4,3,2,1,0:T(8,128)(2,1)S(1)} %collective-permute-done.1.low_ref) | copy-start | bytes 1179652
  84.2 32.7 %copy-start = (bf16[8,2,3,128,128]{4,3,2,1,0:T(8,128)(2,1)S(1)}, bf16[8,2,3,128,128]{4,3,2,1,0:T(8,128)(2,1)}, u32[]{:S(2)}) copy-start(bf16[8,2,3,128,128]{4,3,2,1,0:T(8,128)(2,1)} %get-tuple-element.21.own_ref) | copy-start | bytes 4718596
  84.2 34.6 %all-to-all-start.2 = ((bf16[8,2,448,128]{3,2,1,0:T(8,128)(2,1)}), bf16[8,2,448,128]{3,2,1,0:T(8,128)(2,1)S(1)}, u32[]{:S(2)}, u32[]{:S(2)}) async-start(bf16[8,2,448,128]{3,2,1,0:T(8,128)(2,1)} %get-tuple-element.18), calls=%async_computation.2 | async-start | bytes 3670016 | tf_op jit(solution)/shard_map/all_to_all | solution.py:385
  89.1 27.8 %collective-permute-start.4 = (bf16[8,2,2,128,128]{4,3,2,1,0:T(8,128)(2,1)}, bf16[8,2,2,128,128]{4,3,2,1,0:T(8,128)(2,1)S(1)}, u32[]{:S(2)}, u32[]{:S(2)}) collective-permute-start(bf16[8,2,2,128,128]{4,3,2,1,0:T(8,128)(2,1)} %get-tuple-element.22), channel_id=1, source_target_pairs={{32,0},{64,32},{96,64},{33,1},{65,33},{97,65},{34,2},{66,34},{98,6... | collective-permute-start | bytes 3145736 | tf_op jit(solution)/shard_map/ppermute | solution.py:400
  90.4 3.5 %collective-permute-start.5 = (bf16[8,2,3,32,128]{4,3,2,1,0:T(8,128)(2,1)}, bf16[8,2,3,32,128]{4,3,2,1,0:T(8,128)(2,1)S(1)}, u32[]{:S(2)}, u32[]{:S(2)}) collective-permute-start(bf16[8,2,3,32,128]{4,3,2,1,0:T(8,128)(2,1)} %get-tuple-element.23), channel_id=1, source_target_pairs={{0,1},{1,2},{2,3},{4,5},{5,6},{6,7},{8,9},{9,10},{10,11},{12,13},{... | collective-permute-start | bytes 1179656 | tf_op jit(solution)/shard_map/ppermute | solution.py:402
  92.4 4.0 %collective-permute-start.6 = (bf16[8,2,3,32,128]{4,3,2,1,0:T(8,128)(2,1)}, bf16[8,2,3,32,128]{4,3,2,1,0:T(8,128)(2,1)S(1)}, u32[]{:S(2)}, u32[]{:S(2)}) collective-permute-start(bf16[8,2,3,32,128]{4,3,2,1,0:T(8,128)(2,1)} %get-tuple-element.24), channel_id=1, source_target_pairs={{1,0},{2,1},{3,2},{5,4},{6,5},{7,6},{9,8},{10,9},{11,10},{13,12},{... | collective-permute-start | bytes 1179656 | tf_op jit(solution)/shard_map/ppermute | solution.py:401
  118.7 28.8 %all-to-all-start.3 = ((bf16[8,2,3,128,128]{4,3,2,1,0:T(8,128)(2,1)}), bf16[8,2,3,128,128]{4,3,2,1,0:T(8,128)(2,1)S(1)}, u32[]{:S(2)}, u32[]{:S(2)}) async-start(bf16[8,2,3,128,128]{4,3,2,1,0:T(8,128)(2,1)} %shard_map.88), calls=%async_computation.3 | async-start | bytes 3145728 | tf_op jit(solution)/shard_map/all_to_all | solution.py:385
  127.0 8.8 %collective-permute-start.7 = (bf16[4,2,128,128]{3,2,1,0:T(8,128)(2,1)S(1)}, bf16[4,2,128,128]{3,2,1,0:T(8,128)(2,1)S(1)}, u32[]{:S(2)}, u32[]{:S(2)}) collective-permute-start(bf16[4,2,128,128]{3,2,1,0:T(8,128)(2,1)S(1)} %get-tuple-element.25), channel_id=1, source_target_pairs={{32,0},{64,32},{96,64},{33,1},{65,33},{97,65},{34,2},{66,34},{98,6... | collective-permute-start | bytes 786440 | tf_op jit(solution)/shard_map/ppermute | solution.py:409

commit v5 on v4

--- a/solution.py
+++ b/solution.py
@@ -403,7 +403,7 @@
     out_q = exchange(odq)
     args = (own, got, from_low, from_high)
     outs = [(KV_SHAPE, split(KV_SHAPE, 4))]
-    (merged,) = call(merge_kernel, 4, [split(a.shape, 4) for a in args], args, outs, limit=32)
+    (merged,) = call(merge_kernel, 4, [split(a.shape, 4) for a in args], args, outs, 8 * 10**9, limit=32)
     out_kv = exchange(merged)
     attended, grad_queries, raw = simple(unpack_queries_kernel, (out_q,), [queries.shape, queries.shape, RAW_SHAPE])
     raw = lax.ppermute(raw, "z", down)

time: 149 us -> 149 us (level)
  the two profiles are of different devices: /device:TPU:0 before, /device:TPU:97 now
where the time goes in v5:
time: 149 us; the launch traced here: 148 us
  waiting for transfers between devices  74.6 us (50%)
  starting transfers between devices  42.7 us (29%)
  Pallas kernels  26.5 us (18%)
  local copies, waits for them, and re-layouts  3.65 us (2%)
    pallas_call x6, Pallas kernels, call(): pl.pallas_call(kernel, grid=(grid,), out_shape=[jax.ShapeDtypeStruct(shap...  26.5 us
    all_to_all x4, waiting for transfers between devices, exchange(): return lax.all_to_all(x, PLACES, 0, 0)  25.6 us
    all_to_all x4, starting transfers between devices, exchange(): return lax.all_to_all(x, PLACES, 0, 0)  24.9 us
    ppermute x1, waiting for transfers between devices, shards(): from_low = lax.ppermute(dhigh, TILES, up)  19.9 us
    ppermute x1, waiting for transfers between devices, shards(): high = lax.ppermute(kv[:, :, :, :HALO], TILES, down)  18.2 us
    ppermute x1, waiting for transfers between devices, shards(): raw = lax.ppermute(raw, 'z', up)  7.45 us
    ppermute x1, starting transfers between devices, shards(): high = lax.ppermute(kv[:, :, :, :HALO], TILES, down)  3.81 us
    unnamed x18, local copies, waits for them, and re-layouts  3.46 us
  transfers between devices with their start and end apart: 12, of which 6 were waited for; matrix products, arithmetic and copies ran while one was open for 0% of the time, Pallas kernels for 2%

profile of v5, /device:TPU:97, one launch (start us, length us, event | category | flops | bytes accessed | tf_op | source)
XLA Modules:
  0.0 148.2 jit_solution(14304746089180523911)
XLA Ops:
  0.6 2.8 %shard_map.84 = (bf16[8,2,3,128,128]{4,3,2,1,0:T(8,128)(2,1)}, bf16[4,2,128,128]{3,2,1,0:T(8,128)(2,1)}) custom-call(bf16[128,2560]{1,0:T(8,128)(2,1)} %k_ref.1, bf16[128,2560]{1,0:T(8,128)(2,1)} %v_ref.1), custom_call_target="tpu_custom_call" | custom-call | bytes 3145728 | tf_op jit(solution)/shard_map/pallas_call | solution.py:340
  3.4 0.0 copy-start.8
  3.4 0.0 copy-start.1
  3.4 0.0 copy-start.2
  3.4 6.8 %all-to-all-start = ((bf16[8,2,3,128,128]{4,3,2,1,0:T(8,128)(2,1)}), bf16[8,2,3,128,128]{4,3,2,1,0:T(8,128)(2,1)S(1)}, u32[]{:S(2)}, u32[]{:S(2)}) async-start(bf16[8,2,3,128,128]{4,3,2,1,0:T(8,128)(2,1)} %get-tuple-element.16), calls=%async_computation | async-start | bytes 3145728 | tf_op jit(solution)/shard_map/all_to_all | solution.py:385
  10.2 0.0 copy-done.8
  10.2 1.3 collective-permute-start.3
  11.5 7.5 %collective-permute-done.3.raw_ref = bf16[4,2,128,128]{3,2,1,0:T(8,128)(2,1)S(1)} collective-permute-done((bf16[4,2,128,128]{3,2,1,0:T(8,128)(2,1)S(1)}, bf16[4,2,128,128]{3,2,1,0:T(8,128)(2,1)S(1)}, u32[]{:S(2)}, u32[]{:S(2)}) %collective-permute-start.3) | collective-permute-done | bytes 262176 | tf_op jit(solution)/shard_map/ppermute | solution.py:392
  19.0 0.0 copy-done.1
  19.0 0.0 copy-done.2
  19.0 1.5 %shard_map.85 = bf16[8,2,448,128]{3,2,1,0:T(8,128)(2,1)} custom-call(bf16[128,2560]{1,0:T(8,128)(2,1)S(1)} %copy-done.1, bf16[128,2560]{1,0:T(8,128)(2,1)S(1)} %copy-done.2, bf16[4,2,128,128]{3,2,1,0:T(8,128)(2,1)S(1)} %collective-permute-done.3.raw_ref), custom_call_target="tpu_custom_call" | custom-call | bytes 3407872 | tf_op jit(solution)/shard_map/pallas_call | solution.py:340
  20.5 11.6 %all-to-all-done.kv_ref = bf16[8,2,3,128,128]{4,3,2,1,0:T(8,128)(2,1)S(1)} async-done(((bf16[8,2,3,128,128]{4,3,2,1,0:T(8,128)(2,1)}), bf16[8,2,3,128,128]{4,3,2,1,0:T(8,128)(2,1)S(1)}, u32[]{:S(2)}, u32[]{:S(2)}) %all-to-all-start) | async-done | bytes 1572896 | tf_op jit(solution)/shard_map/all_to_all | solution.py:385
  32.1 0.0 copy-start.4
  32.1 4.3 %all-to-all-start.1 = ((bf16[8,2,448,128]{3,2,1,0:T(8,128)(2,1)}), bf16[8,2,448,128]{3,2,1,0:T(8,128)(2,1)}, u32[]{:S(2)}, u32[]{:S(2)}) async-start(bf16[8,2,448,128]{3,2,1,0:T(8,128)(2,1)} %shard_map.85), calls=%async_computation.1 | async-start | bytes 3670016 | tf_op jit(solution)/shard_map/all_to_all | solution.py:385
  36.5 0.1 slice.12
  36.6 1.3 collective-permute-start
  37.9 0.0 copy-done.4
  37.9 0.1 fusion
  38.0 3.8 %collective-permute-start.2 = (bf16[8,2,3,32,128]{4,3,2,1,0:T(8,128)(2,1)S(1)}, bf16[8,2,3,32,128]{4,3,2,1,0:T(8,128)(2,1)S(1)}, u32[]{:S(2)}, u32[]{:S(2)}) collective-permute-start(bf16[8,2,3,32,128]{4,3,2,1,0:T(8,128)(2,1)S(1)} %get-tuple-element.28), channel_id=1, source_target_pairs={{1,0},{2,1},{3,2},{5,4},{6,5},{7,6},{9,8},{10,9},{11,10},{13,12},{... | collective-permute-start | bytes 1179656 | tf_op jit(solution)/shard_map/ppermute | solution.py:397
  41.8 2.1 %collective-permute-start.1 = (bf16[8,2,3,32,128]{4,3,2,1,0:T(8,128)(2,1)S(1)}, bf16[8,2,3,32,128]{4,3,2,1,0:T(8,128)(2,1)S(1)}, u32[]{:S(2)}, u32[]{:S(2)}) collective-permute-start(bf16[8,2,3,32,128]{4,3,2,1,0:T(8,128)(2,1)S(1)} %get-tuple-element.29), channel_id=1, source_target_pairs={{0,1},{1,2},{2,3},{4,5},{5,6},{6,7},{8,9},{9,10},{10,11},{12,13},{... | collective-permute-start | bytes 1179656 | tf_op jit(solution)/shard_map/ppermute | solution.py:396
  43.9 18.2 %collective-permute-done.2.high_ref = bf16[8,2,3,32,128]{4,3,2,1,0:T(8,128)(2,1)S(1)} collective-permute-done((bf16[8,2,3,32,128]{4,3,2,1,0:T(8,128)(2,1)S(1)}, bf16[8,2,3,32,128]{4,3,2,1,0:T(8,128)(2,1)S(1)}, u32[]{:S(2)}, u32[]{:S(2)}) %collective-permute-start.2) | collective-permute-done | bytes 393248 | tf_op jit(solution)/shard_map/ppermute | solution.py:397
  62.1 0.0 copy-start.5
  62.1 0.0 collective-permute-done.1.low_ref
  62.1 0.0 copy-start.7
  62.1 0.0 all-to-all-done.1.q_ref.past2_ref.q2_ref
  62.1 0.0 collective-permute-done.past_ref
  62.2 0.7 copy-done.5
  62.9 0.1 copy-done.7
  63.0 19.2 %shard_map.86 = (bf16[8,2,448,128]{3,2,1,0:T(8,128)(2,1)}, bf16[8,2,3,128,128]{4,3,2,1,0:T(8,128)(2,1)}, bf16[8,2,2,128,128]{4,3,2,1,0:T(8,128)(2,1)}, bf16[8,2,...) custom-call(s32[20]{0:T(128)} %window_ref.1, bf16[8,2,3,128,128]{4,3,2,1,0:T(8,128)(2,1)} %copy-done.4, ...), custom_call_target="tpu_custom_call" | custom-call | flops 10000000000 | bytes 14155856 | tf_op jit(solution)/shard_map/pallas_call | solution.py:340
  82.3 2.1 %collective-permute-start.4 = (bf16[8,2,2,128,128]{4,3,2,1,0:T(8,128)(2,1)}, bf16[8,2,2,128,128]{4,3,2,1,0:T(8,128)(2,1)S(1)}, u32[]{:S(2)}, u32[]{:S(2)}) collective-permute-start(bf16[8,2,2,128,128]{4,3,2,1,0:T(8,128)(2,1)} %get-tuple-element.22), channel_id=1, source_target_pairs={{32,0},{64,32},{96,64},{33,1},{65,33},{97,65},{34,2},{66,34},{98,6... | collective-permute-start | bytes 3145736 | tf_op jit(solution)/shard_map/ppermute | solution.py:400
  84.3 0.0 copy-start.6
  84.4 7.4 %all-to-all-start.2 = ((bf16[8,2,448,128]{3,2,1,0:T(8,128)(2,1)}), bf16[8,2,448,128]{3,2,1,0:T(8,128)(2,1)S(1)}, u32[]{:S(2)}, u32[]{:S(2)}) async-start(bf16[8,2,448,128]{3,2,1,0:T(8,128)(2,1)} %get-tuple-element.18), calls=%async_computation.2 | async-start | bytes 3670016 | tf_op jit(solution)/shard_map/all_to_all | solution.py:385
  91.7 3.1 %collective-permute-start.5 = (bf16[8,2,3,32,128]{4,3,2,1,0:T(8,128)(2,1)}, bf16[8,2,3,32,128]{4,3,2,1,0:T(8,128)(2,1)S(1)}, u32[]{:S(2)}, u32[]{:S(2)}) collective-permute-start(bf16[8,2,3,32,128]{4,3,2,1,0:T(8,128)(2,1)} %get-tuple-element.23), channel_id=1, source_target_pairs={{0,1},{1,2},{2,3},{4,5},{5,6},{6,7},{8,9},{9,10},{10,11},{12,13},{... | collective-permute-start | bytes 1179656 | tf_op jit(solution)/shard_map/ppermute | solution.py:402
  94.9 0.0 copy-done.6
  94.9 1.9 %collective-permute-start.6 = (bf16[8,2,3,32,128]{4,3,2,1,0:T(8,128)(2,1)S(1)}, bf16[8,2,3,32,128]{4,3,2,1,0:T(8,128)(2,1)S(1)}, u32[]{:S(2)}, u32[]{:S(2)}) collective-permute-start(bf16[8,2,3,32,128]{4,3,2,1,0:T(8,128)(2,1)S(1)} %copy-done.6), channel_id=1, source_target_pairs={{1,0},{2,1},{3,2},{5,4},{6,5},{7,6},{9,8},{10,9},{11,10},{13,12},{... | collective-permute-start | bytes 1179656 | tf_op jit(solution)/shard_map/ppermute | solution.py:401
  96.8 19.9 %collective-permute-done.5.from_low_ref = bf16[8,2,3,32,128]{4,3,2,1,0:T(8,128)(2,1)S(1)} collective-permute-done((bf16[8,2,3,32,128]{4,3,2,1,0:T(8,128)(2,1)}, bf16[8,2,3,32,128]{4,3,2,1,0:T(8,128)(2,1)S(1)}, u32[]{:S(2)}, u32[]{:S(2)}) %collective-permute-start.5) | collective-permute-done | bytes 393248 | tf_op jit(solution)/shard_map/ppermute | solution.py:402
  116.7 0.0 collective-permute-done.6.from_high_ref
  116.7 0.0 collective-permute-done.4.got_ref
  116.7 0.0 copy-start.3
  116.7 1.4 copy-done.3
  118.1 0.4 shard_map.88
  118.5 0.0 copy-start
  118.6 1.2 copy-done
  119.7 0.0 all-to-all-done.2.odq_ref
  119.7 6.4 %all-to-all-start.3 = ((bf16[8,2,3,128,128]{4,3,2,1,0:T(8,128)(2,1)}), bf16[8,2,3,128,128]{4,3,2,1,0:T(8,128)(2,1)S(1)}, u32[]{:S(2)}, u32[]{:S(2)}) async-start(bf16[8,2,3,128,128]{4,3,2,1,0:T(8,128)(2,1)} %copy-done), calls=%async_computation.3 | async-start | bytes 3145728 | tf_op jit(solution)/shard_map/all_to_all | solution.py:385
  126.1 1.3 shard_map.87
  127.4 2.2 %collective-permute-start.7 = (bf16[4,2,128,128]{3,2,1,0:T(8,128)(2,1)S(1)}, bf16[4,2,128,128]{3,2,1,0:T(8,128)(2,1)S(1)}, u32[]{:S(2)}, u32[]{:S(2)}) collective-permute-start(bf16[4,2,128,128]{3,2,1,0:T(8,128)(2,1)S(1)} %get-tuple-element.25), channel_id=1, source_target_pairs={{32,0},{64,32},{96,64},{33,1},{65,33},{97,65},{34,2},{66,34},{98,6... | collective-permute-start | bytes 786440 | tf_op jit(solution)/shard_map/ppermute | solution.py:409
  129.6 3.4 %collective-permute-done.7.raw_ref = bf16[4,2,128,128]{3,2,1,0:T(8,128)(2,1)S(1)} collective-permute-done((bf16[4,2,128,128]{3,2,1,0:T(8,128)(2,1)S(1)}, bf16[4,2,128,128]{3,2,1,0:T(8,128)(2,1)S(1)}, u32[]{:S(2)}, u32[]{:S(2)}) %collective-permute-start.7) | collective-permute-done | bytes 262176 | tf_op jit(solution)/shard_map/ppermute | solution.py:409
  133.0 14.0 %all-to-all-done.3.grads_ref = bf16[8,2,3,128,128]{4,3,2,1,0:T(8,128)(2,1)S(1)} async-done(((bf16[8,2,3,128,128]{4,3,2,1,0:T(8,128)(2,1)}), bf16[8,2,3,128,128]{4,3,2,1,0:T(8,128)(2,1)S(1)}, u32[]{:S(2)}, u32[]{:S(2)}) %all-to-all-start.3) | async-done | bytes 1572896 | tf_op jit(solution)/shard_map/all_to_all | solution.py:385
  146.9 1.3 shard_map.89
Async XLA Ops:
  3.4 6.8 %copy-start.8 = (bf16[4,2,128,128]{3,2,1,0:T(8,128)(2,1)S(1)}, bf16[4,2,128,128]{3,2,1,0:T(8,128)(2,1)}, u32[]{:S(2)}) copy-start(bf16[4,2,128,128]{3,2,1,0:T(8,128)(2,1)} %get-tuple-element.17) | copy-start | bytes 786436
  3.4 15.6 %copy-start.1 = (bf16[128,2560]{1,0:T(8,128)(2,1)S(1)}, bf16[128,2560]{1,0:T(8,128)(2,1)}, u32[]{:S(2)}) copy-start(bf16[128,2560]{1,0:T(8,128)(2,1)} %q_ref.1) | copy-start | bytes 1966084
  3.4 15.6 %copy-start.2 = (bf16[128,2560]{1,0:T(8,128)(2,1)S(1)}, bf16[128,2560]{1,0:T(8,128)(2,1)}, u32[]{:S(2)}) copy-start(bf16[128,2560]{1,0:T(8,128)(2,1)} %do_ref.1) | copy-start | bytes 1966084
  3.4 28.7 %all-to-all-start = ((bf16[8,2,3,128,128]{4,3,2,1,0:T(8,128)(2,1)}), bf16[8,2,3,128,128]{4,3,2,1,0:T(8,128)(2,1)S(1)}, u32[]{:S(2)}, u32[]{:S(2)}) async-start(bf16[8,2,3,128,128]{4,3,2,1,0:T(8,128)(2,1)} %get-tuple-element.16), calls=%async_computation | async-start | bytes 3145728 | tf_op jit(solution)/shard_map/all_to_all | solution.py:385
  10.2 8.8 %collective-permute-start.3 = (bf16[4,2,128,128]{3,2,1,0:T(8,128)(2,1)S(1)}, bf16[4,2,128,128]{3,2,1,0:T(8,128)(2,1)S(1)}, u32[]{:S(2)}, u32[]{:S(2)}) collective-permute-start(bf16[4,2,128,128]{3,2,1,0:T(8,128)(2,1)S(1)} %copy-done.8), channel_id=1, source_target_pairs={{0,32},{32,64},{64,96},{1,33},{33,65},{65,97},{2,34},{34,66},{66,9... | collective-permute-start | bytes 786440 | tf_op jit(solution)/shard_map/ppermute | solution.py:392
  32.1 5.7 %copy-start.4 = (bf16[8,2,3,128,128]{4,3,2,1,0:T(8,128)(2,1)}, bf16[8,2,3,128,128]{4,3,2,1,0:T(8,128)(2,1)S(1)}, u32[]{:S(2)}) copy-start(bf16[8,2,3,128,128]{4,3,2,1,0:T(8,128)(2,1)S(1)} %all-to-all-done.kv_ref) | copy-start | bytes 4718596
  32.1 30.0 %all-to-all-start.1 = ((bf16[8,2,448,128]{3,2,1,0:T(8,128)(2,1)}), bf16[8,2,448,128]{3,2,1,0:T(8,128)(2,1)}, u32[]{:S(2)}, u32[]{:S(2)}) async-start(bf16[8,2,448,128]{3,2,1,0:T(8,128)(2,1)} %shard_map.85), calls=%async_computation.1 | async-start | bytes 3670016 | tf_op jit(solution)/shard_map/all_to_all | solution.py:385
  36.6 25.6 %collective-permute-start = (bf16[8,2,2,128,128]{4,3,2,1,0:T(8,128)(2,1)S(1)}, bf16[8,2,2,128,128]{4,3,2,1,0:T(8,128)(2,1)}, u32[]{:S(2)}, u32[]{:S(2)}) collective-permute-start(bf16[8,2,2,128,128]{4,3,2,1,0:T(8,128)(2,1)S(1)} %slice.12), channel_id=1, source_target_pairs={{0,32},{32,64},{64,96},{1,33},{33,65},{65,97},{2,34},{34,66},{66,9... | collective-permute-start | bytes 3145736 | tf_op jit(solution)/shard_map/ppermute | solution.py:395
  38.0 24.2 %collective-permute-start.2 = (bf16[8,2,3,32,128]{4,3,2,1,0:T(8,128)(2,1)S(1)}, bf16[8,2,3,32,128]{4,3,2,1,0:T(8,128)(2,1)S(1)}, u32[]{:S(2)}, u32[]{:S(2)}) collective-permute-start(bf16[8,2,3,32,128]{4,3,2,1,0:T(8,128)(2,1)S(1)} %get-tuple-element.28), channel_id=1, source_target_pairs={{1,0},{2,1},{3,2},{5,4},{6,5},{7,6},{9,8},{10,9},{11,10},{13,12},{... | collective-permute-start | bytes 1179656 | tf_op jit(solution)/shard_map/ppermute | solution.py:397
  41.8 20.3 %collective-permute-start.1 = (bf16[8,2,3,32,128]{4,3,2,1,0:T(8,128)(2,1)S(1)}, bf16[8,2,3,32,128]{4,3,2,1,0:T(8,128)(2,1)S(1)}, u32[]{:S(2)}, u32[]{:S(2)}) collective-permute-start(bf16[8,2,3,32,128]{4,3,2,1,0:T(8,128)(2,1)S(1)} %get-tuple-element.29), channel_id=1, source_target_pairs={{0,1},{1,2},{2,3},{4,5},{5,6},{6,7},{8,9},{9,10},{10,11},{12,13},{... | collective-permute-start | bytes 1179656 | tf_op jit(solution)/shard_map/ppermute | solution.py:396
  62.1 0.7 copy-start.5
  62.1 0.9 copy-start.7
  82.3 34.5 %collective-permute-start.4 = (bf16[8,2,2,128,128]{4,3,2,1,0:T(8,128)(2,1)}, bf16[8,2,2,128,128]{4,3,2,1,0:T(8,128)(2,1)S(1)}, u32[]{:S(2)}, u32[]{:S(2)}) collective-permute-start(bf16[8,2,2,128,128]{4,3,2,1,0:T(8,128)(2,1)} %get-tuple-element.22), channel_id=1, source_target_pairs={{32,0},{64,32},{96,64},{33,1},{65,33},{97,65},{34,2},{66,34},{98,6... | collective-permute-start | bytes 3145736 | tf_op jit(solution)/shard_map/ppermute | solution.py:400
  84.3 10.5 %copy-start.6 = (bf16[8,2,3,32,128]{4,3,2,1,0:T(8,128)(2,1)S(1)}, bf16[8,2,3,32,128]{4,3,2,1,0:T(8,128)(2,1)}, u32[]{:S(2)}) copy-start(bf16[8,2,3,32,128]{4,3,2,1,0:T(8,128)(2,1)} %get-tuple-element.24) | copy-start | bytes 1179652
  84.4 35.4 %all-to-all-start.2 = ((bf16[8,2,448,128]{3,2,1,0:T(8,128)(2,1)}), bf16[8,2,448,128]{3,2,1,0:T(8,128)(2,1)S(1)}, u32[]{:S(2)}, u32[]{:S(2)}) async-start(bf16[8,2,448,128]{3,2,1,0:T(8,128)(2,1)} %get-tuple-element.18), calls=%async_computation.2 | async-start | bytes 3670016 | tf_op jit(solution)/shard_map/all_to_all | solution.py:385
  91.7 25.0 %collective-permute-start.5 = (bf16[8,2,3,32,128]{4,3,2,1,0:T(8,128)(2,1)}, bf16[8,2,3,32,128]{4,3,2,1,0:T(8,128)(2,1)S(1)}, u32[]{:S(2)}, u32[]{:S(2)}) collective-permute-start(bf16[8,2,3,32,128]{4,3,2,1,0:T(8,128)(2,1)} %get-tuple-element.23), channel_id=1, source_target_pairs={{0,1},{1,2},{2,3},{4,5},{5,6},{6,7},{8,9},{9,10},{10,11},{12,13},{... | collective-permute-start | bytes 1179656 | tf_op jit(solution)/shard_map/ppermute | solution.py:402
  94.9 21.8 %collective-permute-start.6 = (bf16[8,2,3,32,128]{4,3,2,1,0:T(8,128)(2,1)S(1)}, bf16[8,2,3,32,128]{4,3,2,1,0:T(8,128)(2,1)S(1)}, u32[]{:S(2)}, u32[]{:S(2)}) collective-permute-start(bf16[8,2,3,32,128]{4,3,2,1,0:T(8,128)(2,1)S(1)} %copy-done.6), channel_id=1, source_target_pairs={{1,0},{2,1},{3,2},{5,4},{6,5},{7,6},{9,8},{10,9},{11,10},{13,12},{... | collective-permute-start | bytes 1179656 | tf_op jit(solution)/shard_map/ppermute | solution.py:401
  116.7 1.4 copy-start.3
  118.5 1.2 copy-start
  119.7 27.2 %all-to-all-start.3 = ((bf16[8,2,3,128,128]{4,3,2,1,0:T(8,128)(2,1)}), bf16[8,2,3,128,128]{4,3,2,1,0:T(8,128)(2,1)S(1)}, u32[]{:S(2)}, u32[]{:S(2)}) async-start(bf16[8,2,3,128,128]{4,3,2,1,0:T(8,128)(2,1)} %copy-done), calls=%async_computation.3 | async-start | bytes 3145728 | tf_op jit(solution)/shard_map/all_to_all | solution.py:385
  127.4 5.6 %collective-permute-start.7 = (bf16[4,2,128,128]{3,2,1,0:T(8,128)(2,1)S(1)}, bf16[4,2,128,128]{3,2,1,0:T(8,128)(2,1)S(1)}, u32[]{:S(2)}, u32[]{:S(2)}) collective-permute-start(bf16[4,2,128,128]{3,2,1,0:T(8,128)(2,1)S(1)} %get-tuple-element.25), channel_id=1, source_target_pairs={{32,0},{64,32},{96,64},{33,1},{65,33},{97,65},{34,2},{66,34},{98,6... | collective-permute-start | bytes 786440 | tf_op jit(solution)/shard_map/ppermute | solution.py:409
